TPU v7x, 128 devices: a whole 4x4x4 slice. The times are simulated.
128 devices in a mesh: gx: 8 (over y, core), gy: 16 (over z, x).
Axes of the slice: x: 4, y: 4, z: 4, core: 2. Of those that a mesh axis runs over, the one named last changes fastest.
Arguments:
- velocity: float32 [3, 128, 128, 128], P(None, 'gx', 'gy'), may hold values from -6 to 6
- offsets: float32 [3, 16384, 128], P(None, ('gx', 'gy')), may hold values from -1.5 to 1.5
- forces: float32 [3, 16384, 128], P(None, ('gx', 'gy')), may hold values from -24 to 24
- owner: int32 [16384], P(('gx', 'gy')), may hold values from 0 to 127, as said below
- base: int32 [3, 16384], P(None, ('gx', 'gy')), may hold values from 0 to 123, as said below
- counts: int32 [128], P(('gx', 'gy')), may hold values from 64 to 128, as said below
Outputs:
- new_velocity: float32 [3, 128, 128, 128], P(None, 'gx', 'gy')
- pressure: float32 [128, 128, 128], P('gx', 'gy')
- marker_velocity: float32 [3, 16384, 128], P(None, ('gx', 'gy'))
Inputs may be any that keep to these rules, and one draw needn't show every extreme that they name: Owners are device indices of gx+gy, gx major. Among one device's slots no owner appears more than 2 times, and 32 owners appear exactly 2 times among the live slots of every device. Rows 0 and 1: the base cell within the owner's block along x (below 16) and y (below 8); row 2: the cell along z, from 3 to 123. `counts`: slots below a device's count are live, the others are ignored.
All inputs are finite; a program needn't handle non-finite values.
Results may differ from a plain program's by a relative error of at most 0.0003.
Values sent between devices are 32-bit elements; how exact they have to be, the bound alone decides.
A program may use at most 64 MiB of HBM per device.

v0:
```python
import jax
import jax.numpy as jnp
from jax import lax
from jax.sharding import PartitionSpec as P

JAC = 4


time_step = 0.5
viscosity = 0.1
highest = lax.Precision.HIGHEST


def with_halo(block, sides, width):
    for axis, dim in sides:
        count = lax.axis_size(axis)
        forward = [(i, i + 1) for i in range(count - 1)]
        forward.append((count - 1, 0))
        backward = [(target, source) for source, target in forward]
        low = lax.ppermute(
            lax.slice_in_dim(block, block.shape[dim] - width, None, axis=dim), axis, forward
        )
        high = lax.ppermute(lax.slice_in_dim(block, 0, width, axis=dim), axis, backward)
        block = jnp.concatenate([low, block, high], axis=dim)
    return block


def kernel(distance):
    magnitude = jnp.abs(distance)
    inner_part = (
        3.0 - 2.0 * magnitude + jnp.sqrt(1.0 + 4.0 * magnitude - 4.0 * magnitude * magnitude)
    ) / 8.0
    outer_part = (
        5.0 - 2.0 * magnitude - jnp.sqrt(-7.0 + 12.0 * magnitude - 4.0 * magnitude * magnitude)
    ) / 8.0
    return jnp.where(magnitude < 1.0, inner_part, jnp.where(magnitude < 2.0, outer_part, 0.0))


def kernel_table(offsets):
    shifts = jnp.arange(8).astype(jnp.float32) - 3.0
    return kernel(offsets[:, :, None, :] - shifts[None, None, :, None])


def planes_of(weights):
    joined = weights[0][:, :, None, :] * weights[1][:, None, :, :]
    return joined.reshape(joined.shape[0], 64, joined.shape[3])


def spread(offsets, forces):
    weights = kernel_table(offsets)
    loaded = forces[:, :, None, :] * planes_of(weights)[None]
    box_values = jnp.einsum("cspm,skm->cskp", loaded, weights[2], precision=highest)
    return box_values.reshape(3, box_values.shape[1], 512)


def interpolate(offsets, box_values):
    weights = kernel_table(offsets)
    cubes = box_values.reshape(3, box_values.shape[1], 8, 64)
    contracted = jnp.einsum("cskp,skm->cspm", cubes, weights[2], precision=highest)
    return jnp.sum(contracted * planes_of(weights)[None], axis=2)


def by_blocks(function, arrays, block_rows):
    length = arrays[0].shape[1]

    def handle(start):
        pieces = [lax.dynamic_slice_in_dim(member, start, block_rows, 1) for member in arrays]
        return function(*pieces)

    starts = jnp.arange(length // block_rows, dtype=jnp.int32) * block_rows
    stacked = lax.map(handle, starts)
    moved = jnp.moveaxis(stacked, 0, 1)
    return moved.reshape((moved.shape[0], length) + moved.shape[3:])


def one_hot(starts, extent):
    ladder = jnp.arange(8, dtype=jnp.int32)
    spots = jnp.arange(extent, dtype=jnp.int32)
    return (starts[:, None, None] + ladder[None, :, None] == spots[None, None, :]).astype(
        jnp.float32
    )


def deposit_dense(box_values, cells, shape_x, shape_y, z_depth):
    block_rows = 64
    total_rows = box_values.shape[1]

    def add_block(turn, total):
        start = turn * block_rows
        values = lax.dynamic_slice_in_dim(box_values, start, block_rows, 1).reshape(
            3, block_rows, 8, 8, 8
        )
        corner = lax.dynamic_slice_in_dim(cells, start, block_rows, 1)
        along_x = one_hot(corner[0], shape_x)
        along_y = one_hot(corner[1], shape_y)
        along_z = one_hot(corner[2] - 3, z_depth)
        planes = jnp.einsum("cbkij,bkz->cbijz", values, along_z, precision=highest)
        rows_y = jnp.einsum("cbijz,bjy->cbiyz", planes, along_y, precision=highest)
        return total + jnp.einsum("cbiyz,bix->cxyz", rows_y, along_x, precision=highest)

    start_grid = jnp.zeros((3, shape_x, shape_y, z_depth), jnp.float32)
    return lax.fori_loop(0, total_rows // block_rows, add_block, start_grid)


def gather_boxes(grid, cells):
    along_x = one_hot(cells[0], grid.shape[1])
    along_y = one_hot(cells[1], grid.shape[2])
    along_z = one_hot(cells[2] - 3, grid.shape[3])
    rows_x = jnp.einsum("cxyz,bix->cbiyz", grid, along_x, precision=highest)
    planes = jnp.einsum("cbiyz,bjy->cbijz", rows_x, along_y, precision=highest)
    cube = jnp.einsum("cbijz,bkz->cbkij", planes, along_z, precision=highest)
    return cube.reshape(3, cells.shape[1], 512)


def neighbour_sum(padded):
    return (
        padded[..., 2:, 1:-1, 1:-1]
        + padded[..., :-2, 1:-1, 1:-1]
        + padded[..., 1:-1, 2:, 1:-1]
        + padded[..., 1:-1, :-2, 1:-1]
        + padded[..., 1:-1, 1:-1, 2:]
        + padded[..., 1:-1, 1:-1, :-2]
    )


def divergence(padded):
    return (
        0.5
        * (
            padded[0, 2:, 1:-1, 1:-1]
            - padded[0, :-2, 1:-1, 1:-1]
            + (padded[1, 1:-1, 2:, 1:-1] - padded[1, 1:-1, :-2, 1:-1])
            + (padded[2, 1:-1, 1:-1, 2:] - padded[2, 1:-1, 1:-1, :-2])
        )
    )[None]


def gradient(padded):
    return 0.5 * jnp.stack(
        [
            padded[0, 2:, 1:-1, 1:-1] - padded[0, :-2, 1:-1, 1:-1],
            padded[0, 1:-1, 2:, 1:-1] - padded[0, 1:-1, :-2, 1:-1],
            padded[0, 1:-1, 1:-1, 2:] - padded[0, 1:-1, 1:-1, :-2],
        ]
    )


def pad_depth(grid_field):
    return jnp.pad(grid_field, ((0, 0), (0, 0), (0, 0), (1, 1)))


def extend(grid_field):
    widened = with_halo(grid_field, (("gx", 1), ("gy", 2)), 1)
    return pad_depth(widened)


def grow_rims(grid_field):
    return with_halo(grid_field, (("gx", 1), ("gy", 2)), 3)


def fold_rims(widened, axis_dim, length):
    middle = lax.slice_in_dim(widened, 6, 6 + length, axis=axis_dim)
    lower_rim = lax.slice_in_dim(widened, 0, 3, axis=axis_dim)
    upper_rim = lax.slice_in_dim(widened, length + 9, length + 12, axis=axis_dim)
    low_pad = [(0, 0)] * widened.ndim
    low_pad[axis_dim] = (0, length - 3)
    high_pad = [(0, 0)] * widened.ndim
    high_pad[axis_dim] = (length - 3, 0)
    return middle + jnp.pad(lower_rim, low_pad) + jnp.pad(upper_rim, high_pad)


def send_rows(parts):
    return (
        lax.all_to_all(parts[0], ("gx", "gy"), split_axis=1, concat_axis=1, tiled=True),
        lax.all_to_all(parts[1], ("gx", "gy"), split_axis=1, concat_axis=1, tiled=True),
        lax.all_to_all(parts[2], ("gx", "gy"), split_axis=1, concat_axis=1, tiled=True),
    )


def send_back(parts):
    return (lax.all_to_all(parts[0], ("gx", "gy"), split_axis=1, concat_axis=1, tiled=True),)


def shards(velocity, offsets, forces, owner, base, counts):
    devices = lax.axis_size(("gx", "gy"))
    patch_dev = owner.shape[0]
    capacity = 2 * patch_dev // devices
    buffer_rows = devices * capacity
    living = jnp.arange(patch_dev, dtype=jnp.int32) < counts[0]
    matches = (
        (owner[:, None] == jnp.arange(devices, dtype=jnp.int32)[None, :]) & living[:, None]
    ).astype(jnp.int32)
    ranking = jnp.sum((jnp.cumsum(matches, axis=0) - matches) * matches, axis=1)
    target = jnp.where(living, owner * capacity + ranking, buffer_rows)
    fetch = jnp.minimum(target, buffer_rows - 1)
    base_float = base.astype(jnp.float32)
    width_x = velocity.shape[1]
    width_y = velocity.shape[2]
    z_depth = velocity.shape[3]

    def pack(values):
        empty = jnp.zeros(values.shape[:1] + (buffer_rows,) + values.shape[2:], values.dtype)
        return empty.at[:, target].set(values, mode="drop")

    arrived = send_rows((pack(offsets), pack(forces), pack(base_float)))
    moved_offsets = arrived[0]
    moved_base = arrived[2].astype(jnp.int32)
    box_values = by_blocks(spread, (moved_offsets, arrived[1]), 64)
    spread_grid = deposit_dense(box_values, moved_base, width_x + 8, width_y + 8, z_depth)
    widened = grow_rims(spread_grid[:, : width_x + 6, : width_y + 6])
    force_field = fold_rims(fold_rims(widened, 1, width_x), 2, width_y)
    laplace = neighbour_sum(extend(velocity)) - 6.0 * velocity
    provisional = velocity + time_step * (viscosity * laplace + force_field)
    source = divergence(extend(provisional)) / time_step
    pressure = -source / 6.0
    for sweep in range(JAC - 1):
        pressure = (neighbour_sum(extend(pressure)) - source) / 6.0
    new_velocity = provisional - time_step * gradient(extend(pressure))
    sampled = jnp.pad(grow_rims(new_velocity), ((0, 0), (0, 2), (0, 2), (0, 0)))

    def at_markers(offset_rows, cell_rows):
        return interpolate(offset_rows, gather_boxes(sampled, cell_rows))

    answers = by_blocks(at_markers, (moved_offsets, moved_base), 64)
    returned = send_back((answers,))[0]
    marker_velocity = jnp.take(returned, fetch, axis=1)
    marker_velocity = jnp.where(living[None, :, None], marker_velocity, 0.0)
    return (new_velocity, pressure[0], marker_velocity)


def solution(mesh):
    return jax.shard_map(
        shards,
        mesh=mesh,
        in_specs=(
            P(None, "gx", "gy", None),
            P(None, ("gx", "gy"), None),
            P(None, ("gx", "gy"), None),
            P(("gx", "gy")),
            P(None, ("gx", "gy")),
            P(("gx", "gy")),
        ),
        out_specs=(P(None, "gx", "gy", None), P("gx", "gy", None), P(None, ("gx", "gy"), None)),
        check_vma=False,
    )
```

profile of v0, /device:TPU:1, one launch (start us, length us, event | category | flops | bytes accessed | tf_op | source)
XLA Modules:
  0.0 747.9 jit_solution(3141136117276306644)
XLA Ops:
  6.6 11.5 %all-to-all-start = ((f32[3,128,2]{0,2,1:T(2,128)}), f32[3,128,2]{0,2,1:T(2,128)S(1)}, u32[]{:S(2)}, u32[]{:S(2)}) async-start(f32[3,128,2]{0,2,1:T(2,128)} %bitcast.33), calls=%async_computation | async-start | bytes 262144 | tf_op jit(solution)/shard_map/all_to_all | solution.py:176
  20.1 12.8 %scatter_fusion = f32[3,256,128]{2,0,1:T(4,128)} fusion(f32[3,256,128]{2,0,1:T(4,128)} %broadcast.378.clone, s32[128]{0:T(128)S(1)} %compare_select_fusion.1, f32[128,3,128]{2,1,0:T(4,128)S(1)} %copy.86), kind=kCustom, calls=%fused_computation.2 | custom fusion | bytes 590336 | tf_op jit(solution)/shard_map/scatter | solution.py:203
  32.9 9.5 %all-to-all-start.1 = ((f32[3,256,128]{2,0,1:T(4,128)}), f32[3,256,128]{2,0,1:T(4,128)S(1)}, u32[]{:S(2)}, u32[]{:S(2)}) async-start(f32[3,256,128]{2,0,1:T(4,128)} %scatter_fusion), calls=%async_computation.1 | async-start | bytes 1048576 | tf_op jit(solution)/shard_map/all_to_all | solution.py:174
  46.7 12.8 %scatter_fusion.1 = f32[3,256,128]{2,0,1:T(4,128)} fusion(f32[3,256,128]{2,0,1:T(4,128)} %broadcast.378.clone.1, s32[128]{0:T(128)S(1)} %compare_select_fusion.1, f32[128,3,128]{2,1,0:T(4,128)S(1)} %copy.87), kind=kCustom, calls=%fused_computation.3 | custom fusion | bytes 590336 | tf_op jit(solution)/shard_map/scatter | solution.py:203
  59.6 9.9 %all-to-all-start.2 = ((f32[3,256,128]{2,0,1:T(4,128)}), f32[3,256,128]{2,0,1:T(4,128)S(1)}, u32[]{:S(2)}, u32[]{:S(2)}) async-start(f32[3,256,128]{2,0,1:T(4,128)} %scatter_fusion.1), calls=%async_computation.2 | async-start | bytes 1048576 | tf_op jit(solution)/shard_map/all_to_all | solution.py:175
  70.0 13.4 %all-to-all-done.2 = f32[3,256,128]{2,0,1:T(4,128)S(1)} async-done(((f32[3,256,128]{2,0,1:T(4,128)}), f32[3,256,128]{2,0,1:T(4,128)S(1)}, u32[]{:S(2)}, u32[]{:S(2)}) %all-to-all-start.2) | async-done | bytes 393248 | tf_op jit(solution)/shard_map/all_to_all | solution.py:175
  83.5 72.7 %while.40 = (s32[]{:T(128)}, f32[4,3,64,512]{3,2,0,1:T(8,128)}, s32[4]{0:T(128)S(1)}, f32[3,256,128]{2,1,0:T(8,128)S(1)}, f32[3,256,128]{2,0,1:T(4,128)S(1)}, /*index=5*/s32[]{:T(128)}, s32[]{:T(128)}, s32[]{:T(128)}) while((s32[]{:T(128)}, f32[4,3,64,512]{3,2,0,1:T(8,128)}, s32[4]{0:T(128)S(1)}, f32[3,256,128]{2,1,0:T(8,128)S(1)}, ...), condition=%wide.region_5.6_spmd, body=%wide.region_4.5_spmd.sunk | while | flops 157024272 | bytes 9405131 | solution.py:71
  87.4 13.1 %fusion.145 = f32[3,64,8,64]{3,2,0,1:T(8,128)S(1)} fusion(f32[64,64,128]{2,1,0:T(8,128)S(1)} %multiply_bitcast_fusion.4, f32[3,64,128]{2,0,1:T(4,128)S(1)} %constant_dynamic-slice_fusion.13, f32[3,64,8,128]{3,2,1,0:T(8,128)S(1)} %fusion.144), kind=kOutput, calls=%fused_computation.9.clone.1 | convolution fusion | flops 152567808 | bytes 2883584 | tf_op jit(solution)/shard_map/while/body/eval_jaxpr/cspm,skm->cskp/dot_general | solution.py:52
  105.5 13.1 %fusion.145 = f32[3,64,8,64]{3,2,0,1:T(8,128)S(1)} fusion(f32[64,64,128]{2,1,0:T(8,128)S(1)} %multiply_bitcast_fusion.4, f32[3,64,128]{2,0,1:T(4,128)S(1)} %constant_dynamic-slice_fusion.13, f32[3,64,8,128]{3,2,1,0:T(8,128)S(1)} %fusion.144), kind=kOutput, calls=%fused_computation.9.clone.1 | convolution fusion | flops 152567808 | bytes 2883584 | tf_op jit(solution)/shard_map/while/body/eval_jaxpr/cspm,skm->cskp/dot_general | solution.py:52
  123.7 13.1 %fusion.145 = f32[3,64,8,64]{3,2,0,1:T(8,128)S(1)} fusion(f32[64,64,128]{2,1,0:T(8,128)S(1)} %multiply_bitcast_fusion.4, f32[3,64,128]{2,0,1:T(4,128)S(1)} %constant_dynamic-slice_fusion.13, f32[3,64,8,128]{3,2,1,0:T(8,128)S(1)} %fusion.144), kind=kOutput, calls=%fused_computation.9.clone.1 | convolution fusion | flops 152567808 | bytes 2883584 | tf_op jit(solution)/shard_map/while/body/eval_jaxpr/cspm,skm->cskp/dot_general | solution.py:52
  141.9 13.1 %fusion.145 = f32[3,64,8,64]{3,2,0,1:T(8,128)S(1)} fusion(f32[64,64,128]{2,1,0:T(8,128)S(1)} %multiply_bitcast_fusion.4, f32[3,64,128]{2,0,1:T(4,128)S(1)} %constant_dynamic-slice_fusion.13, f32[3,64,8,128]{3,2,1,0:T(8,128)S(1)} %fusion.144), kind=kOutput, calls=%fused_computation.9.clone.1 | convolution fusion | flops 152567808 | bytes 2883584 | tf_op jit(solution)/shard_map/while/body/eval_jaxpr/cspm,skm->cskp/dot_general | solution.py:52
  157.0 149.9 %while.42 = (s32[]{:T(128)}, f32[3,24,16,128]{3,1,2,0:T(8,128)S(1)}, s32[3,256]{1,0:T(4,128)S(1)}, f32[3,256,512]{2,1,0:T(8,128)}, s32[]{:T(128)}, /*index=5*/s32[]{:T(128)}, s32[]{:T(128)}, s32[]{:T(128)}) while((s32[]{:T(128)}, f32[3,24,16,128]{3,1,2,0:T(8,128)S(1)}, s32[3,256]{1,0:T(4,128)S(1)}, f32[3,256,512]{2,1,0:T(8,128)}, ...), condition=%wide.region_8.9_spmd.clone, body=%wide.region_7.8_spmd.clone.sunk | while | flops 1359336960 | bytes 41697172 | solution.py:102
  169.9 9.3 %fusion.164 = f32[3,64,8,16,128]{4,3,2,0,1:T(8,128)} fusion(f32[64,128,3,8,8]{1,4,3,2,0:T(8,128)S(1)} %fusion.163, s32[64,8]{1,0:T(8,128)S(1)} %get-tuple-element.556), kind=kOutput, calls=%fused_computation.73.clone.1 | convolution fusion | flops 301998080 | bytes 18876416 | tf_op jit(solution)/shard_map/while/body/eval_jaxpr/cbijz,bjy->cbiyz/dot_general | solution.py:98
  179.3 15.2 %fusion.165 = f32[3,24,16,128]{3,1,2,0:T(8,128)S(1)} fusion(f32[3,64,8,16,128]{4,3,2,0,1:T(8,128)} %fusion.164, f32[3,24,16,128]{3,1,2,0:T(8,128)S(1)} %get-tuple-element.591, pred[]{:T(512)S(6)} %compare.128, s32[64,8]{0,1:T(8,128)S(1)} %iota_add_fusion.13), kind=kOutput, calls=%fused_computation.75.clone.1 | convolution fusion | flops 906276864 | bytes 13764609 | tf_op jit(solution)/shard_map/while/body/eval_jaxpr/cbiyz,bix->cxyz/dot_general | solution.py:99
  207.3 9.3 %fusion.164 = f32[3,64,8,16,128]{4,3,2,0,1:T(8,128)} fusion(f32[64,128,3,8,8]{1,4,3,2,0:T(8,128)S(1)} %fusion.163, s32[64,8]{1,0:T(8,128)S(1)} %get-tuple-element.556), kind=kOutput, calls=%fused_computation.73.clone.1 | convolution fusion | flops 301998080 | bytes 18876416 | tf_op jit(solution)/shard_map/while/body/eval_jaxpr/cbijz,bjy->cbiyz/dot_general | solution.py:98
  216.6 15.2 %fusion.165 = f32[3,24,16,128]{3,1,2,0:T(8,128)S(1)} fusion(f32[3,64,8,16,128]{4,3,2,0,1:T(8,128)} %fusion.164, f32[3,24,16,128]{3,1,2,0:T(8,128)S(1)} %get-tuple-element.591, pred[]{:T(512)S(6)} %compare.128, s32[64,8]{0,1:T(8,128)S(1)} %iota_add_fusion.13), kind=kOutput, calls=%fused_computation.75.clone.1 | convolution fusion | flops 906276864 | bytes 13764609 | tf_op jit(solution)/shard_map/while/body/eval_jaxpr/cbiyz,bix->cxyz/dot_general | solution.py:99
  244.6 9.3 %fusion.164 = f32[3,64,8,16,128]{4,3,2,0,1:T(8,128)} fusion(f32[64,128,3,8,8]{1,4,3,2,0:T(8,128)S(1)} %fusion.163, s32[64,8]{1,0:T(8,128)S(1)} %get-tuple-element.556), kind=kOutput, calls=%fused_computation.73.clone.1 | convolution fusion | flops 301998080 | bytes 18876416 | tf_op jit(solution)/shard_map/while/body/eval_jaxpr/cbijz,bjy->cbiyz/dot_general | solution.py:98
  253.9 15.2 %fusion.165 = f32[3,24,16,128]{3,1,2,0:T(8,128)S(1)} fusion(f32[3,64,8,16,128]{4,3,2,0,1:T(8,128)} %fusion.164, f32[3,24,16,128]{3,1,2,0:T(8,128)S(1)} %get-tuple-element.591, pred[]{:T(512)S(6)} %compare.128, s32[64,8]{0,1:T(8,128)S(1)} %iota_add_fusion.13), kind=kOutput, calls=%fused_computation.75.clone.1 | convolution fusion | flops 906276864 | bytes 13764609 | tf_op jit(solution)/shard_map/while/body/eval_jaxpr/cbiyz,bix->cxyz/dot_general | solution.py:99
  281.9 9.3 %fusion.164 = f32[3,64,8,16,128]{4,3,2,0,1:T(8,128)} fusion(f32[64,128,3,8,8]{1,4,3,2,0:T(8,128)S(1)} %fusion.163, s32[64,8]{1,0:T(8,128)S(1)} %get-tuple-element.556), kind=kOutput, calls=%fused_computation.73.clone.1 | convolution fusion | flops 301998080 | bytes 18876416 | tf_op jit(solution)/shard_map/while/body/eval_jaxpr/cbijz,bjy->cbiyz/dot_general | solution.py:98
  291.2 15.2 %fusion.165 = f32[3,24,16,128]{3,1,2,0:T(8,128)S(1)} fusion(f32[3,64,8,16,128]{4,3,2,0,1:T(8,128)} %fusion.164, f32[3,24,16,128]{3,1,2,0:T(8,128)S(1)} %get-tuple-element.591, pred[]{:T(512)S(6)} %compare.128, s32[64,8]{0,1:T(8,128)S(1)} %iota_add_fusion.13), kind=kOutput, calls=%fused_computation.75.clone.1 | convolution fusion | flops 906276864 | bytes 13764609 | tf_op jit(solution)/shard_map/while/body/eval_jaxpr/cbiyz,bix->cxyz/dot_general | solution.py:99
  398.2 321.7 %while.41 = (s32[]{:T(128)}, f32[4,3,64,128]{3,2,0,1:T(8,128)S(1)}, s32[4]{0:T(128)S(1)}, f32[3,256,128]{2,1,0:T(8,128)}, s32[3,256]{1,0:T(4,128)S(1)}, /*index=...) while((s32[]{:T(128)}, f32[4,3,64,128]{3,2,0,1:T(8,128)S(1)}, s32[4]{0:T(128)S(1)}, ...), condition=%wide.region_11.12_spmd, body=%wide.region_9.11_spmd.sunk | while | flops 1517614592 | bytes 48545748 | solution.py:71
  425.4 6.0 fusion.154
  431.5 43.3 %fusion.155 = f32[3,64,8,8,8]{4,2,3,0,1:T(8,128)} fusion(f32[64,8,3,8,128]{4,1,3,2,0:T(8,128)S(1)} %fusion.154, s32[64,8]{1,0:T(8,128)S(1)} %iota_add_fusion.11), kind=kOutput, calls=%fused_computation.34.clone.1 | convolution fusion | flops 151060480 | bytes 6686720 | tf_op jit(solution)/shard_map/while/body/eval_jaxpr/cbijz,bkz->cbkij/dot_general | solution.py:111
  482.6 10.3 %fusion.156 = f32[3,64,128]{2,0,1:T(4,128)S(1)} fusion(f32[64,64,128]{2,1,0:T(8,128)S(1)} %multiply_bitcast_fusion.5, f32[3,64,8,64]{3,2,0,1:T(8,128)S(1)} %copy.147, f32[3,64,8,128]{3,2,1,0:T(8,128)S(1)} %fusion.153), kind=kOutput, calls=%fused_computation.30.clone.1 | convolution fusion | flops 154116096 | bytes 3244032 | tf_op jit(solution)/shard_map/while/body/eval_jaxpr/cskp,skm->cspm/dot_general | solution.py:59
  507.2 43.3 %fusion.155 = f32[3,64,8,8,8]{4,2,3,0,1:T(8,128)} fusion(f32[64,8,3,8,128]{4,1,3,2,0:T(8,128)S(1)} %fusion.154, s32[64,8]{1,0:T(8,128)S(1)} %iota_add_fusion.11), kind=kOutput, calls=%fused_computation.34.clone.1 | convolution fusion | flops 151060480 | bytes 6686720 | tf_op jit(solution)/shard_map/while/body/eval_jaxpr/cbijz,bkz->cbkij/dot_general | solution.py:111
  558.3 10.3 %fusion.156 = f32[3,64,128]{2,0,1:T(4,128)S(1)} fusion(f32[64,64,128]{2,1,0:T(8,128)S(1)} %multiply_bitcast_fusion.5, f32[3,64,8,64]{3,2,0,1:T(8,128)S(1)} %copy.147, f32[3,64,8,128]{3,2,1,0:T(8,128)S(1)} %fusion.153), kind=kOutput, calls=%fused_computation.30.clone.1 | convolution fusion | flops 154116096 | bytes 3244032 | tf_op jit(solution)/shard_map/while/body/eval_jaxpr/cskp,skm->cspm/dot_general | solution.py:59
  582.8 43.3 %fusion.155 = f32[3,64,8,8,8]{4,2,3,0,1:T(8,128)} fusion(f32[64,8,3,8,128]{4,1,3,2,0:T(8,128)S(1)} %fusion.154, s32[64,8]{1,0:T(8,128)S(1)} %iota_add_fusion.11), kind=kOutput, calls=%fused_computation.34.clone.1 | convolution fusion | flops 151060480 | bytes 6686720 | tf_op jit(solution)/shard_map/while/body/eval_jaxpr/cbijz,bkz->cbkij/dot_general | solution.py:111
  633.9 10.3 %fusion.156 = f32[3,64,128]{2,0,1:T(4,128)S(1)} fusion(f32[64,64,128]{2,1,0:T(8,128)S(1)} %multiply_bitcast_fusion.5, f32[3,64,8,64]{3,2,0,1:T(8,128)S(1)} %copy.147, f32[3,64,8,128]{3,2,1,0:T(8,128)S(1)} %fusion.153), kind=kOutput, calls=%fused_computation.30.clone.1 | convolution fusion | flops 154116096 | bytes 3244032 | tf_op jit(solution)/shard_map/while/body/eval_jaxpr/cskp,skm->cspm/dot_general | solution.py:59
  658.5 43.3 %fusion.155 = f32[3,64,8,8,8]{4,2,3,0,1:T(8,128)} fusion(f32[64,8,3,8,128]{4,1,3,2,0:T(8,128)S(1)} %fusion.154, s32[64,8]{1,0:T(8,128)S(1)} %iota_add_fusion.11), kind=kOutput, calls=%fused_computation.34.clone.1 | convolution fusion | flops 151060480 | bytes 6686720 | tf_op jit(solution)/shard_map/while/body/eval_jaxpr/cbijz,bkz->cbkij/dot_general | solution.py:111
  709.6 10.3 %fusion.156 = f32[3,64,128]{2,0,1:T(4,128)S(1)} fusion(f32[64,64,128]{2,1,0:T(8,128)S(1)} %multiply_bitcast_fusion.5, f32[3,64,8,64]{3,2,0,1:T(8,128)S(1)} %copy.147, f32[3,64,8,128]{3,2,1,0:T(8,128)S(1)} %fusion.153), kind=kOutput, calls=%fused_computation.30.clone.1 | convolution fusion | flops 154116096 | bytes 3244032 | tf_op jit(solution)/shard_map/while/body/eval_jaxpr/cskp,skm->cspm/dot_general | solution.py:59
  721.0 10.8 %all-to-all-start.3 = ((f32[3,256,128]{2,0,1:T(4,128)}), f32[3,256,128]{2,0,1:T(4,128)S(1)}, u32[]{:S(2)}, u32[]{:S(2)}) async-start(f32[3,256,128]{2,0,1:T(4,128)} %copy.97), calls=%async_computation.3 | async-start | bytes 1048576 | tf_op jit(solution)/shard_map/all_to_all | solution.py:181
  731.8 14.1 %all-to-all-done.3 = f32[3,256,128]{2,0,1:T(4,128)S(1)} async-done(((f32[3,256,128]{2,0,1:T(4,128)}), f32[3,256,128]{2,0,1:T(4,128)S(1)}, u32[]{:S(2)}, u32[]{:S(2)}) %all-to-all-start.3) | async-done | bytes 393248 | tf_op jit(solution)/shard_map/all_to_all | solution.py:181
  (281 shorter events, 243.4 us)
Async XLA Ops:
  6.6 26.3 %all-to-all-start = ((f32[3,128,2]{0,2,1:T(2,128)}), f32[3,128,2]{0,2,1:T(2,128)S(1)}, u32[]{:S(2)}, u32[]{:S(2)}) async-start(f32[3,128,2]{0,2,1:T(2,128)} %bitcast.33), calls=%async_computation | async-start | bytes 262144 | tf_op jit(solution)/shard_map/all_to_all | solution.py:176
  32.9 26.6 %all-to-all-start.1 = ((f32[3,256,128]{2,0,1:T(4,128)}), f32[3,256,128]{2,0,1:T(4,128)S(1)}, u32[]{:S(2)}, u32[]{:S(2)}) async-start(f32[3,256,128]{2,0,1:T(4,128)} %scatter_fusion), calls=%async_computation.1 | async-start | bytes 1048576 | tf_op jit(solution)/shard_map/all_to_all | solution.py:174
  43.2 26.8 %collective-permute-start.1 = (f32[3,1,8,128]{3,2,1,0:T(8,128)S(1)}, f32[3,1,8,128]{3,2,1,0:T(8,128)S(1)}, u32[]{:S(2)}, u32[]{:S(2)}) collective-permute-start(f32[3,1,8,128]{3,2,1,0:T(8,128)S(1)} %get-tuple-element.417), channel_id=1, source_target_pairs={{0,16},{16,32},{32,48},{48,64},{64,80},{80,96},{96,112},{112,0},{1... | collective-permute-start | bytes 36872 | tf_op jit(solution)/shard_map/ppermute | solution.py:20
  44.8 25.2 %collective-permute-start = (f32[3,1,8,128]{3,2,1,0:T(8,128)S(1)}, f32[3,1,8,128]{3,2,1,0:T(8,128)S(1)}, u32[]{:S(2)}, u32[]{:S(2)}) collective-permute-start(f32[3,1,8,128]{3,2,1,0:T(8,128)S(1)} %get-tuple-element.416), channel_id=1, source_target_pairs={{16,0},{32,16},{48,32},{64,48},{80,64},{96,80},{112,96},{0,112},{1... | collective-permute-start | bytes 36872 | tf_op jit(solution)/shard_map/ppermute | solution.py:23
  59.6 23.9 %all-to-all-start.2 = ((f32[3,256,128]{2,0,1:T(4,128)}), f32[3,256,128]{2,0,1:T(4,128)S(1)}, u32[]{:S(2)}, u32[]{:S(2)}) async-start(f32[3,256,128]{2,0,1:T(4,128)} %scatter_fusion.1), calls=%async_computation.2 | async-start | bytes 1048576 | tf_op jit(solution)/shard_map/all_to_all | solution.py:175
  307.0 2.4 collective-permute-start.4
  307.8 4.1 collective-permute-start.5
  307.9 9.0 %collective-permute-start.2 = (f32[3,18,1,128]{3,2,1,0:T(1,128)S(1)}, f32[3,18,1,128]{3,2,1,0:T(1,128)S(1)}, u32[]{:S(2)}, u32[]{:S(2)}) collective-permute-start(f32[3,18,1,128]{3,2,1,0:T(1,128)S(1)} %get-tuple-element.411), channel_id=1, source_target_pairs={{1,0},{2,1},{3,2},{4,3},{5,4},{6,5},{7,6},{8,7},{9,8},{10,9},{11,1... | collective-permute-start | bytes 82952 | tf_op jit(solution)/shard_map/ppermute | solution.py:23
  308.9 7.9 %collective-permute-start.3 = (f32[3,18,1,128]{3,2,1,0:T(1,128)S(1)}, f32[3,18,1,128]{3,2,1,0:T(1,128)S(1)}, u32[]{:S(2)}, u32[]{:S(2)}) collective-permute-start(f32[3,18,1,128]{3,2,1,0:T(1,128)S(1)} %get-tuple-element.410), channel_id=1, source_target_pairs={{0,1},{1,2},{2,3},{3,4},{4,5},{5,6},{6,7},{7,8},{8,9},{9,10},{10,1... | collective-permute-start | bytes 82952 | tf_op jit(solution)/shard_map/ppermute | solution.py:20
  312.0 9.0 %collective-permute-start.6 = (f32[3,28,3,128]{3,2,1,0:T(4,128)S(1)}, f32[3,28,3,128]{3,2,1,0:T(4,128)S(1)}, u32[]{:S(2)}, u32[]{:S(2)}) collective-permute-start(f32[3,28,3,128]{3,2,1,0:T(4,128)S(1)} %get-tuple-element.402), channel_id=1, source_target_pairs={{0,1},{1,2},{2,3},{3,4},{4,5},{5,6},{6,7},{7,8},{8,9},{9,10},{10,1... | collective-permute-start | bytes 387080 | tf_op jit(solution)/shard_map/ppermute | solution.py:20
  312.4 8.6 %collective-permute-start.7 = (f32[3,28,3,128]{3,2,1,0:T(4,128)S(1)}, f32[3,28,3,128]{3,2,1,0:T(4,128)S(1)}, u32[]{:S(2)}, u32[]{:S(2)}) collective-permute-start(f32[3,28,3,128]{3,2,1,0:T(4,128)S(1)} %get-tuple-element.403), channel_id=1, source_target_pairs={{1,0},{2,1},{3,2},{4,3},{5,4},{6,5},{7,6},{8,7},{9,8},{10,9},{11,1... | collective-permute-start | bytes 387080 | tf_op jit(solution)/shard_map/ppermute | solution.py:23
  321.6 3.1 collective-permute-start.8
  323.1 1.7 collective-permute-start.9
  324.8 5.6 collective-permute-start.10
  329.5 6.0 collective-permute-start.11
  336.1 5.9 collective-permute-start.12
  342.4 2.7 collective-permute-start.14
  342.5 5.9 collective-permute-start.15
  348.7 5.1 collective-permute-start.16
  354.2 2.7 collective-permute-start.18
  354.3 5.9 collective-permute-start.19
  360.5 5.1 collective-permute-start.20
  366.0 2.7 collective-permute-start.22
  366.0 5.9 collective-permute-start.23
  372.3 5.1 collective-permute-start.24
  377.7 2.7 collective-permute-start.26
  377.8 5.9 collective-permute-start.27
  384.1 5.0 collective-permute-start.28
  387.1 3.4 collective-permute-start.29
  390.6 7.3 collective-permute-start.30
  390.7 7.2 collective-permute-start.31
  721.0 24.9 %all-to-all-start.3 = ((f32[3,256,128]{2,0,1:T(4,128)}), f32[3,256,128]{2,0,1:T(4,128)S(1)}, u32[]{:S(2)}, u32[]{:S(2)}) async-start(f32[3,256,128]{2,0,1:T(4,128)} %copy.97), calls=%async_computation.3 | async-start | bytes 1048576 | tf_op jit(solution)/shard_map/all_to_all | solution.py:181
  (14 other events, 1191.0 us)
where the time goes:
time: 753 us; the launch traced here: 748 us
  matrix products  431 us (57%)
  local copies, waits for them, and re-layouts  102 us (14%)
  starting transfers between devices  90 us (12%)
  waiting for transfers between devices  68 us (9%)
  loops' own time  36.5 us (5%)
  other arithmetic  18.1 us (2%)
    dot_general x4, matrix products, gather_boxes(): cube = jnp.einsum('cbijz,bkz->cbkij', planes, along_z, precision=highest)  173 us
    dot_general x4, matrix products, add_block(): jnp.einsum('cbiyz,bix->cxyz', rows_y, along_x, precision=highest)  61 us
    dot_general x4, matrix products, spread(): jnp.einsum('cspm,skm->cskp', loaded, weights[2], precision=highest)  52.3 us
    dot_general x4, matrix products, interpolate(): jnp.einsum('cskp,skm->cspm', cubes, weights[2], precision=highest)  41.2 us
    dot_general x4, matrix products, add_block(): rows_y = jnp.einsum('cbijz,bjy->cbiyz', planes, along_y, precision=highest)  37.2 us
    ppermute x16, starting transfers between devices, with_halo(): lax.ppermute(lax.slice_in_dim(block, 0, width, axis=dim), axis, backward)  35.8 us
    another operation x2, loops' own time, by_blocks(): stacked = lax.map(handle, starts)  35.7 us
    scatter x3, local copies, waits for them, and re-layouts, pack(): return empty.at[:, target].set(values, mode='drop')  27.1 us
  transfers between devices with their start and end apart: 36, of which 26 were waited for; matrix products, arithmetic and copies ran while one was open for 4% of the time, Pallas kernels for 0%

commit v1 on v0

v1 whole, which is shorter than its diff:
```python
import functools
import jax, jax.numpy as jnp
from jax import lax
from jax.experimental import pallas as pl
from jax.experimental.pallas import tpu as pltpu
from jax.sharding import PartitionSpec as P

JAC = 4
time_step = 0.5
viscosity = 0.1

F32 = jnp.float32
BF = jnp.bfloat16

def split(v):
    hi = v.astype(BF)
    lo = (v - hi.astype(F32)).astype(BF)
    return hi, lo

def fill_tables(r_ref, fl, a1, a2, q8, sources):
    def body(b, carry):
        t = r_ref[pl.ds(b * 8, 8), 0:8, :].reshape(64, 128)
        whole = jnp.floor(t)
        f = t - whole
        rows = pl.ds(pl.multiple_of(b * 64, 64), 64)
        fl[rows, :] = whole
        a1[rows, :] = (3.0 - 2.0 * f) * 0.125
        a2[rows, :] = (1.0 + 2.0 * f) * 0.125
        q8[rows, :] = jnp.sqrt(1.0 + 4.0 * f * (1.0 - f)) * 0.125
        return carry
    lax.fori_loop(0, sources // 8, body, 0)

def weight(cells, row, tabs):
    fl, a1, a2, q8 = [t[pl.ds(row, 1), :] for t in tabs]
    e = cells - fl
    s = jnp.where(e < 0.5, a1, a2)
    g = e * (e - 1.0)
    return jnp.where(g < 1.0, s + q8, jnp.where(g < 3.0, s - q8, 0.0))

def plane(base_s, p, row, tabs, wxs, iota8, iota16):
    wx = weight(iota8, row, tabs)
    y0 = base_s[p * 3 + 1].astype(F32)
    wy = weight(iota16 - y0, row + 1, tabs)
    wxs[...] = wx
    return jnp.concatenate([wxs[pl.ds(i, 1), :] * wy for i in range(8)], axis=0)

def spread_body(unroll, base_s, r_ref, out, fl, a1, a2, q8, acc, wxs, tot):
    sources = r_ref.shape[0]
    tabs = (fl, a1, a2, q8)
    def zero(x, carry):
        acc[x] = jnp.zeros((3, 128, 128), F32)
        return carry
    lax.fori_loop(0, 16, zero, 0)
    fill_tables(r_ref, *tabs, sources)
    iota8 = lax.broadcasted_iota(jnp.int32, (8, 128), 0).astype(F32) - 3.0
    iota16 = lax.broadcasted_iota(jnp.int32, (16, 128), 0).astype(F32) - 3.0
    def body(t, carry):
        res = []
        for u in range(unroll):
            s = t * unroll + u
            for r in range(2):
                p = s * 2 + r
                row = s * 8 + r * 3
                B = plane(base_s, p, row, tabs, wxs.at[u * 2 + r], iota8, iota16)
                wz = weight(iota8, row + 2, tabs)
                A = jnp.concatenate([r_ref[s, pl.ds(8 + r * 3 + c, 1), :] * wz for c in range(3)], axis=0)
                ah, al = split(A)
                bh, bl = split(B)
                o = lax.dot_general(jnp.concatenate([ah, al], 0), jnp.concatenate([bh, bl], 0), (((1,), (1,)), ((), ())), preferred_element_type=F32)
                res.append((p, o[:24, :128] + o[24:, :128] + o[:24, 128:]))
        for p, o in res:
            x0 = base_s[p * 3]
            z0 = jnp.maximum(base_s[p * 3 + 2] - 3, 0)
            for c in range(3):
                acc[x0, c, pl.ds(z0, 8), :] += o[c * 8:c * 8 + 8]
        return carry
    lax.fori_loop(0, sources // unroll, body, 0)
    lane = lax.broadcasted_iota(jnp.int32, (128, 128), 1)
    for c in range(3):
        tiles = [None] * 3
        for t in range(2):
            for r in range(8):
                a = acc[8 * t + r, c]
                if r == 0:
                    parts = [(t, a)]
                else:
                    a = pltpu.roll(a, 16 * r, 1)
                    parts = [(t, jnp.where(lane >= 16 * r, a, 0.0)), (t + 1, jnp.where(lane < 16 * r, a, 0.0))]
                for k, v in parts:
                    if tiles[k] is None:
                        tot[k] = v
                        tiles[k] = 1
                    else:
                        tot[k] += v
        for k in range(3):
            out[c, 8 * k:8 * k + 8] = tot[k].T.reshape(8, 16, 128)

def spread_call(base, R, unroll=2, vmem=48*2**20):
    n = R.shape[0]
    return pl.pallas_call(
        functools.partial(spread_body, unroll),
        out_shape=jax.ShapeDtypeStruct((3, 24, 16, 128), F32),
        in_specs=[pl.BlockSpec(memory_space=pltpu.SMEM), pl.BlockSpec(memory_space=pltpu.VMEM)],
        out_specs=pl.BlockSpec(memory_space=pltpu.VMEM),
        scratch_shapes=[pltpu.VMEM((n * 8, 128), F32)] * 4 + [pltpu.VMEM((16, 3, 128, 128), F32), pltpu.VMEM((2 * unroll, 8, 128), F32), pltpu.VMEM((3, 128, 128), F32)],
        compiler_params=pltpu.CompilerParams(vmem_limit_bytes=vmem),
        name="spread",
    )(base, R)

def interp_body(unroll, base_s, r_ref, v_ref, out, fl, a1, a2, q8, cop, wxs):
    sources = r_ref.shape[0]
    tabs = (fl, a1, a2, q8)
    fill_tables(r_ref, *tabs, sources)
    lane = lax.broadcasted_iota(jnp.int32, (128, 128), 1)
    for c in range(3):
        tiles = [v_ref[c, 8 * k:8 * k + 8].reshape(128, 128).T for k in range(3)]
        for r in range(8):
            if r == 0:
                cop[0, c], cop[8, c] = tiles[0], tiles[1]
            else:
                ro = [pltpu.roll(x, 128 - 16 * r, 1) for x in tiles]
                for t in range(2):
                    cop[8 * t + r, c] = jnp.where(lane < 128 - 16 * r, ro[t], ro[t + 1])
    iota8 = lax.broadcasted_iota(jnp.int32, (8, 128), 0).astype(F32) - 3.0
    iota16 = lax.broadcasted_iota(jnp.int32, (16, 128), 0).astype(F32) - 3.0
    def body(t, carry):
        for u in range(unroll):
            s = t * unroll + u
            for r in range(2):
                p = s * 2 + r
                row = s * 8 + r * 3
                B = plane(base_s, p, row, tabs, wxs.at[u * 2 + r], iota8, iota16)
                wz = weight(iota8, row + 2, tabs)
                x0 = base_s[p * 3]
                z0 = jnp.maximum(base_s[p * 3 + 2] - 3, 0)
                A = jnp.concatenate([cop[x0, c, pl.ds(z0, 8), :] for c in range(3)], axis=0)
                ah, al = split(A)
                bh, bl = split(B)
                o = jnp.dot(jnp.concatenate([ah, al], 0), jnp.concatenate([bh, bl], 1), preferred_element_type=F32)
                o = o[:24, :128] + o[24:, :128] + o[:24, 128:]
                for c in range(3):
                    out[s, pl.ds(r * 3 + c, 1), :] = jnp.sum(o[8 * c:8 * c + 8] * wz, axis=0, keepdims=True)
        return carry
    lax.fori_loop(0, sources // unroll, body, 0)

def interp_call(base, R, V, unroll=2, vmem=48*2**20):
    n = R.shape[0]
    return pl.pallas_call(
        functools.partial(interp_body, unroll),
        out_shape=jax.ShapeDtypeStruct((n, 8, 128), F32),
        in_specs=[pl.BlockSpec(memory_space=pltpu.SMEM), pl.BlockSpec(memory_space=pltpu.VMEM), pl.BlockSpec(memory_space=pltpu.VMEM)],
        out_specs=pl.BlockSpec(memory_space=pltpu.VMEM),
        scratch_shapes=[pltpu.VMEM((n * 8, 128), F32)] * 4 + [pltpu.VMEM((16, 3, 128, 128), F32), pltpu.VMEM((2 * unroll, 8, 128), F32)],
        compiler_params=pltpu.CompilerParams(vmem_limit_bytes=vmem),
        name="interp",
    )(base, R, V)


def split3(v):
    hi = v.astype(BF)
    rest = v - hi.astype(F32)
    mid = rest.astype(BF)
    return hi, mid, (rest - mid.astype(F32)).astype(BF)


def routes(owner_row, count):
    rows = lax.broadcasted_iota(jnp.int32, (128, 128), 0)
    slots = lax.broadcasted_iota(jnp.int32, (128, 128), 1)
    match = jnp.where((owner_row == rows) & (slots < count), 1.0, 0.0)
    before = jnp.where(rows < slots, 1.0, 0.0)
    rank = jnp.dot(match.astype(BF), before.astype(BF), preferred_element_type=F32)
    return jnp.where(rank < 0.5, match, 0.0), jnp.where(rank < 0.5, 0.0, match)


def spread_rows(stage, row, values):
    for d in range(0, 128, 8):
        stage[pl.ds(d * 16 + row, 8, stride=16), :] = values[d:d + 8]


def pack_rows(first, second, off_ref, frc_ref, base_ref, stage):
    both = jnp.concatenate([first, second], axis=0).astype(BF)
    for q in range(6):
        data = off_ref[q] if q < 3 else frc_ref[q - 3]
        parts = jnp.concatenate(split3(data), axis=1)
        got = jnp.dot(both, parts, preferred_element_type=F32)
        got = got[:, :128] + (got[:, 128:256] + got[:, 256:])
        for r in range(2):
            spread_rows(stage, (q // 3) * 8 + r * 3 + q % 3, got[r * 128:r * 128 + 128])
    rows = base_ref[...].astype(F32)
    none = jnp.zeros((122, 128), F32)
    blank = jnp.zeros((3, 128), F32)
    dims = (((1,), (1,)), ((), ()))
    one = jnp.concatenate([rows, blank, none], axis=0).astype(BF)
    two = jnp.concatenate([blank, rows, none], axis=0).astype(BF)
    corner = lax.dot_general(both[:128], one, dims, preferred_element_type=F32)
    corner += lax.dot_general(both[128:], two, dims, preferred_element_type=F32)
    spread_rows(stage, 6, corner)
    for row in (7, 14, 15):
        spread_rows(stage, row, jnp.zeros((128, 128), F32))


def pack_body(count_s, owner_ref, off_ref, frc_ref, base_ref, stage, back):
    first, second = routes(owner_ref[...], count_s[0])
    back[:, :128] = first.T
    back[:, 128:] = second.T
    pack_rows(first, second, off_ref, frc_ref, base_ref, stage)


def unpack_body(back, ret_ref, out):
    pick = back[...].astype(BF)
    for c in range(3):
        data = jnp.concatenate([ret_ref[pl.ds(r * 3 + c, 128, stride=8), :] for r in range(2)], axis=0)
        got = jnp.dot(pick, jnp.concatenate(split3(data), axis=1), preferred_element_type=F32)
        out[c] = got[:, :128] + (got[:, 128:256] + got[:, 256:])


VM = pl.BlockSpec(memory_space=pltpu.VMEM)
SM = pl.BlockSpec(memory_space=pltpu.SMEM)


def with_halo(block, sides, width):
    for axis, dim in sides:
        count = lax.axis_size(axis)
        forward = [(i, i + 1) for i in range(count - 1)]
        forward.append((count - 1, 0))
        backward = [(target, source) for source, target in forward]
        low = lax.ppermute(
            lax.slice_in_dim(block, block.shape[dim] - width, None, axis=dim), axis, forward
        )
        high = lax.ppermute(lax.slice_in_dim(block, 0, width, axis=dim), axis, backward)
        block = jnp.concatenate([low, block, high], axis=dim)
    return block


def neighbour_sum(padded):
    return (
        padded[..., 2:, 1:-1, 1:-1]
        + padded[..., :-2, 1:-1, 1:-1]
        + padded[..., 1:-1, 2:, 1:-1]
        + padded[..., 1:-1, :-2, 1:-1]
        + padded[..., 1:-1, 1:-1, 2:]
        + padded[..., 1:-1, 1:-1, :-2]
    )


def divergence(padded):
    return (
        0.5
        * (
            padded[0, 2:, 1:-1, 1:-1]
            - padded[0, :-2, 1:-1, 1:-1]
            + (padded[1, 1:-1, 2:, 1:-1] - padded[1, 1:-1, :-2, 1:-1])
            + (padded[2, 1:-1, 1:-1, 2:] - padded[2, 1:-1, 1:-1, :-2])
        )
    )[None]


def gradient(padded):
    return 0.5 * jnp.stack(
        [
            padded[0, 2:, 1:-1, 1:-1] - padded[0, :-2, 1:-1, 1:-1],
            padded[0, 1:-1, 2:, 1:-1] - padded[0, 1:-1, :-2, 1:-1],
            padded[0, 1:-1, 1:-1, 2:] - padded[0, 1:-1, 1:-1, :-2],
        ]
    )


def pad_depth(grid_field):
    return jnp.pad(grid_field, ((0, 0), (0, 0), (0, 0), (1, 1)))


def extend(grid_field):
    widened = with_halo(grid_field, (("gx", 1), ("gy", 2)), 1)
    return pad_depth(widened)


def grow_rims(grid_field):
    return with_halo(grid_field, (("gx", 1), ("gy", 2)), 3)


def fold_rims(widened, axis_dim, length):
    middle = lax.slice_in_dim(widened, 6, 6 + length, axis=axis_dim)
    lower_rim = lax.slice_in_dim(widened, 0, 3, axis=axis_dim)
    upper_rim = lax.slice_in_dim(widened, length + 9, length + 12, axis=axis_dim)
    low_pad = [(0, 0)] * widened.ndim
    low_pad[axis_dim] = (0, length - 3)
    high_pad = [(0, 0)] * widened.ndim
    high_pad[axis_dim] = (length - 3, 0)
    return middle + jnp.pad(lower_rim, low_pad) + jnp.pad(upper_rim, high_pad)


def shards(velocity, offsets, forces, owner, base, counts):
    width_x = velocity.shape[1]
    width_y = velocity.shape[2]
    axes = ("gx", "gy")
    stage, back = pl.pallas_call(
        pack_body,
        out_shape=(jax.ShapeDtypeStruct((2048, 128), F32), jax.ShapeDtypeStruct((128, 256), F32)),
        in_specs=[SM, VM, VM, VM, VM],
        out_specs=(VM, VM),
        compiler_params=pltpu.CompilerParams(vmem_limit_bytes=32 * 2**20),
        name="pack",
    )(counts, owner.reshape(1, 128), offsets, forces, base)
    arrived = lax.all_to_all(stage.reshape(128, 16, 128), axes, split_axis=0, concat_axis=0, tiled=True)
    corners = arrived[:, 6, :6].astype(jnp.int32).reshape(-1)
    spread_grid = spread_call(corners, arrived, 4)
    widened = grow_rims(spread_grid[:, : width_x + 6, : width_y + 6])
    force_field = fold_rims(fold_rims(widened, 1, width_x), 2, width_y)
    laplace = neighbour_sum(extend(velocity)) - 6.0 * velocity
    provisional = velocity + time_step * (viscosity * laplace + force_field)
    source = divergence(extend(provisional)) / time_step
    pressure = -source / 6.0
    for sweep in range(JAC - 1):
        pressure = (neighbour_sum(extend(pressure)) - source) / 6.0
    new_velocity = provisional - time_step * gradient(extend(pressure))
    sampled = jnp.pad(grow_rims(new_velocity), ((0, 0), (0, 2), (0, 2), (0, 0)))
    answers = interp_call(corners, arrived, sampled, 4)
    returned = lax.all_to_all(answers, axes, split_axis=0, concat_axis=0, tiled=True)
    marker_velocity = pl.pallas_call(
        unpack_body,
        out_shape=jax.ShapeDtypeStruct((3, 128, 128), F32),
        in_specs=[VM, VM],
        out_specs=VM,
        compiler_params=pltpu.CompilerParams(vmem_limit_bytes=32 * 2**20),
        name="unpack",
    )(back, returned.reshape(1024, 128))
    return (new_velocity, pressure[0], marker_velocity)


def solution(mesh):
    return jax.shard_map(
        shards,
        mesh=mesh,
        in_specs=(
            P(None, "gx", "gy", None),
            P(None, ("gx", "gy"), None),
            P(None, ("gx", "gy"), None),
            P(("gx", "gy")),
            P(None, ("gx", "gy")),
            P(("gx", "gy")),
        ),
        out_specs=(P(None, "gx", "gy", None), P("gx", "gy", None), P(None, ("gx", "gy"), None)),
        check_vma=False,
    )
```

time: 753 us -> 179 us (0.24)
  matrix products: 431 us -> 0 us
  local copies, waits for them, and re-layouts: 102 us -> 3.47 us
  loops' own time: 36.5 us -> 0 us
  starting transfers between devices: 90 us -> 60.3 us
  Pallas kernels: 0 us -> 26.8 us
  blocking collectives: 0 us -> 24.7 us
  other arithmetic: 18.1 us -> 3.55 us
  waiting for transfers between devices: 68 us -> 58.1 us
    dot_general x32 -> x0, matrix products: 431 us -> none  [the longest x4 173 us: gather_boxes(): cube = jnp.einsum('cbijz,bkz->cbkij', planes, along_z, precision=highest)]
    another operation x3 -> x0, loops' own time: 36.5 us -> none  [the longest x2 35.7 us: by_blocks(): stacked = lax.map(handle, starts)]
    all_to_all x4 -> x1, starting transfers between devices: 41.7 us -> 11.5 us  [shards(): lax.all_to_all(stage.reshape(128, 16, 128), axes, split_axis=0, concat_ax...]
    scatter x3 -> x0, local copies, waits for them, and re-layouts: 27.1 us -> none  [pack(): return empty.at[:, target].set(values, mode='drop')]
    pallas_call x0 -> x4, Pallas kernels: none -> 26.8 us  [the longest x1 12.8 us: spread_call(): pl.pallas_call(functools.partial(spread_body, unroll), out_shape=jax.Shap...]
    reshape x9 -> x0, local copies, waits for them, and re-layouts: 25.9 us -> none  [the longest x4 23.6 us: add_block(): lax.dynamic_slice_in_dim(box_values, start, block_rows, 1)]
    all_to_all x0 -> x1, blocking collectives: none -> 24.7 us  [shards(): lax.all_to_all(answers, axes, split_axis=0, concat_axis=0, tiled=True)]
    transpose x4 -> x0, local copies, waits for them, and re-layouts: 20.9 us -> none  [gather_boxes(): cube = jnp.einsum('cbijz,bkz->cbkij', planes, along_z, precision=highest)]
  transfers between devices with their start and end apart: 36 -> 33, of which waited for: 26 -> 27; matrix products, arithmetic and copies ran while one was open for 4% -> 0% of each run, Pallas kernels for 0% -> 0%
where the time goes in v1:
time: 179 us; the launch traced here: 178 us
  starting transfers between devices  60.3 us (34%)
  waiting for transfers between devices  58.1 us (32%)
  Pallas kernels  26.8 us (15%)
  blocking collectives  24.7 us (14%)
  other arithmetic  3.55 us (2%)
  local copies, waits for them, and re-layouts  3.47 us (2%)
    ppermute x16, starting transfers between devices, with_halo(): lax.ppermute(lax.slice_in_dim(block, 0, width, axis=dim), axis, backward)  35.8 us
    ppermute x16, waiting for transfers between devices, with_halo(): lax.ppermute(lax.slice_in_dim(block, block.shape[dim] - width, None, axis...  27.3 us
    all_to_all x1, blocking collectives, shards(): lax.all_to_all(answers, axes, split_axis=0, concat_axis=0, tiled=True)  24.7 us
    ppermute x16, waiting for transfers between devices, with_halo(): lax.ppermute(lax.slice_in_dim(block, 0, width, axis=dim), axis, backward)  20.2 us
    ppermute x16, starting transfers between devices, with_halo(): lax.ppermute(lax.slice_in_dim(block, block.shape[dim] - width, None, axis...  13 us
    pallas_call x1, Pallas kernels, spread_call(): pl.pallas_call(functools.partial(spread_body, unroll), out_shape=jax.Shap...  12.8 us
    all_to_all x1, starting transfers between devices, shards(): lax.all_to_all(stage.reshape(128, 16, 128), axes, split_axis=0, concat_ax...  11.5 us
    pallas_call x1, Pallas kernels, interp_call(): pl.pallas_call(functools.partial(interp_body, unroll), out_shape=jax.Shap...  11.1 us
  transfers between devices with their start and end apart: 33, of which 27 were waited for; matrix products, arithmetic and copies ran while one was open for 0% of the time, Pallas kernels for 0%

profile of v1, /device:TPU:1, one launch (start us, length us, event | category | flops | bytes accessed | tf_op | source)
XLA Modules:
  0.0 178.5 jit_solution(10019308499212664795)
XLA Ops:
  3.8 1.9 %pack.1 = (f32[2048,128]{1,0:T(8,128)}, f32[128,256]{1,0:T(8,128)S(1)}) custom-call(s32[1]{0:T(128)S(6)} %copy.11.count_s, s32[1,128]{1,0:T(1,128)S(1)} %bitcast.5, f32[3,128,128]{2,1,0:T(8,128)S(1)} %copy-done, f32[3,128,128]{2,1,0:T(8,128)S(1)} %copy-done.1, s32[3,128]{1,0:T(4,128)S(1)} %copy-done.2), custom_call_target="tpu_custom_call" | custom-call | tf_op jit(solution)/shard_map/pack/pallas_call | solution.py:296
  5.7 11.5 %all-to-all-start = ((f32[128,16,128]{2,1,0:T(8,128)}), f32[128,16,128]{2,1,0:T(8,128)S(1)}, u32[]{:S(2)}, u32[]{:S(2)}) async-start(f32[128,16,128]{2,1,0:T(8,128)} %bitcast.1), calls=%async_computation | async-start | bytes 2097152 | tf_op jit(solution)/shard_map/all_to_all | solution.py:304
  17.2 1.6 collective-permute-start.1
  19.8 6.1 %collective-permute-done = f32[3,1,8,128]{3,2,1,0:T(8,128)S(1)} collective-permute-done((f32[3,1,8,128]{3,2,1,0:T(8,128)S(1)}, f32[3,1,8,128]{3,2,1,0:T(8,128)S(1)}, u32[]{:S(2)}, u32[]{:S(2)}) %collective-permute-start) | collective-permute-done | bytes 12320 | tf_op jit(solution)/shard_map/ppermute | solution.py:230
  25.9 10.6 %all-to-all-done.r_ref = f32[128,16,128]{2,1,0:T(8,128)S(1)} async-done(((f32[128,16,128]{2,1,0:T(8,128)}), f32[128,16,128]{2,1,0:T(8,128)S(1)}, u32[]{:S(2)}, u32[]{:S(2)}) %all-to-all-start) | async-done | bytes 1048608 | tf_op jit(solution)/shard_map/all_to_all | solution.py:304
  36.9 12.8 %spread.1 = f32[3,24,16,128]{3,2,1,0:T(8,128)S(1)} custom-call(s32[768]{0:T(1024)S(1)} %convert_element_type.26.base_s, f32[128,16,128]{2,1,0:T(8,128)S(1)} %all-to-all-done.r_ref), custom_call_target="tpu_custom_call" | custom-call | tf_op jit(solution)/shard_map/spread/pallas_call | solution.py:100
  52.4 2.4 %collective-permute-done.5 = f32[3,3,14,128]{3,2,1,0:T(8,128)S(1)} collective-permute-done((f32[3,3,14,128]{3,2,1,0:T(8,128)S(1)}, f32[3,3,14,128]{3,2,1,0:T(8,128)S(1)}, u32[]{:S(2)}, u32[]{:S(2)}) %collective-permute-start.5) | collective-permute-done | bytes 64544 | tf_op jit(solution)/shard_map/ppermute | solution.py:230
  55.4 4.4 %collective-permute-start.7 = (f32[3,28,3,128]{3,2,1,0:T(4,128)S(1)}, f32[3,28,3,128]{3,2,1,0:T(4,128)S(1)}, u32[]{:S(2)}, u32[]{:S(2)}) collective-permute-start(f32[3,28,3,128]{3,2,1,0:T(4,128)S(1)} %get-tuple-element.10), channel_id=1, source_target_pairs={{1,0},{2,1},{3,2},{4,3},{5,4},{6,5},{7,6},{8,7},{9,8},{10,9},{11,1... | collective-permute-start | bytes 387080 | tf_op jit(solution)/shard_map/ppermute | solution.py:230
  60.3 3.7 %collective-permute-done.6 = f32[3,28,3,128]{3,2,1,0:T(4,128)S(1)} collective-permute-done((f32[3,28,3,128]{3,2,1,0:T(4,128)S(1)}, f32[3,28,3,128]{3,2,1,0:T(4,128)S(1)}, u32[]{:S(2)}, u32[]{:S(2)}) %collective-permute-start.6) | collective-permute-done | bytes 129056 | tf_op jit(solution)/shard_map/ppermute | solution.py:227
  65.2 1.4 collective-permute-start.8
  67.0 1.4 collective-permute-done.8
  68.4 4.6 %collective-permute-start.10 = (f32[3,18,1,128]{3,2,1,0:T(1,128)S(1)}, f32[3,18,1,128]{3,2,1,0:T(1,128)S(1)}, u32[]{:S(2)}, u32[]{:S(2)}) collective-permute-start(f32[3,18,1,128]{3,2,1,0:T(1,128)S(1)} %get-tuple-element.16), channel_id=1, source_target_pairs={{1,0},{2,1},{3,2},{4,3},{5,4},{6,5},{7,6},{8,7},{9,8},{10,9},{11,1... | collective-permute-start | bytes 82952 | tf_op jit(solution)/shard_map/ppermute | solution.py:230
  74.0 5.1 %collective-permute-done.11 = f32[3,18,1,128]{3,2,1,0:T(1,128)S(1)} collective-permute-done((f32[3,18,1,128]{3,2,1,0:T(1,128)S(1)}, f32[3,18,1,128]{3,2,1,0:T(1,128)S(1)}, u32[]{:S(2)}, u32[]{:S(2)}) %collective-permute-start.11) | collective-permute-done | bytes 27680 | tf_op jit(solution)/shard_map/ppermute | solution.py:227
  79.7 5.1 %collective-permute-start.12 = (f32[1,1,8,128]{3,2,1,0:T(8,128)S(1)}, f32[1,1,8,128]{3,2,1,0:T(8,128)S(1)}, u32[]{:S(2)}, u32[]{:S(2)}) collective-permute-start(f32[1,1,8,128]{3,2,1,0:T(8,128)S(1)} %get-tuple-element.42), channel_id=1, source_target_pairs={{16,0},{32,16},{48,32},{64,48},{80,64},{96,80},{112,96},{0,112},{1... | collective-permute-start | bytes 12296 | tf_op jit(solution)/shard_map/ppermute | solution.py:230
  86.0 1.5 collective-permute-start.15
  88.6 3.3 %collective-permute-done.15 = f32[1,18,1,128]{3,2,1,0:T(1,128)S(1)} collective-permute-done((f32[1,18,1,128]{3,2,1,0:T(1,128)S(1)}, f32[1,18,1,128]{3,2,1,0:T(1,128)S(1)}, u32[]{:S(2)}, u32[]{:S(2)}) %collective-permute-start.15) | collective-permute-done | bytes 9248 | tf_op jit(solution)/shard_map/ppermute | solution.py:227
  92.3 4.3 %collective-permute-start.16 = (f32[1,1,8,128]{3,2,1,0:T(8,128)S(1)}, f32[1,1,8,128]{3,2,1,0:T(8,128)S(1)}, u32[]{:S(2)}, u32[]{:S(2)}) collective-permute-start(f32[1,1,8,128]{3,2,1,0:T(8,128)S(1)} %get-tuple-element.40), channel_id=1, source_target_pairs={{16,0},{32,16},{48,32},{64,48},{80,64},{96,80},{112,96},{0,112},{1... | collective-permute-start | bytes 12296 | tf_op jit(solution)/shard_map/ppermute | solution.py:230
  97.8 1.5 collective-permute-start.19
  100.4 3.3 %collective-permute-done.19 = f32[1,18,1,128]{3,2,1,0:T(1,128)S(1)} collective-permute-done((f32[1,18,1,128]{3,2,1,0:T(1,128)S(1)}, f32[1,18,1,128]{3,2,1,0:T(1,128)S(1)}, u32[]{:S(2)}, u32[]{:S(2)}) %collective-permute-start.19) | collective-permute-done | bytes 9248 | tf_op jit(solution)/shard_map/ppermute | solution.py:227
  104.0 4.3 %collective-permute-start.20 = (f32[1,1,8,128]{3,2,1,0:T(8,128)S(1)}, f32[1,1,8,128]{3,2,1,0:T(8,128)S(1)}, u32[]{:S(2)}, u32[]{:S(2)}) collective-permute-start(f32[1,1,8,128]{3,2,1,0:T(8,128)S(1)} %get-tuple-element.38), channel_id=1, source_target_pairs={{16,0},{32,16},{48,32},{64,48},{80,64},{96,80},{112,96},{0,112},{1... | collective-permute-start | bytes 12296 | tf_op jit(solution)/shard_map/ppermute | solution.py:230
  109.6 1.5 collective-permute-start.23
  112.2 3.3 %collective-permute-done.23 = f32[1,18,1,128]{3,2,1,0:T(1,128)S(1)} collective-permute-done((f32[1,18,1,128]{3,2,1,0:T(1,128)S(1)}, f32[1,18,1,128]{3,2,1,0:T(1,128)S(1)}, u32[]{:S(2)}, u32[]{:S(2)}) %collective-permute-start.23) | collective-permute-done | bytes 9248 | tf_op jit(solution)/shard_map/ppermute | solution.py:227
  115.8 4.3 %collective-permute-start.24 = (f32[1,1,8,128]{3,2,1,0:T(8,128)S(1)}, f32[1,1,8,128]{3,2,1,0:T(8,128)S(1)}, u32[]{:S(2)}, u32[]{:S(2)}) collective-permute-start(f32[1,1,8,128]{3,2,1,0:T(8,128)S(1)} %get-tuple-element.36), channel_id=1, source_target_pairs={{16,0},{32,16},{48,32},{64,48},{80,64},{96,80},{112,96},{0,112},{1... | collective-permute-start | bytes 12296 | tf_op jit(solution)/shard_map/ppermute | solution.py:230
  121.3 1.5 collective-permute-start.27
  123.9 3.3 %collective-permute-done.27 = f32[1,18,1,128]{3,2,1,0:T(1,128)S(1)} collective-permute-done((f32[1,18,1,128]{3,2,1,0:T(1,128)S(1)}, f32[1,18,1,128]{3,2,1,0:T(1,128)S(1)}, u32[]{:S(2)}, u32[]{:S(2)}) %collective-permute-start.27) | collective-permute-done | bytes 9248 | tf_op jit(solution)/shard_map/ppermute | solution.py:227
  127.6 3.0 %collective-permute-start.28 = (f32[3,3,8,128]{3,2,1,0:T(8,128)S(1)}, f32[3,3,8,128]{3,2,1,0:T(8,128)S(1)}, u32[]{:S(2)}, u32[]{:S(2)}) collective-permute-start(f32[3,3,8,128]{3,2,1,0:T(8,128)S(1)} %get-tuple-element.19), channel_id=1, source_target_pairs={{0,16},{16,32},{32,48},{48,64},{64,80},{80,96},{96,112},{112,0},{1... | collective-permute-start | bytes 110600 | tf_op jit(solution)/shard_map/ppermute | solution.py:227
  130.6 1.3 collective-permute-start.29
  132.6 1.4 collective-permute-done.29
  134.4 4.8 %collective-permute-start.31 = (f32[3,22,3,128]{3,2,1,0:T(4,128)S(1)}, f32[3,22,3,128]{3,2,1,0:T(4,128)S(1)}, u32[]{:S(2)}, u32[]{:S(2)}) collective-permute-start(f32[3,22,3,128]{3,2,1,0:T(4,128)S(1)} %get-tuple-element.14), channel_id=1, source_target_pairs={{1,0},{2,1},{3,2},{4,3},{5,4},{6,5},{7,6},{8,7},{9,8},{10,9},{11,1... | collective-permute-start | bytes 304136 | tf_op jit(solution)/shard_map/ppermute | solution.py:230
  139.1 2.4 %collective-permute-done.30 = f32[3,22,3,128]{3,2,1,0:T(4,128)S(1)} collective-permute-done((f32[3,22,3,128]{3,2,1,0:T(4,128)S(1)}, f32[3,22,3,128]{3,2,1,0:T(4,128)S(1)}, u32[]{:S(2)}, u32[]{:S(2)}) %collective-permute-start.30) | collective-permute-done | bytes 101408 | tf_op jit(solution)/shard_map/ppermute | solution.py:227
  141.7 11.1 %interp.1 = f32[128,8,128]{2,1,0:T(8,128)S(1)} custom-call(s32[768]{0:T(1024)S(1)} %convert_element_type.26.base_s, f32[128,16,128]{2,1,0:T(8,128)S(1)} %all-to-all-done.r_ref, f32[3,24,16,128]{3,2,1,0:T(8,128)S(1)} %select_maximum_fusion.6.v_ref), custom_call_target="tpu_custom_call" | custom-call | tf_op jit(solution)/shard_map/interp/pallas_call | solution.py:148
  152.8 24.7 %all_to_all.10 = f32[128,8,128]{2,1,0:T(8,128)S(1)} all-to-all(f32[128,8,128]{2,1,0:T(8,128)S(1)} %interp.1), channel_id=1, replica_groups=mesh['gx'=8,'gy'=16] {'gx','gy'}, dimensions={0} | all-to-all | bytes 1048576 | tf_op jit(solution)/shard_map/all_to_all | solution.py:318
  (97 shorter events, 23.8 us)
Async XLA Ops:
  5.7 30.8 %all-to-all-start = ((f32[128,16,128]{2,1,0:T(8,128)}), f32[128,16,128]{2,1,0:T(8,128)S(1)}, u32[]{:S(2)}, u32[]{:S(2)}) async-start(f32[128,16,128]{2,1,0:T(8,128)} %bitcast.1), calls=%async_computation | async-start | bytes 2097152 | tf_op jit(solution)/shard_map/all_to_all | solution.py:304
  17.2 2.6 %collective-permute-start.1 = (f32[3,1,8,128]{3,2,1,0:T(8,128)S(1)}, f32[3,1,8,128]{3,2,1,0:T(8,128)S(1)}, u32[]{:S(2)}, u32[]{:S(2)}) collective-permute-start(f32[3,1,8,128]{3,2,1,0:T(8,128)S(1)} %get-tuple-element.24), channel_id=1, source_target_pairs={{0,16},{16,32},{32,48},{48,64},{64,80},{80,96},{96,112},{112,0},{1... | collective-permute-start | bytes 36872 | tf_op jit(solution)/shard_map/ppermute | solution.py:227
  18.9 7.0 %collective-permute-start = (f32[3,1,8,128]{3,2,1,0:T(8,128)S(1)}, f32[3,1,8,128]{3,2,1,0:T(8,128)S(1)}, u32[]{:S(2)}, u32[]{:S(2)}) collective-permute-start(f32[3,1,8,128]{3,2,1,0:T(8,128)S(1)} %get-tuple-element.23), channel_id=1, source_target_pairs={{16,0},{32,16},{48,32},{64,48},{80,64},{96,80},{112,96},{0,112},{1... | collective-permute-start | bytes 36872 | tf_op jit(solution)/shard_map/ppermute | solution.py:230
  49.7 2.7 %collective-permute-start.4 = (f32[3,3,14,128]{3,2,1,0:T(8,128)S(1)}, f32[3,3,14,128]{3,2,1,0:T(8,128)S(1)}, u32[]{:S(2)}, u32[]{:S(2)}) collective-permute-start(f32[3,3,14,128]{3,2,1,0:T(8,128)S(1)} %get-tuple-element.11), channel_id=1, source_target_pairs={{0,16},{16,32},{32,48},{48,64},{64,80},{80,96},{96,112},{112,0},{1... | collective-permute-start | bytes 193544 | tf_op jit(solution)/shard_map/ppermute | solution.py:227
  50.8 4.1 %collective-permute-start.5 = (f32[3,3,14,128]{3,2,1,0:T(8,128)S(1)}, f32[3,3,14,128]{3,2,1,0:T(8,128)S(1)}, u32[]{:S(2)}, u32[]{:S(2)}) collective-permute-start(f32[3,3,14,128]{3,2,1,0:T(8,128)S(1)} %get-tuple-element.12), channel_id=1, source_target_pairs={{16,0},{32,16},{48,32},{64,48},{80,64},{96,80},{112,96},{0,112},{1... | collective-permute-start | bytes 193544 | tf_op jit(solution)/shard_map/ppermute | solution.py:230
  50.8 9.0 %collective-permute-start.2 = (f32[3,18,1,128]{3,2,1,0:T(1,128)S(1)}, f32[3,18,1,128]{3,2,1,0:T(1,128)S(1)}, u32[]{:S(2)}, u32[]{:S(2)}) collective-permute-start(f32[3,18,1,128]{3,2,1,0:T(1,128)S(1)} %get-tuple-element.18), channel_id=1, source_target_pairs={{1,0},{2,1},{3,2},{4,3},{5,4},{6,5},{7,6},{8,7},{9,8},{10,9},{11,1... | collective-permute-start | bytes 82952 | tf_op jit(solution)/shard_map/ppermute | solution.py:230
  52.0 7.8 %collective-permute-start.3 = (f32[3,18,1,128]{3,2,1,0:T(1,128)S(1)}, f32[3,18,1,128]{3,2,1,0:T(1,128)S(1)}, u32[]{:S(2)}, u32[]{:S(2)}) collective-permute-start(f32[3,18,1,128]{3,2,1,0:T(1,128)S(1)} %get-tuple-element.17), channel_id=1, source_target_pairs={{0,1},{1,2},{2,3},{3,4},{4,5},{5,6},{6,7},{7,8},{8,9},{9,10},{10,1... | collective-permute-start | bytes 82952 | tf_op jit(solution)/shard_map/ppermute | solution.py:227
  54.9 9.1 %collective-permute-start.6 = (f32[3,28,3,128]{3,2,1,0:T(4,128)S(1)}, f32[3,28,3,128]{3,2,1,0:T(4,128)S(1)}, u32[]{:S(2)}, u32[]{:S(2)}) collective-permute-start(f32[3,28,3,128]{3,2,1,0:T(4,128)S(1)} %get-tuple-element.9), channel_id=1, source_target_pairs={{0,1},{1,2},{2,3},{3,4},{4,5},{5,6},{6,7},{7,8},{8,9},{9,10},{10,1... | collective-permute-start | bytes 387080 | tf_op jit(solution)/shard_map/ppermute | solution.py:227
  55.4 8.6 %collective-permute-start.7 = (f32[3,28,3,128]{3,2,1,0:T(4,128)S(1)}, f32[3,28,3,128]{3,2,1,0:T(4,128)S(1)}, u32[]{:S(2)}, u32[]{:S(2)}) collective-permute-start(f32[3,28,3,128]{3,2,1,0:T(4,128)S(1)} %get-tuple-element.10), channel_id=1, source_target_pairs={{1,0},{2,1},{3,2},{4,3},{5,4},{6,5},{7,6},{8,7},{9,8},{10,9},{11,1... | collective-permute-start | bytes 387080 | tf_op jit(solution)/shard_map/ppermute | solution.py:230
  65.2 3.1 %collective-permute-start.8 = (f32[3,1,8,128]{3,2,1,0:T(8,128)S(1)}, f32[3,1,8,128]{3,2,1,0:T(8,128)S(1)}, u32[]{:S(2)}, u32[]{:S(2)}) collective-permute-start(f32[3,1,8,128]{3,2,1,0:T(8,128)S(1)} %get-tuple-element.22), channel_id=1, source_target_pairs={{16,0},{32,16},{48,32},{64,48},{80,64},{96,80},{112,96},{0,112},{1... | collective-permute-start | bytes 36872 | tf_op jit(solution)/shard_map/ppermute | solution.py:230
  66.7 1.7 collective-permute-start.9
  68.4 5.5 %collective-permute-start.10 = (f32[3,18,1,128]{3,2,1,0:T(1,128)S(1)}, f32[3,18,1,128]{3,2,1,0:T(1,128)S(1)}, u32[]{:S(2)}, u32[]{:S(2)}) collective-permute-start(f32[3,18,1,128]{3,2,1,0:T(1,128)S(1)} %get-tuple-element.16), channel_id=1, source_target_pairs={{1,0},{2,1},{3,2},{4,3},{5,4},{6,5},{7,6},{8,7},{9,8},{10,9},{11,1... | collective-permute-start | bytes 82952 | tf_op jit(solution)/shard_map/ppermute | solution.py:230
  73.0 6.0 %collective-permute-start.11 = (f32[3,18,1,128]{3,2,1,0:T(1,128)S(1)}, f32[3,18,1,128]{3,2,1,0:T(1,128)S(1)}, u32[]{:S(2)}, u32[]{:S(2)}) collective-permute-start(f32[3,18,1,128]{3,2,1,0:T(1,128)S(1)} %get-tuple-element.15), channel_id=1, source_target_pairs={{0,1},{1,2},{2,3},{3,4},{4,5},{5,6},{6,7},{7,8},{8,9},{9,10},{10,1... | collective-permute-start | bytes 82952 | tf_op jit(solution)/shard_map/ppermute | solution.py:227
  79.7 5.9 %collective-permute-start.12 = (f32[1,1,8,128]{3,2,1,0:T(8,128)S(1)}, f32[1,1,8,128]{3,2,1,0:T(8,128)S(1)}, u32[]{:S(2)}, u32[]{:S(2)}) collective-permute-start(f32[1,1,8,128]{3,2,1,0:T(8,128)S(1)} %get-tuple-element.42), channel_id=1, source_target_pairs={{16,0},{32,16},{48,32},{64,48},{80,64},{96,80},{112,96},{0,112},{1... | collective-permute-start | bytes 12296 | tf_op jit(solution)/shard_map/ppermute | solution.py:230
  85.9 2.7 %collective-permute-start.14 = (f32[1,18,1,128]{3,2,1,0:T(1,128)S(1)}, f32[1,18,1,128]{3,2,1,0:T(1,128)S(1)}, u32[]{:S(2)}, u32[]{:S(2)}) collective-permute-start(f32[1,18,1,128]{3,2,1,0:T(1,128)S(1)} %get-tuple-element.34), channel_id=1, source_target_pairs={{1,0},{2,1},{3,2},{4,3},{5,4},{6,5},{7,6},{8,7},{9,8},{10,9},{11,1... | collective-permute-start | bytes 27656 | tf_op jit(solution)/shard_map/ppermute | solution.py:230
  86.0 5.9 %collective-permute-start.15 = (f32[1,18,1,128]{3,2,1,0:T(1,128)S(1)}, f32[1,18,1,128]{3,2,1,0:T(1,128)S(1)}, u32[]{:S(2)}, u32[]{:S(2)}) collective-permute-start(f32[1,18,1,128]{3,2,1,0:T(1,128)S(1)} %get-tuple-element.33), channel_id=1, source_target_pairs={{0,1},{1,2},{2,3},{3,4},{4,5},{5,6},{6,7},{7,8},{8,9},{9,10},{10,1... | collective-permute-start | bytes 27656 | tf_op jit(solution)/shard_map/ppermute | solution.py:227
  92.3 5.1 %collective-permute-start.16 = (f32[1,1,8,128]{3,2,1,0:T(8,128)S(1)}, f32[1,1,8,128]{3,2,1,0:T(8,128)S(1)}, u32[]{:S(2)}, u32[]{:S(2)}) collective-permute-start(f32[1,1,8,128]{3,2,1,0:T(8,128)S(1)} %get-tuple-element.40), channel_id=1, source_target_pairs={{16,0},{32,16},{48,32},{64,48},{80,64},{96,80},{112,96},{0,112},{1... | collective-permute-start | bytes 12296 | tf_op jit(solution)/shard_map/ppermute | solution.py:230
  96.5 1.2 collective-permute-start.17
  97.7 2.7 %collective-permute-start.18 = (f32[1,18,1,128]{3,2,1,0:T(1,128)S(1)}, f32[1,18,1,128]{3,2,1,0:T(1,128)S(1)}, u32[]{:S(2)}, u32[]{:S(2)}) collective-permute-start(f32[1,18,1,128]{3,2,1,0:T(1,128)S(1)} %get-tuple-element.32), channel_id=1, source_target_pairs={{1,0},{2,1},{3,2},{4,3},{5,4},{6,5},{7,6},{8,7},{9,8},{10,9},{11,1... | collective-permute-start | bytes 27656 | tf_op jit(solution)/shard_map/ppermute | solution.py:230
  97.8 5.9 %collective-permute-start.19 = (f32[1,18,1,128]{3,2,1,0:T(1,128)S(1)}, f32[1,18,1,128]{3,2,1,0:T(1,128)S(1)}, u32[]{:S(2)}, u32[]{:S(2)}) collective-permute-start(f32[1,18,1,128]{3,2,1,0:T(1,128)S(1)} %get-tuple-element.31), channel_id=1, source_target_pairs={{0,1},{1,2},{2,3},{3,4},{4,5},{5,6},{6,7},{7,8},{8,9},{9,10},{10,1... | collective-permute-start | bytes 27656 | tf_op jit(solution)/shard_map/ppermute | solution.py:227
  104.0 5.1 %collective-permute-start.20 = (f32[1,1,8,128]{3,2,1,0:T(8,128)S(1)}, f32[1,1,8,128]{3,2,1,0:T(8,128)S(1)}, u32[]{:S(2)}, u32[]{:S(2)}) collective-permute-start(f32[1,1,8,128]{3,2,1,0:T(8,128)S(1)} %get-tuple-element.38), channel_id=1, source_target_pairs={{16,0},{32,16},{48,32},{64,48},{80,64},{96,80},{112,96},{0,112},{1... | collective-permute-start | bytes 12296 | tf_op jit(solution)/shard_map/ppermute | solution.py:230
  108.3 1.2 collective-permute-start.21
  109.5 2.7 %collective-permute-start.22 = (f32[1,18,1,128]{3,2,1,0:T(1,128)S(1)}, f32[1,18,1,128]{3,2,1,0:T(1,128)S(1)}, u32[]{:S(2)}, u32[]{:S(2)}) collective-permute-start(f32[1,18,1,128]{3,2,1,0:T(1,128)S(1)} %get-tuple-element.30), channel_id=1, source_target_pairs={{1,0},{2,1},{3,2},{4,3},{5,4},{6,5},{7,6},{8,7},{9,8},{10,9},{11,1... | collective-permute-start | bytes 27656 | tf_op jit(solution)/shard_map/ppermute | solution.py:230
  109.6 5.9 %collective-permute-start.23 = (f32[1,18,1,128]{3,2,1,0:T(1,128)S(1)}, f32[1,18,1,128]{3,2,1,0:T(1,128)S(1)}, u32[]{:S(2)}, u32[]{:S(2)}) collective-permute-start(f32[1,18,1,128]{3,2,1,0:T(1,128)S(1)} %get-tuple-element.29), channel_id=1, source_target_pairs={{0,1},{1,2},{2,3},{3,4},{4,5},{5,6},{6,7},{7,8},{8,9},{9,10},{10,1... | collective-permute-start | bytes 27656 | tf_op jit(solution)/shard_map/ppermute | solution.py:227
  115.8 5.1 %collective-permute-start.24 = (f32[1,1,8,128]{3,2,1,0:T(8,128)S(1)}, f32[1,1,8,128]{3,2,1,0:T(8,128)S(1)}, u32[]{:S(2)}, u32[]{:S(2)}) collective-permute-start(f32[1,1,8,128]{3,2,1,0:T(8,128)S(1)} %get-tuple-element.36), channel_id=1, source_target_pairs={{16,0},{32,16},{48,32},{64,48},{80,64},{96,80},{112,96},{0,112},{1... | collective-permute-start | bytes 12296 | tf_op jit(solution)/shard_map/ppermute | solution.py:230
  120.1 1.2 collective-permute-start.25
  121.2 2.7 %collective-permute-start.26 = (f32[1,18,1,128]{3,2,1,0:T(1,128)S(1)}, f32[1,18,1,128]{3,2,1,0:T(1,128)S(1)}, u32[]{:S(2)}, u32[]{:S(2)}) collective-permute-start(f32[1,18,1,128]{3,2,1,0:T(1,128)S(1)} %get-tuple-element.28), channel_id=1, source_target_pairs={{1,0},{2,1},{3,2},{4,3},{5,4},{6,5},{7,6},{8,7},{9,8},{10,9},{11,1... | collective-permute-start | bytes 27656 | tf_op jit(solution)/shard_map/ppermute | solution.py:230
  121.3 5.9 %collective-permute-start.27 = (f32[1,18,1,128]{3,2,1,0:T(1,128)S(1)}, f32[1,18,1,128]{3,2,1,0:T(1,128)S(1)}, u32[]{:S(2)}, u32[]{:S(2)}) collective-permute-start(f32[1,18,1,128]{3,2,1,0:T(1,128)S(1)} %get-tuple-element.27), channel_id=1, source_target_pairs={{0,1},{1,2},{2,3},{3,4},{4,5},{5,6},{6,7},{7,8},{8,9},{9,10},{10,1... | collective-permute-start | bytes 27656 | tf_op jit(solution)/shard_map/ppermute | solution.py:227
  127.6 5.0 %collective-permute-start.28 = (f32[3,3,8,128]{3,2,1,0:T(8,128)S(1)}, f32[3,3,8,128]{3,2,1,0:T(8,128)S(1)}, u32[]{:S(2)}, u32[]{:S(2)}) collective-permute-start(f32[3,3,8,128]{3,2,1,0:T(8,128)S(1)} %get-tuple-element.19), channel_id=1, source_target_pairs={{0,16},{16,32},{32,48},{48,64},{64,80},{80,96},{96,112},{112,0},{1... | collective-permute-start | bytes 110600 | tf_op jit(solution)/shard_map/ppermute | solution.py:227
  130.6 3.4 %collective-permute-start.29 = (f32[3,3,8,128]{3,2,1,0:T(8,128)S(1)}, f32[3,3,8,128]{3,2,1,0:T(8,128)S(1)}, u32[]{:S(2)}, u32[]{:S(2)}) collective-permute-start(f32[3,3,8,128]{3,2,1,0:T(8,128)S(1)} %get-tuple-element.20), channel_id=1, source_target_pairs={{16,0},{32,16},{48,32},{64,48},{80,64},{96,80},{112,96},{0,112},{1... | collective-permute-start | bytes 110600 | tf_op jit(solution)/shard_map/ppermute | solution.py:230
  134.1 7.4 %collective-permute-start.30 = (f32[3,22,3,128]{3,2,1,0:T(4,128)S(1)}, f32[3,22,3,128]{3,2,1,0:T(4,128)S(1)}, u32[]{:S(2)}, u32[]{:S(2)}) collective-permute-start(f32[3,22,3,128]{3,2,1,0:T(4,128)S(1)} %get-tuple-element.13), channel_id=1, source_target_pairs={{0,1},{1,2},{2,3},{3,4},{4,5},{5,6},{6,7},{7,8},{8,9},{9,10},{10,1... | collective-permute-start | bytes 304136 | tf_op jit(solution)/shard_map/ppermute | solution.py:227
  134.4 7.2 %collective-permute-start.31 = (f32[3,22,3,128]{3,2,1,0:T(4,128)S(1)}, f32[3,22,3,128]{3,2,1,0:T(4,128)S(1)}, u32[]{:S(2)}, u32[]{:S(2)}) collective-permute-start(f32[3,22,3,128]{3,2,1,0:T(4,128)S(1)} %get-tuple-element.14), channel_id=1, source_target_pairs={{1,0},{2,1},{3,2},{4,3},{5,4},{6,5},{7,6},{8,7},{9,8},{10,9},{11,1... | collective-permute-start | bytes 304136 | tf_op jit(solution)/shard_map/ppermute | solution.py:230
  (10 other events, 46.0 us)

commit v2 on v1

--- a/solution.py
+++ b/solution.py
@@ -5,7 +5,6 @@
 from jax.experimental.pallas import tpu as pltpu
 from jax.sharding import PartitionSpec as P
 
-JAC = 4
 time_step = 0.5
 viscosity = 0.1
 
@@ -218,80 +217,165 @@
 SM = pl.BlockSpec(memory_space=pltpu.SMEM)
 
 
-def with_halo(block, sides, width):
-    for axis, dim in sides:
-        count = lax.axis_size(axis)
-        forward = [(i, i + 1) for i in range(count - 1)]
-        forward.append((count - 1, 0))
-        backward = [(target, source) for source, target in forward]
-        low = lax.ppermute(
-            lax.slice_in_dim(block, block.shape[dim] - width, None, axis=dim), axis, forward
-        )
-        high = lax.ppermute(lax.slice_in_dim(block, 0, width, axis=dim), axis, backward)
-        block = jnp.concatenate([low, block, high], axis=dim)
-    return block
-
-
-def neighbour_sum(padded):
-    return (
-        padded[..., 2:, 1:-1, 1:-1]
-        + padded[..., :-2, 1:-1, 1:-1]
-        + padded[..., 1:-1, 2:, 1:-1]
-        + padded[..., 1:-1, :-2, 1:-1]
-        + padded[..., 1:-1, 1:-1, 2:]
-        + padded[..., 1:-1, 1:-1, :-2]
-    )
-
-
-def divergence(padded):
-    return (
-        0.5
-        * (
-            padded[0, 2:, 1:-1, 1:-1]
-            - padded[0, :-2, 1:-1, 1:-1]
-            + (padded[1, 1:-1, 2:, 1:-1] - padded[1, 1:-1, :-2, 1:-1])
-            + (padded[2, 1:-1, 1:-1, 2:] - padded[2, 1:-1, 1:-1, :-2])
-        )
-    )[None]
-
-
-def gradient(padded):
-    return 0.5 * jnp.stack(
-        [
-            padded[0, 2:, 1:-1, 1:-1] - padded[0, :-2, 1:-1, 1:-1],
-            padded[0, 1:-1, 2:, 1:-1] - padded[0, 1:-1, :-2, 1:-1],
-            padded[0, 1:-1, 1:-1, 2:] - padded[0, 1:-1, 1:-1, :-2],
-        ]
-    )
-
-
-def pad_depth(grid_field):
-    return jnp.pad(grid_field, ((0, 0), (0, 0), (0, 0), (1, 1)))
-
-
-def extend(grid_field):
-    widened = with_halo(grid_field, (("gx", 1), ("gy", 2)), 1)
-    return pad_depth(widened)
-
-
-def grow_rims(grid_field):
-    return with_halo(grid_field, (("gx", 1), ("gy", 2)), 3)
-
-
-def fold_rims(widened, axis_dim, length):
-    middle = lax.slice_in_dim(widened, 6, 6 + length, axis=axis_dim)
-    lower_rim = lax.slice_in_dim(widened, 0, 3, axis=axis_dim)
-    upper_rim = lax.slice_in_dim(widened, length + 9, length + 12, axis=axis_dim)
-    low_pad = [(0, 0)] * widened.ndim
-    low_pad[axis_dim] = (0, length - 3)
-    high_pad = [(0, 0)] * widened.ndim
-    high_pad[axis_dim] = (length - 3, 0)
-    return middle + jnp.pad(lower_rim, low_pad) + jnp.pad(upper_rim, high_pad)
+MESH = pl.DeviceIdType.MESH
+SIDES = ((1, 0), (-1, 0), (0, 1), (0, -1), (1, 1), (1, -1), (-1, 1), (-1, -1))
+
+
+def neighbours():
+    gx, gy = lax.axis_index("gx"), lax.axis_index("gy")
+    nx, ny = lax.axis_size("gx"), lax.axis_size("gy")
+    return [(lax.rem(gx + dx + nx, nx), lax.rem(gy + dy + ny, ny)) for dx, dy in SIDES]
+
+
+def near(step, size, width):
+    return (0, size) if step == 0 else ((size - width, width) if step > 0 else (0, width))
+
+
+def there(step, size, width):
+    return (0, size) if step == 0 else ((-width, width) if step > 0 else (size, width))
+
+
+def inward(lane, v):
+    above = jnp.where(lane == 127, 0.0, pltpu.roll(v, 127, 1))
+    below = jnp.where(lane == 0, 0.0, pltpu.roll(v, 1, 1))
+    return above, below
+
+
+def fluid_body(w_ref, vel_ref, new_ref, prs_ref, v_ref, ve, pe, src, pa, pb, fold, send, recv):
+    peers = neighbours()
+    barrier = pltpu.get_barrier_semaphore()
+    fold[...] = jnp.zeros(fold.shape, F32)
+    for peer in peers:
+        pl.semaphore_signal(barrier, inc=1, device_id=peer, device_id_type=MESH)
+    ve[:, 1:17, 8:16, :] = vel_ref[...]
+    pl.semaphore_wait(barrier, 8)
+    started = []
+
+    def push(source, target, k):
+        n = len(started)
+        copy = pltpu.make_async_remote_copy(source, target, send.at[n], recv.at[n], device_id=peers[k], device_id_type=MESH)
+        copy.start()
+        started.append(copy)
+        return copy
+
+    def box(ref, xs, ys, x_at, y_at):
+        return ref.at[..., pl.ds(xs[0] + x_at, xs[1]), pl.ds(ys[0] + y_at, ys[1]), :]
+
+    first = []
+    for k, (dx, dy) in enumerate(SIDES):
+        xs = (3, 16) if dx == 0 else ((19, 3) if dx > 0 else (0, 3))
+        ys = (3, 8) if dy == 0 else ((11, 3) if dy > 0 else (0, 3))
+        xd = (0, 16) if dx == 0 else ((0, 3) if dx > 0 else (13, 3))
+        yd = (0, 8) if dy == 0 else ((0, 3) if dy > 0 else (5, 3))
+        layer = 0 if dy == 0 else (1 if dx == 0 else 2)
+        first.append(push(w_ref.at[:, pl.ds(xs[0], xs[1]), pl.ds(ys[0], ys[1]), :],
+                          fold.at[layer, :, pl.ds(xd[0], xd[1]), pl.ds(yd[0], yd[1]), :], k))
+        if k < 4:
+            first.append(push(box(vel_ref, near(dx, 16, 1), near(dy, 8, 1), 0, 0),
+                              box(ve, there(dx, 16, 1), there(dy, 8, 1), 1, 8), k))
+    for copy in first:
+        copy.wait_recv()
+    lane = lax.broadcasted_iota(jnp.int32, (8, 128), 1)
+
+    def provide(x, carry):
+        for c in range(3):
+            v = ve[c, x + 1, 8:16, :]
+            above, below = inward(lane, v)
+            lap = (ve[c, x + 2, 8:16, :] + ve[c, x, 8:16, :]) + (ve[c, x + 1, 9:17, :] + ve[c, x + 1, 7:15, :]) + (above + below) - 6.0 * v
+            force = w_ref[c, x + 3, 3:11, :] + fold[0, c, x] + fold[1, c, x] + fold[2, c, x]
+            pe[c, x + 8, 8:16, :] = v + time_step * (viscosity * lap + force)
+        return carry
+
+    lax.fori_loop(0, 16, provide, 0, unroll=4)
+
+    second = [push(box(pe, near(dx, 16, 1), near(dy, 8, 1), 8, 8),
+                   box(pe, there(dx, 16, 1), there(dy, 8, 1), 8, 8), k) for k, (dx, dy) in enumerate(SIDES[:4])]
+    for copy in second:
+        copy.wait_recv()
+
+    def diverge(x, carry):
+        above, below = inward(lane, pe[2, x + 8, 8:16, :])
+        total = (pe[0, x + 9, 8:16, :] - pe[0, x + 7, 8:16, :]) + (pe[1, x + 8, 9:17, :] - pe[1, x + 8, 7:15, :]) + (above - below)
+        src[x + 8, 8:16, :] = total * (0.5 / time_step)
+        return carry
+
+    lax.fori_loop(0, 16, diverge, 0, unroll=4)
+
+    third = [push(box(src, near(dx, 16, 7), near(dy, 8, 7), 8, 8),
+                  box(src, there(dx, 16, 7), there(dy, 8, 7), 8, 8), k) for k, (dx, dy) in enumerate(SIDES)]
+    fourth = []
+    for k, (dx, dy) in enumerate(SIDES):
+        if k < 4:
+            xs = (0, 16) if dx == 0 else ((13, 2) if dx > 0 else (1, 2))
+            ys = (0, 8) if dy == 0 else ((5, 2) if dy > 0 else (1, 2))
+            xd = (0, 16) if dx == 0 else ((-3, 2) if dx > 0 else (17, 2))
+            yd = (0, 8) if dy == 0 else ((-3, 2) if dy > 0 else (9, 2))
+        else:
+            xs, ys, xd, yd = near(dx, 16, 3), near(dy, 8, 3), there(dx, 16, 3), there(dy, 8, 3)
+        fourth.append(push(box(pe, xs, ys, 8, 8), box(pe, xd, yd, 8, 8), k))
+    for copy in third:
+        copy.wait_recv()
+
+    def relax(old, new, reach, starts, first_sweep):
+        scale = -1.0 / 6.0 if first_sweep else 1.0
+
+        def step(x, carry):
+            for s in starts:
+                here = pl.ds(s, 8)
+                v = old[x, here, :] * scale
+                above, below = inward(lane, v)
+                total = (old[x + 1, here, :] + old[x - 1, here, :]) + (old[x, s + 1:s + 9, :] + old[x, s - 1:s + 7, :])
+                new[x, here, :] = (total * scale + (above + below) - src[x, here, :]) * (1.0 / 6.0)
+            return carry
+
+        lax.fori_loop(8 - reach, 24 + reach, step, 0, unroll=2)
+
+    relax(src, pa, 6, (2, 8, 14), True)
+    relax(pa, pb, 5, (3, 8, 13), False)
+    relax(pb, pa, 4, (4, 12), False)
+    for copy in fourth:
+        copy.wait_recv()
+    v_ref[:, :, 8:16, :] = jnp.zeros((3, 24, 8, 128), F32)
+    v_ref[:, 22:24, 0:8, :] = jnp.zeros((3, 2, 8, 128), F32)
+
+    def finish(x, carry):
+        for s in (5, 11):
+            here = pl.ds(s, 8)
+            above, below = inward(lane, pa[x, here, :])
+            grad = (pa[x + 1, here, :] - pa[x - 1, here, :], pa[x, s + 1:s + 9, :] - pa[x, s - 1:s + 7, :], above - below)
+            for c in range(3):
+                v_ref[c, x - 5, pl.ds(s - 5, 8), :] = pe[c, x, here, :] - (0.5 * time_step) * grad[c]
+        return carry
+
+    lax.fori_loop(5, 27, finish, 0, unroll=2)
+    new_ref[...] = v_ref[:, 3:19, 3:11, :]
+    prs_ref[...] = pa[8:24, 8:16, :]
+    for copy in started:
+        copy.wait_send()
+
+
+def fluid_call(widened, velocity):
+    return pl.pallas_call(
+        fluid_body,
+        out_shape=(jax.ShapeDtypeStruct((3, 16, 8, 128), F32), jax.ShapeDtypeStruct((16, 8, 128), F32), jax.ShapeDtypeStruct((3, 24, 16, 128), F32)),
+        in_specs=[VM, VM],
+        out_specs=(VM, VM, VM),
+        scratch_shapes=[
+            pltpu.VMEM((3, 18, 24, 128), F32),
+            pltpu.VMEM((3, 32, 24, 128), F32),
+            pltpu.VMEM((32, 24, 128), F32),
+            pltpu.VMEM((32, 24, 128), F32),
+            pltpu.VMEM((32, 24, 128), F32),
+            pltpu.VMEM((3, 3, 16, 8, 128), F32),
+            pltpu.SemaphoreType.DMA((32,)),
+            pltpu.SemaphoreType.DMA((32,)),
+        ],
+        compiler_params=pltpu.CompilerParams(vmem_limit_bytes=32 * 2**20, collective_id=0, has_side_effects=True),
+        name="fluid",
+    )(widened, velocity)
 
 
 def shards(velocity, offsets, forces, owner, base, counts):
-    width_x = velocity.shape[1]
-    width_y = velocity.shape[2]
     axes = ("gx", "gy")
     stage, back = pl.pallas_call(
         pack_body,
@@ -304,16 +388,7 @@
     arrived = lax.all_to_all(stage.reshape(128, 16, 128), axes, split_axis=0, concat_axis=0, tiled=True)
     corners = arrived[:, 6, :6].astype(jnp.int32).reshape(-1)
     spread_grid = spread_call(corners, arrived, 4)
-    widened = grow_rims(spread_grid[:, : width_x + 6, : width_y + 6])
-    force_field = fold_rims(fold_rims(widened, 1, width_x), 2, width_y)
-    laplace = neighbour_sum(extend(velocity)) - 6.0 * velocity
-    provisional = velocity + time_step * (viscosity * laplace + force_field)
-    source = divergence(extend(provisional)) / time_step
-    pressure = -source / 6.0
-    for sweep in range(JAC - 1):
-        pressure = (neighbour_sum(extend(pressure)) - source) / 6.0
-    new_velocity = provisional - time_step * gradient(extend(pressure))
-    sampled = jnp.pad(grow_rims(new_velocity), ((0, 0), (0, 2), (0, 2), (0, 0)))
+    new_velocity, pressure, sampled = fluid_call(spread_grid, velocity)
     answers = interp_call(corners, arrived, sampled, 4)
     returned = lax.all_to_all(answers, axes, split_axis=0, concat_axis=0, tiled=True)
     marker_velocity = pl.pallas_call(
@@ -324,7 +399,7 @@
         compiler_params=pltpu.CompilerParams(vmem_limit_bytes=32 * 2**20),
         name="unpack",
     )(back, returned.reshape(1024, 128))
-    return (new_velocity, pressure[0], marker_velocity)
+    return (new_velocity, pressure, marker_velocity)
 
 
 def solution(mesh):

time: 179 us -> 108 us (0.60)
  starting transfers between devices: 60.3 us -> 4.57 us
  waiting for transfers between devices: 58.1 us -> 14.1 us
  Pallas kernels: 26.8 us -> 52.4 us
  blocking collectives: 24.7 us -> 30.6 us
  other arithmetic: 3.55 us -> 0.23 us
    ppermute x32 -> x0, starting transfers between devices: 48.8 us -> none  [the longest x16 35.8 us: with_halo(): lax.ppermute(lax.slice_in_dim(block, 0, width, axis=dim), axis, backward)]
    ppermute x32 -> x0, waiting for transfers between devices: 47.5 us -> none  [the longest x16 27.3 us: with_halo(): lax.ppermute(lax.slice_in_dim(block, block.shape[dim] - width, None, axis...]
    pallas_call x0 -> x1, Pallas kernels: none -> 25.9 us  [fluid_call(): pl.pallas_call(fluid_body, out_shape=(jax.ShapeDtypeStruct((3, 16, 8, 128...]
    all_to_all x1, starting transfers between devices: 11.5 us -> 4.57 us  [shards(): lax.all_to_all(answers, axes, split_axis=0, concat_axis=0, tiled=True)]
    all_to_all x1, blocking collectives: 24.7 us -> 30.6 us  [shards(): lax.all_to_all(stage.reshape(128, 16, 128), axes, split_axis=0, concat_ax...]
    all_to_all x1, waiting for transfers between devices: 10.6 us -> 14.1 us  [shards(): lax.all_to_all(answers, axes, split_axis=0, concat_axis=0, tiled=True)]
    concatenate x14 -> x0, other arithmetic: 2.36 us -> none  [with_halo(): block = jnp.concatenate([low, block, high], axis=dim)]
    unnamed x20 -> x12, local copies, waits for them, and re-layouts: 3.16 us -> 3.81 us
  transfers between devices with their start and end apart: 33 -> 1, of which waited for: 27 -> 1; matrix products, arithmetic and copies ran while one was open for 0% -> 0% of each run, Pallas kernels for 0% -> 0%
where the time goes in v2:
time: 108 us; the launch traced here: 107 us
  Pallas kernels  52.4 us (49%)
  blocking collectives  30.6 us (28%)
  waiting for transfers between devices  14.1 us (13%)
  starting transfers between devices  4.57 us (4%)
  local copies, waits for them, and re-layouts  3.94 us (4%)
  between operations  1.37 us (1%)
    all_to_all x1, blocking collectives, shards(): lax.all_to_all(stage.reshape(128, 16, 128), axes, split_axis=0, concat_ax...  30.6 us
    pallas_call x1, Pallas kernels, fluid_call(): pl.pallas_call(fluid_body, out_shape=(jax.ShapeDtypeStruct((3, 16, 8, 128...  25.9 us
    all_to_all x1, waiting for transfers between devices, shards(): lax.all_to_all(answers, axes, split_axis=0, concat_axis=0, tiled=True)  14.1 us
    pallas_call x1, Pallas kernels, spread_call(): pl.pallas_call(functools.partial(spread_body, unroll), out_shape=jax.Shap...  12.8 us
    pallas_call x1, Pallas kernels, interp_call(): pl.pallas_call(functools.partial(interp_body, unroll), out_shape=jax.Shap...  11.9 us
    all_to_all x1, starting transfers between devices, shards(): lax.all_to_all(answers, axes, split_axis=0, concat_axis=0, tiled=True)  4.57 us
    unnamed x12, local copies, waits for them, and re-layouts  3.81 us
  transfers between devices with their start and end apart: 1, of which 1 were waited for; matrix products, arithmetic and copies ran while one was open for 0% of the time, Pallas kernels for 0%

profile of v2, /device:TPU:1, one launch (start us, length us, event | category | flops | bytes accessed | tf_op | source)
XLA Modules:
  0.0 107.2 jit_solution(14766804891889258639)
XLA Ops:
  0.6 0.0 copy-start.3
  1.3 0.0 copy-start.4
  1.3 0.0 copy-done.3
  1.3 0.6 copy-done.4
  2.0 0.0 copy-start
  2.0 0.9 copy-done
  2.9 0.0 copy-start.1
  2.9 0.9 copy-done.1
  3.8 0.9 pack.1
  4.7 30.6 %all_to_all.10.r_ref = f32[128,16,128]{2,1,0:T(8,128)S(1)} all-to-all(f32[128,16,128]{2,1,0:T(8,128)S(1)} %bitcast.4), channel_id=1, replica_groups=mesh['gx'=8,'gy'=16] {'gx','gy'}, dimensions={0} | all-to-all | bytes 2097152 | tf_op jit(solution)/shard_map/all_to_all | solution.py:388
  35.3 0.2 fusion
  35.5 0.1 convert_element_type.8.base_s
  35.6 0.0 copy-start.2
  35.7 12.8 %spread.1.w_ref = f32[3,24,16,128]{3,2,1,0:T(8,128)S(1)} custom-call(s32[768]{0:T(1024)S(1)} %convert_element_type.8.base_s, f32[128,16,128]{2,1,0:T(8,128)S(1)} %all_to_all.10.r_ref), custom_call_target="tpu_custom_call" | custom-call | tf_op jit(solution)/shard_map/spread/pallas_call | solution.py:99
  48.5 0.0 copy-done.2
  48.5 25.9 %fluid.1 = (f32[3,16,8,128]{3,2,1,0:T(8,128)S(1)}, f32[16,8,128]{2,1,0:T(8,128)S(1)}, f32[3,24,16,128]{3,2,1,0:T(8,128)S(1)}) custom-call(f32[3,24,16,128]{3,2,1,0:T(8,128)S(1)} %spread.1.w_ref, f32[3,16,8,128]{3,2,1,0:T(8,128)S(1)} %copy-done.2), custom_call_target="tpu_custom_call" | custom-call | tf_op jit(solution)/shard_map/fluid/pallas_call | solution.py:358
  74.4 11.9 %interp.1 = f32[128,8,128]{2,1,0:T(8,128)} custom-call(s32[768]{0:T(1024)S(1)} %convert_element_type.8.base_s, f32[128,16,128]{2,1,0:T(8,128)S(1)} %all_to_all.10.r_ref, f32[3,24,16,128]{3,2,1,0:T(8,128)S(1)} %get-tuple-element.12.v_ref), custom_call_target="tpu_custom_call" | custom-call | tf_op jit(solution)/shard_map/interp/pallas_call | solution.py:147
  86.3 4.6 %all-to-all-start.1 = ((f32[128,8,128]{2,1,0:T(8,128)}), f32[128,8,128]{2,1,0:T(8,128)S(1)}, u32[]{:S(2)}, u32[]{:S(2)}) async-start(f32[128,8,128]{2,1,0:T(8,128)} %interp.1), calls=%async_computation.1 | async-start | bytes 1048576 | tf_op jit(solution)/shard_map/all_to_all | solution.py:393
  90.9 14.1 %all-to-all-done.1 = f32[128,8,128]{2,1,0:T(8,128)S(1)} async-done(((f32[128,8,128]{2,1,0:T(8,128)}), f32[128,8,128]{2,1,0:T(8,128)S(1)}, u32[]{:S(2)}, u32[]{:S(2)}) %all-to-all-start.1) | async-done | bytes 524320 | tf_op jit(solution)/shard_map/all_to_all | solution.py:393
  105.0 1.0 unpack.1
  105.9 0.7 copy.12
  106.6 0.6 copy.13
Async XLA Ops:
  0.6 0.7 copy-start.3
  1.3 0.7 copy-start.4
  2.0 0.9 copy-start
  2.9 0.9 copy-start.1
  35.6 12.8 %copy-start.2 = (f32[3,16,8,128]{3,2,1,0:T(8,128)S(1)}, f32[3,16,8,128]{3,2,1,0:T(8,128)}, u32[]{:S(2)}) copy-start(f32[3,16,8,128]{3,2,1,0:T(8,128)} %vel_ref.1) | copy-start | bytes 589828
  86.3 18.7 %all-to-all-start.1 = ((f32[128,8,128]{2,1,0:T(8,128)}), f32[128,8,128]{2,1,0:T(8,128)S(1)}, u32[]{:S(2)}, u32[]{:S(2)}) async-start(f32[128,8,128]{2,1,0:T(8,128)} %interp.1), calls=%async_computation.1 | async-start | bytes 1048576 | tf_op jit(solution)/shard_map/all_to_all | solution.py:393

commit v3 on v2

--- a/solution.py
+++ b/solution.py
@@ -16,18 +16,6 @@
     lo = (v - hi.astype(F32)).astype(BF)
     return hi, lo
 
-def fill_tables(r_ref, fl, a1, a2, q8, sources):
-    def body(b, carry):
-        t = r_ref[pl.ds(b * 8, 8), 0:8, :].reshape(64, 128)
-        whole = jnp.floor(t)
-        f = t - whole
-        rows = pl.ds(pl.multiple_of(b * 64, 64), 64)
-        fl[rows, :] = whole
-        a1[rows, :] = (3.0 - 2.0 * f) * 0.125
-        a2[rows, :] = (1.0 + 2.0 * f) * 0.125
-        q8[rows, :] = jnp.sqrt(1.0 + 4.0 * f * (1.0 - f)) * 0.125
-        return carry
-    lax.fori_loop(0, sources // 8, body, 0)
 
 def weight(cells, row, tabs):
     fl, a1, a2, q8 = [t[pl.ds(row, 1), :] for t in tabs]
@@ -36,123 +24,11 @@
     g = e * (e - 1.0)
     return jnp.where(g < 1.0, s + q8, jnp.where(g < 3.0, s - q8, 0.0))
 
-def plane(base_s, p, row, tabs, wxs, iota8, iota16):
-    wx = weight(iota8, row, tabs)
-    y0 = base_s[p * 3 + 1].astype(F32)
+
+def plane_of(y0, row, tabs, wxs, iota8, iota16):
+    wxs[...] = weight(iota8, row, tabs)
     wy = weight(iota16 - y0, row + 1, tabs)
-    wxs[...] = wx
     return jnp.concatenate([wxs[pl.ds(i, 1), :] * wy for i in range(8)], axis=0)
-
-def spread_body(unroll, base_s, r_ref, out, fl, a1, a2, q8, acc, wxs, tot):
-    sources = r_ref.shape[0]
-    tabs = (fl, a1, a2, q8)
-    def zero(x, carry):
-        acc[x] = jnp.zeros((3, 128, 128), F32)
-        return carry
-    lax.fori_loop(0, 16, zero, 0)
-    fill_tables(r_ref, *tabs, sources)
-    iota8 = lax.broadcasted_iota(jnp.int32, (8, 128), 0).astype(F32) - 3.0
-    iota16 = lax.broadcasted_iota(jnp.int32, (16, 128), 0).astype(F32) - 3.0
-    def body(t, carry):
-        res = []
-        for u in range(unroll):
-            s = t * unroll + u
-            for r in range(2):
-                p = s * 2 + r
-                row = s * 8 + r * 3
-                B = plane(base_s, p, row, tabs, wxs.at[u * 2 + r], iota8, iota16)
-                wz = weight(iota8, row + 2, tabs)
-                A = jnp.concatenate([r_ref[s, pl.ds(8 + r * 3 + c, 1), :] * wz for c in range(3)], axis=0)
-                ah, al = split(A)
-                bh, bl = split(B)
-                o = lax.dot_general(jnp.concatenate([ah, al], 0), jnp.concatenate([bh, bl], 0), (((1,), (1,)), ((), ())), preferred_element_type=F32)
-                res.append((p, o[:24, :128] + o[24:, :128] + o[:24, 128:]))
-        for p, o in res:
-            x0 = base_s[p * 3]
-            z0 = jnp.maximum(base_s[p * 3 + 2] - 3, 0)
-            for c in range(3):
-                acc[x0, c, pl.ds(z0, 8), :] += o[c * 8:c * 8 + 8]
-        return carry
-    lax.fori_loop(0, sources // unroll, body, 0)
-    lane = lax.broadcasted_iota(jnp.int32, (128, 128), 1)
-    for c in range(3):
-        tiles = [None] * 3
-        for t in range(2):
-            for r in range(8):
-                a = acc[8 * t + r, c]
-                if r == 0:
-                    parts = [(t, a)]
-                else:
-                    a = pltpu.roll(a, 16 * r, 1)
-                    parts = [(t, jnp.where(lane >= 16 * r, a, 0.0)), (t + 1, jnp.where(lane < 16 * r, a, 0.0))]
-                for k, v in parts:
-                    if tiles[k] is None:
-                        tot[k] = v
-                        tiles[k] = 1
-                    else:
-                        tot[k] += v
-        for k in range(3):
-            out[c, 8 * k:8 * k + 8] = tot[k].T.reshape(8, 16, 128)
-
-def spread_call(base, R, unroll=2, vmem=48*2**20):
-    n = R.shape[0]
-    return pl.pallas_call(
-        functools.partial(spread_body, unroll),
-        out_shape=jax.ShapeDtypeStruct((3, 24, 16, 128), F32),
-        in_specs=[pl.BlockSpec(memory_space=pltpu.SMEM), pl.BlockSpec(memory_space=pltpu.VMEM)],
-        out_specs=pl.BlockSpec(memory_space=pltpu.VMEM),
-        scratch_shapes=[pltpu.VMEM((n * 8, 128), F32)] * 4 + [pltpu.VMEM((16, 3, 128, 128), F32), pltpu.VMEM((2 * unroll, 8, 128), F32), pltpu.VMEM((3, 128, 128), F32)],
-        compiler_params=pltpu.CompilerParams(vmem_limit_bytes=vmem),
-        name="spread",
-    )(base, R)
-
-def interp_body(unroll, base_s, r_ref, v_ref, out, fl, a1, a2, q8, cop, wxs):
-    sources = r_ref.shape[0]
-    tabs = (fl, a1, a2, q8)
-    fill_tables(r_ref, *tabs, sources)
-    lane = lax.broadcasted_iota(jnp.int32, (128, 128), 1)
-    for c in range(3):
-        tiles = [v_ref[c, 8 * k:8 * k + 8].reshape(128, 128).T for k in range(3)]
-        for r in range(8):
-            if r == 0:
-                cop[0, c], cop[8, c] = tiles[0], tiles[1]
-            else:
-                ro = [pltpu.roll(x, 128 - 16 * r, 1) for x in tiles]
-                for t in range(2):
-                    cop[8 * t + r, c] = jnp.where(lane < 128 - 16 * r, ro[t], ro[t + 1])
-    iota8 = lax.broadcasted_iota(jnp.int32, (8, 128), 0).astype(F32) - 3.0
-    iota16 = lax.broadcasted_iota(jnp.int32, (16, 128), 0).astype(F32) - 3.0
-    def body(t, carry):
-        for u in range(unroll):
-            s = t * unroll + u
-            for r in range(2):
-                p = s * 2 + r
-                row = s * 8 + r * 3
-                B = plane(base_s, p, row, tabs, wxs.at[u * 2 + r], iota8, iota16)
-                wz = weight(iota8, row + 2, tabs)
-                x0 = base_s[p * 3]
-                z0 = jnp.maximum(base_s[p * 3 + 2] - 3, 0)
-                A = jnp.concatenate([cop[x0, c, pl.ds(z0, 8), :] for c in range(3)], axis=0)
-                ah, al = split(A)
-                bh, bl = split(B)
-                o = jnp.dot(jnp.concatenate([ah, al], 0), jnp.concatenate([bh, bl], 1), preferred_element_type=F32)
-                o = o[:24, :128] + o[24:, :128] + o[:24, 128:]
-                for c in range(3):
-                    out[s, pl.ds(r * 3 + c, 1), :] = jnp.sum(o[8 * c:8 * c + 8] * wz, axis=0, keepdims=True)
-        return carry
-    lax.fori_loop(0, sources // unroll, body, 0)
-
-def interp_call(base, R, V, unroll=2, vmem=48*2**20):
-    n = R.shape[0]
-    return pl.pallas_call(
-        functools.partial(interp_body, unroll),
-        out_shape=jax.ShapeDtypeStruct((n, 8, 128), F32),
-        in_specs=[pl.BlockSpec(memory_space=pltpu.SMEM), pl.BlockSpec(memory_space=pltpu.VMEM), pl.BlockSpec(memory_space=pltpu.VMEM)],
-        out_specs=pl.BlockSpec(memory_space=pltpu.VMEM),
-        scratch_shapes=[pltpu.VMEM((n * 8, 128), F32)] * 4 + [pltpu.VMEM((16, 3, 128, 128), F32), pltpu.VMEM((2 * unroll, 8, 128), F32)],
-        compiler_params=pltpu.CompilerParams(vmem_limit_bytes=vmem),
-        name="interp",
-    )(base, R, V)
 
 
 def split3(v):
@@ -198,21 +74,6 @@
         spread_rows(stage, row, jnp.zeros((128, 128), F32))
 
 
-def pack_body(count_s, owner_ref, off_ref, frc_ref, base_ref, stage, back):
-    first, second = routes(owner_ref[...], count_s[0])
-    back[:, :128] = first.T
-    back[:, 128:] = second.T
-    pack_rows(first, second, off_ref, frc_ref, base_ref, stage)
-
-
-def unpack_body(back, ret_ref, out):
-    pick = back[...].astype(BF)
-    for c in range(3):
-        data = jnp.concatenate([ret_ref[pl.ds(r * 3 + c, 128, stride=8), :] for r in range(2)], axis=0)
-        got = jnp.dot(pick, jnp.concatenate(split3(data), axis=1), preferred_element_type=F32)
-        out[c] = got[:, :128] + (got[:, 128:256] + got[:, 256:])
-
-
 VM = pl.BlockSpec(memory_space=pltpu.VMEM)
 SM = pl.BlockSpec(memory_space=pltpu.SMEM)
 
@@ -375,30 +236,281 @@
     )(widened, velocity)
 
 
+def position():
+    gx, gy = lax.axis_index("gx"), lax.axis_index("gy")
+    return gx >> 1, gx & 1, gy >> 2, gy & 3
+
+
+def shifted(k, here, sign):
+    y, core, z, x = here
+    kc, kx, ky, kz = k & 1, (k >> 1) & 3, (k >> 3) & 3, k >> 5
+    if sign < 0:
+        kx, ky, kz = 4 - kx, 4 - ky, 4 - kz
+    return (((y + ky) & 3) * 2 + ((core + kc) & 1), ((z + kz) & 3) * 4 + ((x + kx) & 3))
+
+
+def steps_to(owner, here):
+    y, core, z, x = here
+    row, column = owner >> 4, owner & 15
+    kc, ky = ((row & 1) - core) & 1, ((row >> 1) - y) & 3
+    kz, kx = ((column >> 2) - z) & 3, ((column & 3) - x) & 3
+    return kc + 2 * kx + 8 * ky + 32 * kz
+
+
+def greet_all(line_sem, between):
+    gx, gy = lax.axis_index("gx"), lax.axis_index("gy")
+    barrier = pltpu.get_barrier_semaphore()
+    for i in range(1, 16):
+        pl.semaphore_signal(barrier, inc=1, device_id=(gx, (gy + i) & 15), device_id_type=MESH)
+    for i in range(1, 8):
+        pl.semaphore_signal(barrier, inc=1, device_id=((gx + i) & 7, gy), device_id_type=MESH)
+    between()
+    pl.semaphore_wait(barrier, 22)
+    for i in range(1, 8):
+        pl.semaphore_signal(line_sem, inc=1, device_id=((gx + i) & 7, gy), device_id_type=MESH)
+    pl.semaphore_wait(line_sem, 7)
+
+
+def exchange_body(unroll, count_s, owner_ref, off_ref, frc_ref, base_ref, arrived, boxes, corners, back, stage, fl, a1, a2, q8, wxs, line_sem, send, recv):
+    here = position()
+
+    def prepare():
+        first, second = routes(steps_to(owner_ref[...], here), count_s[0])
+        back[:, :128] = first.T
+        back[:, 128:] = second.T
+        pack_rows(first, second, off_ref, frc_ref, base_ref, stage)
+
+    greet_all(line_sem, prepare)
+
+    def message(k):
+        rows = pl.ds(pl.multiple_of(k * 16, 16), 14)
+        return pltpu.make_async_remote_copy(stage.at[rows], arrived.at[rows], send.at[k], recv.at[k], device_id=shifted(k, here, 1), device_id_type=MESH)
+
+    def begin(k, carry):
+        message(k).start()
+        return carry
+
+    lax.fori_loop(1, 128, begin, 0)
+    arrived[0:16] = stage[0:16]
+    iota8 = lax.broadcasted_iota(jnp.int32, (8, 128), 0).astype(F32) - 3.0
+    iota16 = lax.broadcasted_iota(jnp.int32, (16, 128), 0).astype(F32) - 3.0
+    tabs = (fl, a1, a2, q8)
+
+    def work(ks):
+        for u, k in enumerate(ks):
+            at = k * 16 if isinstance(k, int) else pl.multiple_of(k * 16, 16)
+            t = arrived[pl.ds(at, 8), :]
+            whole = jnp.floor(t)
+            f = t - whole
+            fl[u * 8:u * 8 + 8, :] = whole
+            a1[u * 8:u * 8 + 8, :] = (3.0 - 2.0 * f) * 0.125
+            a2[u * 8:u * 8 + 8, :] = (1.0 + 2.0 * f) * 0.125
+            q8[u * 8:u * 8 + 8, :] = jnp.sqrt(1.0 + 4.0 * f * (1.0 - f)) * 0.125
+        for u, k in enumerate(ks):
+            for r in range(2):
+                row = u * 8 + r * 3
+                y0 = arrived[pl.ds(k * 16 + 6, 1), r * 3 + 1:r * 3 + 2]
+                B = plane_of(y0, row, tabs, wxs.at[u * 2 + r], iota8, iota16)
+                wz = weight(iota8, row + 2, tabs)
+                A = jnp.concatenate([arrived[pl.ds(k * 16 + 8 + r * 3 + c, 1), :] * wz for c in range(3)], axis=0)
+                ah, al = split(A)
+                bh, bl = split(B)
+                o = lax.dot_general(jnp.concatenate([ah, al], 0), jnp.concatenate([bh, bl], 0), (((1,), (1,)), ((), ())), preferred_element_type=F32)
+                boxes[k * 2 + r] = o[:24, :128] + o[24:, :128] + o[:24, 128:]
+
+    for k in range(1, unroll):
+        message(k).wait_recv()
+    work(list(range(unroll)))
+
+    def turn(t, carry):
+        ks = [t * unroll + u for u in range(unroll)]
+        for k in ks:
+            message(k).wait_recv()
+        work(ks)
+        return carry
+
+    lax.fori_loop(1, 128 // unroll, turn, 0)
+    gathered = jnp.concatenate([arrived[pl.ds(d * 16 + 6, 8, stride=16), :] for d in range(0, 128, 8)], axis=0)
+    corners[...] = gathered.T[0:8].astype(jnp.int32)
+
+    def end(k, carry):
+        message(k).wait_send()
+        return carry
+
+    lax.fori_loop(1, 128, end, 0)
+
+
+def exchange_call(counts, owner, offsets, forces, base, unroll=4):
+    shapes = ((2048, 128), F32), ((256, 24, 128), F32), ((8, 128), jnp.int32), ((128, 256), F32)
+    return pl.pallas_call(
+        functools.partial(exchange_body, unroll),
+        out_shape=tuple(jax.ShapeDtypeStruct(*s) for s in shapes),
+        in_specs=[SM, VM, VM, VM, VM],
+        out_specs=(VM,) * 4,
+        scratch_shapes=[pltpu.VMEM((2048, 128), F32)] + [pltpu.VMEM((8 * unroll, 128), F32)] * 4 + [
+            pltpu.VMEM((2 * unroll, 8, 128), F32),
+            pltpu.SemaphoreType.REGULAR,
+            pltpu.SemaphoreType.DMA((128,)),
+            pltpu.SemaphoreType.DMA((128,)),
+        ],
+        compiler_params=pltpu.CompilerParams(vmem_limit_bytes=40 * 2**20, collective_id=1, has_side_effects=True),
+        name="exchange",
+    )(counts, owner.reshape(1, 128), offsets, forces, base)
+
+
+def deposit_body(corners_s, boxes, out, acc, tot):
+    def zero(x, carry):
+        acc[x] = jnp.zeros((3, 128, 128), F32)
+        return carry
+
+    lax.fori_loop(0, 16, zero, 0)
+
+    def add(k, carry):
+        for r in range(2):
+            x0 = corners_s[r * 3, k]
+            z0 = jnp.maximum(corners_s[r * 3 + 2, k] - 3, 0)
+            for c in range(3):
+                acc[x0, c, pl.ds(z0, 8), :] += boxes[k * 2 + r, c * 8:c * 8 + 8]
+        return carry
+
+    lax.fori_loop(0, 128, add, 0, unroll=4)
+    lane = lax.broadcasted_iota(jnp.int32, (128, 128), 1)
+    for c in range(3):
+        filled = [False] * 3
+        for t in range(2):
+            for r in range(8):
+                a = acc[8 * t + r, c]
+                if r == 0:
+                    parts = [(t, a)]
+                else:
+                    a = pltpu.roll(a, 16 * r, 1)
+                    parts = [(t, jnp.where(lane >= 16 * r, a, 0.0)), (t + 1, jnp.where(lane < 16 * r, a, 0.0))]
+                for k, v in parts:
+                    tot[k] = tot[k] + v if filled[k] else v
+                    filled[k] = True
+        for k in range(3):
+            out[c, 8 * k:8 * k + 8] = tot[k].T.reshape(8, 16, 128)
+
+
+def deposit_call(corners, boxes):
+    return pl.pallas_call(
+        deposit_body,
+        out_shape=jax.ShapeDtypeStruct((3, 24, 16, 128), F32),
+        in_specs=[SM, VM],
+        out_specs=VM,
+        scratch_shapes=[pltpu.VMEM((16, 3, 128, 128), F32), pltpu.VMEM((3, 128, 128), F32)],
+        compiler_params=pltpu.CompilerParams(vmem_limit_bytes=40 * 2**20),
+        name="deposit",
+    )(corners, boxes)
+
+
+def answer_body(unroll, corners_s, arrived, v_ref, back, out, ans, ret, fl, a1, a2, q8, cop, wxs, line_sem, send, recv):
+    here = position()
+    lane = lax.broadcasted_iota(jnp.int32, (128, 128), 1)
+    tabs = (fl, a1, a2, q8)
+
+    def prepare():
+        for c in range(3):
+            tiles = [v_ref[c, 8 * k:8 * k + 8].reshape(128, 128).T for k in range(3)]
+            for r in range(8):
+                if r == 0:
+                    cop[0, c], cop[8, c] = tiles[0], tiles[1]
+                else:
+                    ro = [pltpu.roll(x, 128 - 16 * r, 1) for x in tiles]
+                    for t in range(2):
+                        cop[8 * t + r, c] = jnp.where(lane < 128 - 16 * r, ro[t], ro[t + 1])
+
+        def body(b, carry):
+            t = arrived[pl.ds(b * 8, 8), 0:8, :].reshape(64, 128)
+            whole = jnp.floor(t)
+            f = t - whole
+            rows = pl.ds(pl.multiple_of(b * 64, 64), 64)
+            fl[rows, :] = whole
+            a1[rows, :] = (3.0 - 2.0 * f) * 0.125
+            a2[rows, :] = (1.0 + 2.0 * f) * 0.125
+            q8[rows, :] = jnp.sqrt(1.0 + 4.0 * f * (1.0 - f)) * 0.125
+            return carry
+
+        lax.fori_loop(0, 16, body, 0)
+
+    greet_all(line_sem, prepare)
+    iota8 = lax.broadcasted_iota(jnp.int32, (8, 128), 0).astype(F32) - 3.0
+    iota16 = lax.broadcasted_iota(jnp.int32, (16, 128), 0).astype(F32) - 3.0
+
+    def message(k):
+        rows = pl.ds(pl.multiple_of(k * 8, 8), 6)
+        return pltpu.make_async_remote_copy(ans.at[rows], ret.at[rows], send.at[k], recv.at[k], device_id=shifted(k, here, -1), device_id_type=MESH)
+
+    def work(ks):
+        for u, k in enumerate(ks):
+            for r in range(2):
+                row = k * 8 + r * 3
+                B = plane_of(corners_s[r * 3 + 1, k].astype(F32), row, tabs, wxs.at[u * 2 + r], iota8, iota16)
+                wz = weight(iota8, row + 2, tabs)
+                x0 = corners_s[r * 3, k]
+                z0 = jnp.maximum(corners_s[r * 3 + 2, k] - 3, 0)
+                A = jnp.concatenate([cop[x0, c, pl.ds(z0, 8), :] for c in range(3)], axis=0)
+                ah, al = split(A)
+                bh, bl = split(B)
+                o = jnp.dot(jnp.concatenate([ah, al], 0), jnp.concatenate([bh, bl], 1), preferred_element_type=F32)
+                o = o[:24, :128] + o[24:, :128] + o[:24, 128:]
+                for c in range(3):
+                    ans[pl.ds(k * 8 + r * 3 + c, 1), :] = jnp.sum(o[8 * c:8 * c + 8] * wz, axis=0, keepdims=True)
+
+    work(list(range(unroll)))
+    for k in range(1, unroll):
+        message(k).start()
+
+    def turn(t, carry):
+        ks = [t * unroll + u for u in range(unroll)]
+        work(ks)
+        for k in ks:
+            message(k).start()
+        return carry
+
+    lax.fori_loop(1, 128 // unroll, turn, 0)
+    ret[0:8] = ans[0:8]
+    pick = back[...].astype(BF)
+
+    def settle(k, carry):
+        message(k).wait_recv()
+        return carry
+
+    lax.fori_loop(1, 128, settle, 0)
+    for c in range(3):
+        data = jnp.concatenate([ret[pl.ds(r * 3 + c, 128, stride=8), :] for r in range(2)], axis=0)
+        got = jnp.dot(pick, jnp.concatenate(split3(data), axis=1), preferred_element_type=F32)
+        out[c] = got[:, :128] + (got[:, 128:256] + got[:, 256:])
+
+    def end(k, carry):
+        message(k).wait_send()
+        return carry
+
+    lax.fori_loop(1, 128, end, 0)
+
+
+def answer_call(corners, arrived, sampled, back, unroll=4):
+    return pl.pallas_call(
+        functools.partial(answer_body, unroll),
+        out_shape=jax.ShapeDtypeStruct((3, 128, 128), F32),
+        in_specs=[SM, VM, VM, VM],
+        out_specs=VM,
+        scratch_shapes=[pltpu.VMEM((1024, 128), F32)] * 2 + [pltpu.VMEM((1024, 128), F32)] * 4 + [
+            pltpu.VMEM((16, 3, 128, 128), F32),
+            pltpu.VMEM((2 * unroll, 8, 128), F32),
+            pltpu.SemaphoreType.REGULAR,
+            pltpu.SemaphoreType.DMA((128,)),
+            pltpu.SemaphoreType.DMA((128,)),
+        ],
+        compiler_params=pltpu.CompilerParams(vmem_limit_bytes=40 * 2**20, collective_id=2, has_side_effects=True),
+        name="answer",
+    )(corners, arrived, sampled, back)
+
+
 def shards(velocity, offsets, forces, owner, base, counts):
-    axes = ("gx", "gy")
-    stage, back = pl.pallas_call(
-        pack_body,
-        out_shape=(jax.ShapeDtypeStruct((2048, 128), F32), jax.ShapeDtypeStruct((128, 256), F32)),
-        in_specs=[SM, VM, VM, VM, VM],
-        out_specs=(VM, VM),
-        compiler_params=pltpu.CompilerParams(vmem_limit_bytes=32 * 2**20),
-        name="pack",
-    )(counts, owner.reshape(1, 128), offsets, forces, base)
-    arrived = lax.all_to_all(stage.reshape(128, 16, 128), axes, split_axis=0, concat_axis=0, tiled=True)
-    corners = arrived[:, 6, :6].astype(jnp.int32).reshape(-1)
-    spread_grid = spread_call(corners, arrived, 4)
-    new_velocity, pressure, sampled = fluid_call(spread_grid, velocity)
-    answers = interp_call(corners, arrived, sampled, 4)
-    returned = lax.all_to_all(answers, axes, split_axis=0, concat_axis=0, tiled=True)
-    marker_velocity = pl.pallas_call(
-        unpack_body,
-        out_shape=jax.ShapeDtypeStruct((3, 128, 128), F32),
-        in_specs=[VM, VM],
-        out_specs=VM,
-        compiler_params=pltpu.CompilerParams(vmem_limit_bytes=32 * 2**20),
-        name="unpack",
-    )(back, returned.reshape(1024, 128))
+    arrived, boxes, corners, back = exchange_call(counts, owner, offsets, forces, base)
+    new_velocity, pressure, sampled = fluid_call(deposit_call(corners, boxes), velocity)
+    marker_velocity = answer_call(corners, arrived.reshape(128, 16, 128), sampled, back)
     return (new_velocity, pressure, marker_velocity)
 
 

time: 108 us -> 92.8 us (0.86)
  Pallas kernels: 52.4 us -> 86.1 us
  blocking collectives: 30.6 us -> 0 us
  waiting for transfers between devices: 14.1 us -> 0 us
  starting transfers between devices: 4.57 us -> 0 us
  local copies, waits for them, and re-layouts: 3.94 us -> 5.17 us
    pallas_call x4 -> x3, Pallas kernels: 26.5 us -> 61.3 us  [the longest x1 33.3 us: exchange_call(): pl.pallas_call(functools.partial(exchange_body, unroll), out_shape=tuple(...]
    all_to_all x1 -> x0, blocking collectives: 30.6 us -> none  [shards(): lax.all_to_all(stage.reshape(128, 16, 128), axes, split_axis=0, concat_ax...]
    all_to_all x1 -> x0, waiting for transfers between devices: 14.1 us -> none  [shards(): lax.all_to_all(answers, axes, split_axis=0, concat_axis=0, tiled=True)]
    all_to_all x1 -> x0, starting transfers between devices: 4.57 us -> none  [shards(): lax.all_to_all(answers, axes, split_axis=0, concat_axis=0, tiled=True)]
    unnamed x12 -> x13, local copies, waits for them, and re-layouts: 3.81 us -> 5.17 us
    pallas_call x1, Pallas kernels: 25.9 us -> 24.8 us  [fluid_call(): pl.pallas_call(fluid_body, out_shape=(jax.ShapeDtypeStruct((3, 16, 8, 128...]
  transfers between devices with their start and end apart: 1 -> 0, of which waited for: 1 -> 0; matrix products, arithmetic and copies ran while one was open for 0% -> 0% of each run, Pallas kernels for 0% -> 0%
where the time goes in v3:
time: 92.8 us; the launch traced here: 92.6 us
  Pallas kernels  86.1 us (93%)
  local copies, waits for them, and re-layouts  5.17 us (6%)
  between operations  1.33 us (1%)
    pallas_call x1, Pallas kernels, exchange_call(): pl.pallas_call(functools.partial(exchange_body, unroll), out_shape=tuple(...  33.3 us
    pallas_call x1, Pallas kernels, fluid_call(): pl.pallas_call(fluid_body, out_shape=(jax.ShapeDtypeStruct((3, 16, 8, 128...  24.8 us
    pallas_call x1, Pallas kernels, answer_call(): pl.pallas_call(functools.partial(answer_body, unroll), out_shape=jax.Shap...  24.6 us
    unnamed x13, local copies, waits for them, and re-layouts  5.17 us
    pallas_call x1, Pallas kernels, deposit_call(): pl.pallas_call(deposit_body, out_shape=jax.ShapeDtypeStruct((3, 24, 16, 1...  3.38 us

profile of v3, /device:TPU:1, one launch (start us, length us, event | category | flops | bytes accessed | tf_op | source)
XLA Modules:
  0.0 92.6 jit_solution(2707791616238576923)
XLA Ops:
  1.3 0.0 copy-start
  1.3 0.9 copy-done
  2.2 0.0 copy-start.1
  2.2 0.9 copy-done.1
  3.1 0.0 copy-start.3
  3.1 0.7 copy-done.3
  3.8 0.0 copy-start.4
  3.8 0.7 copy-done.4
  4.5 0.0 copy-start.2
  4.5 33.3 %exchange.1 = (f32[2048,128]{1,0:T(8,128)S(1)}, f32[256,24,128]{2,1,0:T(8,128)S(1)}, s32[8,128]{1,0:T(8,128)S(1)}, f32[128,256]{1,0:T(8,128)S(1)}) custom-call(s32[1]{0:T(128)S(6)} %copy.12.count_s, s32[1,128]{1,0:T(1,128)S(1)} %bitcast.3, f32[3,128,128]{2,1,0:T(8,128)S(1)} %copy-done, f32[3,128,128]{2,1,0:T(8,128)S(1)} %copy-done.1, s32[3,128]{1,0:T(4,128)S(1)} %copy-done.3), custom_call_target="tpu_custom_call" | custom-call | tf_op jit(solution)/shard_map/exchange/pallas_call | solution.py:345
  37.8 3.4 %deposit.1.w_ref = f32[3,24,16,128]{3,2,1,0:T(8,128)S(1)} custom-call(s32[8,128]{1,0:T(8,128)S(1)} %get-tuple-element.10.corners_s, f32[256,24,128]{2,1,0:T(8,128)S(1)} %get-tuple-element.11.boxes), custom_call_target="tpu_custom_call" | custom-call | tf_op jit(solution)/shard_map/deposit/pallas_call | solution.py:396
  41.2 0.0 copy-done.2
  41.2 24.8 %fluid.1 = (f32[3,16,8,128]{3,2,1,0:T(8,128)S(1)}, f32[16,8,128]{2,1,0:T(8,128)S(1)}, f32[3,24,16,128]{3,2,1,0:T(8,128)S(1)}) custom-call(f32[3,24,16,128]{3,2,1,0:T(8,128)S(1)} %deposit.1.w_ref, f32[3,16,8,128]{3,2,1,0:T(8,128)S(1)} %copy-done.2), custom_call_target="tpu_custom_call" | custom-call | tf_op jit(solution)/shard_map/fluid/pallas_call | solution.py:219
  66.0 24.6 %answer.1 = f32[3,128,128]{2,1,0:T(8,128)S(1)} custom-call(s32[8,128]{1,0:T(8,128)S(1)} %get-tuple-element.10.corners_s, f32[128,16,128]{2,1,0:T(8,128)S(1)} %bitcast.2, f32[3,24,16,128]{3,2,1,0:T(8,128)S(1)} %get-tuple-element.15.v_ref, f32[128,256]{1,0:T(8,128)S(1)} %get-tuple-element.16.back), custom_call_target="tpu_custom_call" | custom-call | tf_op jit(solution)/shard_map/answer/pallas_call | solution.py:493
  90.6 0.7 copy.13
  91.2 0.6 copy.14
  91.9 0.7 copy.15
Async XLA Ops:
  1.3 0.9 %copy-start = (f32[3,128,128]{2,1,0:T(8,128)S(1)}, f32[3,128,128]{2,1,0:T(8,128)}, u32[]{:S(2)}) copy-start(f32[3,128,128]{2,1,0:T(8,128)} %off_ref.1) | copy-start | bytes 589828
  2.2 0.9 %copy-start.1 = (f32[3,128,128]{2,1,0:T(8,128)S(1)}, f32[3,128,128]{2,1,0:T(8,128)}, u32[]{:S(2)}) copy-start(f32[3,128,128]{2,1,0:T(8,128)} %frc_ref.1) | copy-start | bytes 589828
  3.1 0.7 copy-start.3
  3.8 0.7 copy-start.4
  4.5 36.7 %copy-start.2 = (f32[3,16,8,128]{3,2,1,0:T(8,128)S(1)}, f32[3,16,8,128]{3,2,1,0:T(8,128)}, u32[]{:S(2)}) copy-start(f32[3,16,8,128]{3,2,1,0:T(8,128)} %vel_ref.1) | copy-start | bytes 589828

commit v4 on v3

v4 whole, which is shorter than its diff:
```python
import functools
import jax, jax.numpy as jnp
from jax import lax
from jax.experimental import pallas as pl
from jax.experimental.pallas import tpu as pltpu
from jax.sharding import PartitionSpec as P

time_step = 0.5
viscosity = 0.1

F32 = jnp.float32
BF = jnp.bfloat16

def split(v):
    hi = v.astype(BF)
    lo = (v - hi.astype(F32)).astype(BF)
    return hi, lo


def weight(cells, row, tabs):
    fl, a1, a2, q8 = [t[pl.ds(row, 1), :] for t in tabs]
    e = cells - fl
    s = jnp.where(e < 0.5, a1, a2)
    g = e * (e - 1.0)
    return jnp.where(g < 1.0, s + q8, jnp.where(g < 3.0, s - q8, 0.0))


def plane_of(y0, row, tabs, wxs, iota8, iota16):
    wxs[...] = weight(iota8, row, tabs)
    wy = weight(iota16 - y0, row + 1, tabs)
    return jnp.concatenate([wxs[pl.ds(i, 1), :] * wy for i in range(8)], axis=0)


def split3(v):
    hi = v.astype(BF)
    rest = v - hi.astype(F32)
    mid = rest.astype(BF)
    return hi, mid, (rest - mid.astype(F32)).astype(BF)


def routes(owner_row, count):
    rows = lax.broadcasted_iota(jnp.int32, (128, 128), 0)
    slots = lax.broadcasted_iota(jnp.int32, (128, 128), 1)
    match = jnp.where((owner_row == rows) & (slots < count), 1.0, 0.0)
    before = jnp.where(rows < slots, 1.0, 0.0)
    rank = jnp.dot(match.astype(BF), before.astype(BF), preferred_element_type=F32)
    return jnp.where(rank < 0.5, match, 0.0), jnp.where(rank < 0.5, 0.0, match)


def spread_rows(stage, row, values):
    for d in range(0, 128, 8):
        stage[pl.ds(d * 16 + row, 8, stride=16), :] = values[d:d + 8]


def pack_rows(first, second, off_ref, frc_ref, base_ref, stage):
    both = jnp.concatenate([first, second], axis=0).astype(BF)
    for q in range(6):
        data = off_ref[q] if q < 3 else frc_ref[q - 3]
        parts = jnp.concatenate(split3(data), axis=1)
        got = jnp.dot(both, parts, preferred_element_type=F32)
        got = got[:, :128] + (got[:, 128:256] + got[:, 256:])
        for r in range(2):
            spread_rows(stage, (q // 3) * 8 + r * 3 + q % 3, got[r * 128:r * 128 + 128])
    rows = base_ref[...].astype(F32)
    none = jnp.zeros((122, 128), F32)
    blank = jnp.zeros((3, 128), F32)
    dims = (((1,), (1,)), ((), ()))
    one = jnp.concatenate([rows, blank, none], axis=0).astype(BF)
    two = jnp.concatenate([blank, rows, none], axis=0).astype(BF)
    corner = lax.dot_general(both[:128], one, dims, preferred_element_type=F32)
    corner += lax.dot_general(both[128:], two, dims, preferred_element_type=F32)
    spread_rows(stage, 6, corner)
    for row in (7, 14, 15):
        spread_rows(stage, row, jnp.zeros((128, 128), F32))


VM = pl.BlockSpec(memory_space=pltpu.VMEM)
SM = pl.BlockSpec(memory_space=pltpu.SMEM)
ANY = pl.BlockSpec(memory_space=pltpu.HBM)


def position():
    gx, gy = lax.axis_index("gx"), lax.axis_index("gy")
    return gx >> 1, gx & 1, gy >> 2, gy & 3


def shifted(k, here, sign):
    y, core, z, x = here
    kc, kx, ky, kz = k & 1, (k >> 1) & 3, (k >> 3) & 3, k >> 5
    if sign < 0:
        kx, ky, kz = 4 - kx, 4 - ky, 4 - kz
    return (((y + ky) & 3) * 2 + ((core + kc) & 1), ((z + kz) & 3) * 4 + ((x + kx) & 3))


def steps_to(owner, here):
    y, core, z, x = here
    row, column = owner >> 4, owner & 15
    kc, ky = ((row & 1) - core) & 1, ((row >> 1) - y) & 3
    kz, kx = ((column >> 2) - z) & 3, ((column & 3) - x) & 3
    return kc + 2 * kx + 8 * ky + 32 * kz


def greet_all(line_sem, between):
    gx, gy = lax.axis_index("gx"), lax.axis_index("gy")
    barrier = pltpu.get_barrier_semaphore()
    for i in range(1, 16):
        pl.semaphore_signal(barrier, inc=1, device_id=(gx, (gy + i) & 15), device_id_type=MESH)
    for i in range(1, 8):
        pl.semaphore_signal(barrier, inc=1, device_id=((gx + i) & 7, gy), device_id_type=MESH)
    between()
    pl.semaphore_wait(barrier, 22)
    for i in range(1, 8):
        pl.semaphore_signal(line_sem, inc=1, device_id=((gx + i) & 7, gy), device_id_type=MESH)
    pl.semaphore_wait(line_sem, 7)


def exchange_body(unroll, count_s, owner_ref, off_hbm, frc_hbm, base_ref, arrived, boxes, corners, back, off_ref, frc_ref, load, stage, fl, a1, a2, q8, wxs, line_sem, send, recv):
    here = position()
    loads = [pltpu.make_async_copy(off_hbm, off_ref, load.at[0]), pltpu.make_async_copy(frc_hbm, frc_ref, load.at[1])]
    for copy in loads:
        copy.start()

    def prepare():
        first, second = routes(steps_to(owner_ref[...], here), count_s[0])
        back[:, :128] = first.T
        back[:, 128:] = second.T
        for copy in loads:
            copy.wait()
        pack_rows(first, second, off_ref, frc_ref, base_ref, stage)

    greet_all(line_sem, prepare)

    def message(k):
        rows = pl.ds(pl.multiple_of(k * 16, 16), 14)
        return pltpu.make_async_remote_copy(stage.at[rows], arrived.at[rows], send.at[k], recv.at[k], device_id=shifted(k, here, 1), device_id_type=MESH)

    def begin(k, carry):
        message(k).start()
        return carry

    lax.fori_loop(1, 128, begin, 0)
    arrived[0:16] = stage[0:16]
    iota8 = lax.broadcasted_iota(jnp.int32, (8, 128), 0).astype(F32) - 3.0
    iota16 = lax.broadcasted_iota(jnp.int32, (16, 128), 0).astype(F32) - 3.0
    tabs = (fl, a1, a2, q8)

    def work(ks):
        for u, k in enumerate(ks):
            at = k * 16 if isinstance(k, int) else pl.multiple_of(k * 16, 16)
            t = arrived[pl.ds(at, 8), :]
            whole = jnp.floor(t)
            f = t - whole
            fl[u * 8:u * 8 + 8, :] = whole
            a1[u * 8:u * 8 + 8, :] = (3.0 - 2.0 * f) * 0.125
            a2[u * 8:u * 8 + 8, :] = (1.0 + 2.0 * f) * 0.125
            q8[u * 8:u * 8 + 8, :] = jnp.sqrt(1.0 + 4.0 * f * (1.0 - f)) * 0.125
        for u, k in enumerate(ks):
            for r in range(2):
                row = u * 8 + r * 3
                y0 = arrived[pl.ds(k * 16 + 6, 1), r * 3 + 1:r * 3 + 2]
                B = plane_of(y0, row, tabs, wxs.at[u * 2 + r], iota8, iota16)
                wz = weight(iota8, row + 2, tabs)
                A = jnp.concatenate([arrived[pl.ds(k * 16 + 8 + r * 3 + c, 1), :] * wz for c in range(3)], axis=0)
                ah, al = split(A)
                bh, bl = split(B)
                o = lax.dot_general(jnp.concatenate([ah, al], 0), jnp.concatenate([bh, bl], 0), (((1,), (1,)), ((), ())), preferred_element_type=F32)
                boxes[k * 2 + r] = o[:24, :128] + o[24:, :128] + o[:24, 128:]

    for k in range(1, unroll):
        message(k).wait_recv()
    work(list(range(unroll)))

    def turn(t, carry):
        ks = [t * unroll + u for u in range(unroll)]
        for k in ks:
            message(k).wait_recv()
        work(ks)
        return carry

    lax.fori_loop(1, 128 // unroll, turn, 0)
    gathered = jnp.concatenate([arrived[pl.ds(d * 16 + 6, 8, stride=16), :] for d in range(0, 128, 8)], axis=0)
    corners[...] = gathered.T[0:8].astype(jnp.int32)

    def end(k, carry):
        message(k).wait_send()
        return carry

    lax.fori_loop(1, 128, end, 0)


def exchange_call(counts, owner, offsets, forces, base, unroll=8):
    shapes = ((2048, 128), F32), ((256, 24, 128), F32), ((8, 128), jnp.int32), ((128, 256), F32)
    return pl.pallas_call(
        functools.partial(exchange_body, unroll),
        out_shape=tuple(jax.ShapeDtypeStruct(*s) for s in shapes),
        in_specs=[SM, VM, ANY, ANY, VM],
        out_specs=(VM,) * 4,
        scratch_shapes=[pltpu.VMEM((3, 128, 128), F32), pltpu.VMEM((3, 128, 128), F32), pltpu.SemaphoreType.DMA((2,))] + [pltpu.VMEM((2048, 128), F32)] + [pltpu.VMEM((8 * unroll, 128), F32)] * 4 + [
            pltpu.VMEM((2 * unroll, 8, 128), F32),
            pltpu.SemaphoreType.REGULAR,
            pltpu.SemaphoreType.DMA((128,)),
            pltpu.SemaphoreType.DMA((128,)),
        ],
        compiler_params=pltpu.CompilerParams(vmem_limit_bytes=40 * 2**20, collective_id=1, has_side_effects=True),
        name="exchange",
    )(counts, owner.reshape(1, 128), offsets, forces, base)


def deposit_body(corners_s, boxes, out, acc, tot):
    def zero(x, carry):
        acc[x] = jnp.zeros((3, 128, 128), F32)
        return carry

    lax.fori_loop(0, 16, zero, 0)

    def add(k, carry):
        for r in range(2):
            x0 = corners_s[r * 3, k]
            z0 = jnp.maximum(corners_s[r * 3 + 2, k] - 3, 0)
            for c in range(3):
                acc[x0, c, pl.ds(z0, 8), :] += boxes[k * 2 + r, c * 8:c * 8 + 8]
        return carry

    lax.fori_loop(0, 128, add, 0, unroll=4)
    lane = lax.broadcasted_iota(jnp.int32, (128, 128), 1)
    for c in range(3):
        filled = [False] * 3
        for t in range(2):
            for r in range(8):
                a = acc[8 * t + r, c]
                if r == 0:
                    parts = [(t, a)]
                else:
                    a = pltpu.roll(a, 16 * r, 1)
                    parts = [(t, jnp.where(lane >= 16 * r, a, 0.0)), (t + 1, jnp.where(lane < 16 * r, a, 0.0))]
                for k, v in parts:
                    tot[k] = tot[k] + v if filled[k] else v
                    filled[k] = True
        for k in range(3):
            out[c, 8 * k:8 * k + 8] = tot[k].T.reshape(8, 16, 128)


def deposit_call(corners, boxes):
    return pl.pallas_call(
        deposit_body,
        out_shape=jax.ShapeDtypeStruct((3, 24, 16, 128), F32),
        in_specs=[SM, VM],
        out_specs=VM,
        scratch_shapes=[pltpu.VMEM((16, 3, 128, 128), F32), pltpu.VMEM((3, 128, 128), F32)],
        compiler_params=pltpu.CompilerParams(vmem_limit_bytes=40 * 2**20),
        name="deposit",
    )(corners, boxes)


MESH = pl.DeviceIdType.MESH
SIDES = ((1, 0), (-1, 0), (0, 1), (0, -1), (1, 1), (1, -1), (-1, 1), (-1, -1))


def neighbours():
    gx, gy = lax.axis_index("gx"), lax.axis_index("gy")
    nx, ny = lax.axis_size("gx"), lax.axis_size("gy")
    return [(lax.rem(gx + dx + nx, nx), lax.rem(gy + dy + ny, ny)) for dx, dy in SIDES]


def near(step, size, width):
    return (0, size) if step == 0 else ((size - width, width) if step > 0 else (0, width))


def there(step, size, width):
    return (0, size) if step == 0 else ((-width, width) if step > 0 else (size, width))


def inward(lane, v):
    above = jnp.where(lane == 127, 0.0, pltpu.roll(v, 127, 1))
    below = jnp.where(lane == 0, 0.0, pltpu.roll(v, 1, 1))
    return above, below


def project_body(unroll, chunks, corners_s, arrived, w_ref, vel_hbm, new_ref, prs_ref, ret, vel_ref, load, v_ref, ve, pe, src, pa, pb, fold, tables, wxs, planes, depths, cop, ans, line_sem, send, recv, out_sem, in_sem):
    here = position()
    peers = neighbours()
    gx, gy = lax.axis_index("gx"), lax.axis_index("gy")
    barrier = pltpu.get_barrier_semaphore()
    velocity_in = pltpu.make_async_copy(vel_hbm, vel_ref, load)
    velocity_in.start()
    fold[...] = jnp.zeros(fold.shape, F32)
    for i in range(1, 16):
        pl.semaphore_signal(barrier, inc=1, device_id=(gx, (gy + i) & 15), device_id_type=MESH)
    for i in range(1, 8):
        pl.semaphore_signal(barrier, inc=1, device_id=((gx + i) & 7, gy), device_id_type=MESH)
    velocity_in.wait()
    ve[:, 1:17, 8:16, :] = vel_ref[...]
    iota8 = lax.broadcasted_iota(jnp.int32, (8, 128), 0).astype(F32) - 3.0
    iota16 = lax.broadcasted_iota(jnp.int32, (16, 128), 0).astype(F32) - 3.0

    def weigh(begin, end):
        def turn(t, carry):
            for u in range(unroll):
                k = t * unroll + u
                rows = pl.ds(u * 8, 8)
                whole = jnp.floor(arrived[k, 0:8, :])
                f = arrived[k, 0:8, :] - whole
                for n, v in enumerate((whole, (3.0 - 2.0 * f) * 0.125, (1.0 + 2.0 * f) * 0.125, jnp.sqrt(1.0 + 4.0 * f * (1.0 - f)) * 0.125)):
                    tables[n, rows, :] = v
                for r in range(2):
                    row, p = u * 8 + r * 3, k * 2 + r
                    tabs = [tables.at[n] for n in range(4)]
                    bh, bl = split(plane_of(corners_s[r * 3 + 1, k].astype(F32), row, tabs, wxs.at[u * 2 + r], iota8, iota16))
                    planes[p, :, :128] = bh
                    planes[p, :, 128:] = bl
                    depths[p] = weight(iota8, row + 2, tabs)
            return carry

        lax.fori_loop(begin // unroll, end // unroll, turn, 0)

    weigh(chunks[0], chunks[1])
    pl.semaphore_wait(barrier, 22)
    for i in range(1, 8):
        pl.semaphore_signal(line_sem, inc=1, device_id=((gx + i) & 7, gy), device_id_type=MESH)
    started = []

    def push(source, target, k):
        n = len(started)
        copy = pltpu.make_async_remote_copy(source, target, send.at[n], recv.at[n], device_id=peers[k], device_id_type=MESH)
        copy.start()
        started.append(copy)
        return copy

    def box(ref, xs, ys, x_at, y_at):
        return ref.at[..., pl.ds(xs[0] + x_at, xs[1]), pl.ds(ys[0] + y_at, ys[1]), :]

    first = []
    for k, (dx, dy) in enumerate(SIDES):
        if k == 4:
            pl.semaphore_wait(line_sem, 7)
        xs = (3, 16) if dx == 0 else ((19, 3) if dx > 0 else (0, 3))
        ys = (3, 8) if dy == 0 else ((11, 3) if dy > 0 else (0, 3))
        xd = (0, 16) if dx == 0 else ((0, 3) if dx > 0 else (13, 3))
        yd = (0, 8) if dy == 0 else ((0, 3) if dy > 0 else (5, 3))
        layer = 0 if dy == 0 else (1 if dx == 0 else 2)
        first.append(push(w_ref.at[:, pl.ds(xs[0], xs[1]), pl.ds(ys[0], ys[1]), :],
                          fold.at[layer, :, pl.ds(xd[0], xd[1]), pl.ds(yd[0], yd[1]), :], k))
        if k < 4:
            first.append(push(box(vel_ref, near(dx, 16, 1), near(dy, 8, 1), 0, 0),
                              box(ve, there(dx, 16, 1), there(dy, 8, 1), 1, 8), k))
    weigh(chunks[1], chunks[2])
    for copy in first:
        copy.wait_recv()
    lane = lax.broadcasted_iota(jnp.int32, (8, 128), 1)

    def provide(x, carry):
        for c in range(3):
            v = ve[c, x + 1, 8:16, :]
            above, below = inward(lane, v)
            lap = (ve[c, x + 2, 8:16, :] + ve[c, x, 8:16, :]) + (ve[c, x + 1, 9:17, :] + ve[c, x + 1, 7:15, :]) + (above + below) - 6.0 * v
            force = w_ref[c, x + 3, 3:11, :] + fold[0, c, x] + fold[1, c, x] + fold[2, c, x]
            pe[c, x + 8, 8:16, :] = v + time_step * (viscosity * lap + force)
        return carry

    lax.fori_loop(0, 16, provide, 0, unroll=8)

    second = [push(box(pe, near(dx, 16, 1), near(dy, 8, 1), 8, 8),
                   box(pe, there(dx, 16, 1), there(dy, 8, 1), 8, 8), k) for k, (dx, dy) in enumerate(SIDES[:4])]
    weigh(chunks[2], chunks[3])
    for copy in second:
        copy.wait_recv()

    def diverge(x, carry):
        above, below = inward(lane, pe[2, x + 8, 8:16, :])
        total = (pe[0, x + 9, 8:16, :] - pe[0, x + 7, 8:16, :]) + (pe[1, x + 8, 9:17, :] - pe[1, x + 8, 7:15, :]) + (above - below)
        src[x + 8, 8:16, :] = total * (0.5 / time_step)
        return carry

    lax.fori_loop(0, 16, diverge, 0, unroll=16)

    third = [push(box(src, near(dx, 16, 7), near(dy, 8, 7), 8, 8),
                  box(src, there(dx, 16, 7), there(dy, 8, 7), 8, 8), k) for k, (dx, dy) in enumerate(SIDES)]
    fourth = []
    for k, (dx, dy) in enumerate(SIDES):
        if k < 4:
            xs = (0, 16) if dx == 0 else ((13, 2) if dx > 0 else (1, 2))
            ys = (0, 8) if dy == 0 else ((5, 2) if dy > 0 else (1, 2))
            xd = (0, 16) if dx == 0 else ((-3, 2) if dx > 0 else (17, 2))
            yd = (0, 8) if dy == 0 else ((-3, 2) if dy > 0 else (9, 2))
        else:
            xs, ys, xd, yd = near(dx, 16, 3), near(dy, 8, 3), there(dx, 16, 3), there(dy, 8, 3)
        fourth.append(push(box(pe, xs, ys, 8, 8), box(pe, xd, yd, 8, 8), k))
    weigh(chunks[3], chunks[4])
    for copy in third:
        copy.wait_recv()

    def relax(old, new, reach, starts, first_sweep):
        scale = -1.0 / 6.0 if first_sweep else 1.0

        def step(x, carry):
            for s in starts:
                here = pl.ds(s, 8)
                v = old[x, here, :] * scale
                above, below = inward(lane, v)
                total = (old[x + 1, here, :] + old[x - 1, here, :]) + (old[x, s + 1:s + 9, :] + old[x, s - 1:s + 7, :])
                new[x, here, :] = (total * scale + (above + below) - src[x, here, :]) * (1.0 / 6.0)
            return carry

        lax.fori_loop(8 - reach, 24 + reach, step, 0, unroll=(16 + 2 * reach) // 2)

    relax(src, pa, 6, (2, 8, 14), True)
    relax(pa, pb, 5, (3, 8, 13), False)
    relax(pb, pa, 4, (4, 12), False)
    for copy in fourth:
        copy.wait_recv()
    v_ref[:, :, 8:16, :] = jnp.zeros((3, 24, 8, 128), F32)
    v_ref[:, 22:24, 0:8, :] = jnp.zeros((3, 2, 8, 128), F32)

    def finish(x, carry):
        for s in (5, 11):
            here = pl.ds(s, 8)
            above, below = inward(lane, pa[x, here, :])
            grad = (pa[x + 1, here, :] - pa[x - 1, here, :], pa[x, s + 1:s + 9, :] - pa[x, s - 1:s + 7, :], above - below)
            for c in range(3):
                v_ref[c, x - 5, pl.ds(s - 5, 8), :] = pe[c, x, here, :] - (0.5 * time_step) * grad[c]
        return carry

    lax.fori_loop(5, 27, finish, 0, unroll=11)
    new_ref[...] = v_ref[:, 3:19, 3:11, :]
    prs_ref[...] = pa[8:24, 8:16, :]
    for copy in started:
        copy.wait_send()


    for c in range(3):
        tiles = [v_ref[c, 8 * k:8 * k + 8].reshape(128, 128).T for k in range(3)]
        wide = lax.broadcasted_iota(jnp.int32, (128, 128), 1)
        for r in range(8):
            if r == 0:
                cop[0, c], cop[8, c] = tiles[0], tiles[1]
            else:
                ro = [pltpu.roll(x, 128 - 16 * r, 1) for x in tiles]
                for t in range(2):
                    cop[8 * t + r, c] = jnp.where(wide < 128 - 16 * r, ro[t], ro[t + 1])

    def message(k):
        rows = pl.ds(pl.multiple_of(k * 8, 8), 6)
        return pltpu.make_async_remote_copy(ans.at[rows], ret.at[rows], out_sem.at[k], in_sem.at[k], device_id=shifted(k, here, -1), device_id_type=MESH)

    def work(ks):
        for k in ks:
            for r in range(2):
                p = k * 2 + r
                x0 = corners_s[r * 3, k]
                z0 = jnp.maximum(corners_s[r * 3 + 2, k] - 3, 0)
                ah, al = split(jnp.concatenate([cop[x0, c, pl.ds(z0, 8), :] for c in range(3)], axis=0))
                o = jnp.dot(jnp.concatenate([ah, al], 0), planes[p], preferred_element_type=F32)
                o = o[:24, :128] + o[24:, :128] + o[:24, 128:]
                wz = depths[p]
                for c in range(3):
                    ans[pl.ds(k * 8 + r * 3 + c, 1), :] = jnp.sum(o[8 * c:8 * c + 8] * wz, axis=0, keepdims=True)

    work(list(range(unroll)))
    for k in range(1, unroll):
        message(k).start()

    def turn(t, carry):
        ks = [t * unroll + u for u in range(unroll)]
        work(ks)
        for k in ks:
            message(k).start()
        return carry

    lax.fori_loop(1, 128 // unroll, turn, 0)
    ret[0:8] = ans[0:8]

    def settle(k, carry):
        message(k).wait_recv()
        return carry

    lax.fori_loop(1, 128, settle, 0)

    def end(k, carry):
        message(k).wait_send()
        return carry

    lax.fori_loop(1, 128, end, 0)


def project_call(corners, arrived, widened, velocity, unroll=4, chunks=(0, 16, 56, 88, 128)):
    shapes = (3, 16, 8, 128), (16, 8, 128), (1024, 128)
    return pl.pallas_call(
        functools.partial(project_body, unroll, chunks),
        out_shape=tuple(jax.ShapeDtypeStruct(s, F32) for s in shapes),
        in_specs=[SM, VM, VM, ANY],
        out_specs=(VM,) * 3,
        scratch_shapes=[
            pltpu.VMEM((3, 16, 8, 128), F32),
            pltpu.SemaphoreType.DMA,
            pltpu.VMEM((3, 24, 16, 128), F32),
            pltpu.VMEM((3, 18, 24, 128), F32),
            pltpu.VMEM((3, 32, 24, 128), F32),
            pltpu.VMEM((32, 24, 128), F32),
            pltpu.VMEM((32, 24, 128), F32),
            pltpu.VMEM((32, 24, 128), F32),
            pltpu.VMEM((3, 3, 16, 8, 128), F32),
            pltpu.VMEM((4, 8 * unroll, 128), F32),
            pltpu.VMEM((2 * unroll, 8, 128), F32),
            pltpu.VMEM((256, 128, 256), BF),
            pltpu.VMEM((256, 8, 128), F32),
            pltpu.VMEM((16, 3, 128, 128), F32),
            pltpu.VMEM((1024, 128), F32),
            pltpu.SemaphoreType.REGULAR,
            pltpu.SemaphoreType.DMA((32,)),
            pltpu.SemaphoreType.DMA((32,)),
            pltpu.SemaphoreType.DMA((128,)),
            pltpu.SemaphoreType.DMA((128,)),
        ],
        compiler_params=pltpu.CompilerParams(vmem_limit_bytes=40 * 2**20, collective_id=0, has_side_effects=True),
        name="project",
    )(corners, arrived, widened, velocity)


def finish_body(back, ret, new_ref, prs_ref, out_new, out_prs, out, sems):
    copies = [pltpu.make_async_copy(new_ref, out_new, sems.at[0]), pltpu.make_async_copy(prs_ref, out_prs, sems.at[1])]
    for copy in copies:
        copy.start()
    pick = back[...].astype(BF)
    for c in range(3):
        data = jnp.concatenate([ret[pl.ds(r * 3 + c, 128, stride=8), :] for r in range(2)], axis=0)
        got = jnp.dot(pick, jnp.concatenate(split3(data), axis=1), preferred_element_type=F32)
        out[c] = got[:, :128] + (got[:, 128:256] + got[:, 256:])
    for copy in copies:
        copy.wait()


def finish_call(back, ret, new, pressure):
    shapes = (3, 16, 8, 128), (16, 8, 128), (3, 128, 128)
    return pl.pallas_call(
        finish_body,
        out_shape=tuple(jax.ShapeDtypeStruct(s, F32) for s in shapes),
        in_specs=[VM, VM, VM, VM],
        out_specs=(ANY, ANY, VM),
        scratch_shapes=[pltpu.SemaphoreType.DMA((2,))],
        compiler_params=pltpu.CompilerParams(vmem_limit_bytes=32 * 2**20),
        name="finish",
    )(back, ret, new, pressure)


def shards(velocity, offsets, forces, owner, base, counts):
    arrived, boxes, corners, back = exchange_call(counts, owner, offsets, forces, base)
    widened = deposit_call(corners, boxes)
    new_velocity, pressure, returned = project_call(corners, arrived.reshape(128, 16, 128), widened, velocity)
    return finish_call(back, returned, new_velocity, pressure)


def solution(mesh):
    return jax.shard_map(
        shards,
        mesh=mesh,
        in_specs=(
            P(None, "gx", "gy", None),
            P(None, ("gx", "gy"), None),
            P(None, ("gx", "gy"), None),
            P(("gx", "gy")),
            P(None, ("gx", "gy")),
            P(("gx", "gy")),
        ),
        out_specs=(P(None, "gx", "gy", None), P("gx", "gy", None), P(None, ("gx", "gy"), None)),
        check_vma=False,
    )
```

time: 92.8 us -> 83.4 us (0.90)
  Pallas kernels: 86.1 us -> 78.6 us
  local copies, waits for them, and re-layouts: 5.17 us -> 3.19 us
    pallas_call x2, Pallas kernels: 49.4 us -> 43.1 us  [the longest x1 41.7 us: project_call(): pl.pallas_call(functools.partial(project_body, unroll, chunks), out_shape...]
    unnamed x13 -> x10, local copies, waits for them, and re-layouts: 5.17 us -> 3.19 us
    pallas_call x1, Pallas kernels: 33.3 us -> 32.3 us  [exchange_call(): pl.pallas_call(functools.partial(exchange_body, unroll), out_shape=tuple(...]
where the time goes in v4:
time: 83.4 us; the launch traced here: 83.2 us
  Pallas kernels  78.6 us (94%)
  local copies, waits for them, and re-layouts  3.19 us (4%)
  between operations  1.37 us (2%)
    pallas_call x1, Pallas kernels, project_call(): pl.pallas_call(functools.partial(project_body, unroll, chunks), out_shape...  41.7 us
    pallas_call x1, Pallas kernels, exchange_call(): pl.pallas_call(functools.partial(exchange_body, unroll), out_shape=tuple(...  32.3 us
    pallas_call x1, Pallas kernels, deposit_call(): pl.pallas_call(deposit_body, out_shape=jax.ShapeDtypeStruct((3, 24, 16, 1...  3.22 us
    unnamed x10, local copies, waits for them, and re-layouts  3.19 us

profile of v4, /device:TPU:1, one launch (start us, length us, event | category | flops | bytes accessed | tf_op | source)
XLA Modules:
  0.0 83.2 jit_solution(3844487077835860899)
XLA Ops:
  0.6 0.0 copy-start
  1.3 0.0 copy-start.1
  1.3 0.9 %copy-done.1 = f32[3,128,128]{2,1,0:T(8,128)S(1)} copy-done((f32[3,128,128]{2,1,0:T(8,128)S(1)}, f32[3,128,128]{2,1,0:T(8,128)}, u32[]{:S(2)}) %copy-start.1) | copy-done | bytes 196632
  2.3 0.0 copy-start.2
  2.3 0.9 %copy-done.2 = f32[3,128,128]{2,1,0:T(8,128)S(1)} copy-done((f32[3,128,128]{2,1,0:T(8,128)S(1)}, f32[3,128,128]{2,1,0:T(8,128)}, u32[]{:S(2)}) %copy-start.2) | copy-done | bytes 196632
  3.2 0.0 copy-start.3
  3.2 0.7 copy-done.3
  3.9 0.0 copy-start.4
  3.9 0.7 copy-done.4
  4.5 32.3 %exchange.1 = (f32[2048,128]{1,0:T(8,128)S(1)}, f32[256,24,128]{2,1,0:T(8,128)S(1)}, s32[8,128]{1,0:T(8,128)S(1)}, f32[128,256]{1,0:T(8,128)S(1)}) custom-call(s32[1]{0:T(128)S(6)} %copy.9.count_s, s32[1,128]{1,0:T(1,128)S(1)} %bitcast.3, f32[3,128,128]{2,1,0:T(8,128)S(1)} %copy-done.1, f32[3,128,128]{2,1,0:T(8,128)S(1)} %copy-done.2, s32[3,128]{1,0:T(4,128)S(1)} %copy-done.3), custom_call_target="tpu_custom_call" | custom-call | tf_op jit(solution)/shard_map/exchange/pallas_call | solution.py:193
  36.8 3.2 %deposit.1.w_ref = f32[3,24,16,128]{3,2,1,0:T(8,128)S(1)} custom-call(s32[8,128]{1,0:T(8,128)S(1)} %get-tuple-element.11.corners_s, f32[256,24,128]{2,1,0:T(8,128)S(1)} %get-tuple-element.13.boxes), custom_call_target="tpu_custom_call" | custom-call | tf_op jit(solution)/shard_map/deposit/pallas_call | solution.py:244
  40.1 0.0 copy-done
  40.1 41.7 %project.1 = (f32[3,16,8,128]{3,2,1,0:T(8,128)S(1)}, f32[16,8,128]{2,1,0:T(8,128)S(1)}, f32[1024,128]{1,0:T(8,128)S(1)}) custom-call(s32[8,128]{1,0:T(8,128)S(1)} %get-tuple-element.11.corners_s, f32[128,16,128]{2,1,0:T(8,128)S(1)} %bitcast.2, f32[3,24,16,128]{3,2,1,0:T(8,128)S(1)} %deposit.1.w_ref, f32[3,16,8,128]{3,2,1,0:T(8,128)S(1)} %copy-done), custom_call_target="tpu_custom_call" | custom-call | tf_op jit(solution)/shard_map/project/pallas_call | solution.py:487
  81.8 1.4 %finish.1 = (f32[3,16,8,128]{3,2,1,0:T(8,128)}, f32[16,8,128]{2,1,0:T(8,128)}, f32[3,128,128]{2,1,0:T(8,128)}) custom-call(f32[128,256]{1,0:T(8,128)S(1)} %get-tuple-element.10.back, f32[1024,128]{1,0:T(8,128)S(1)} %get-tuple-element.14.ret, f32[3,16,8,128]{3,2,1,0:T(8,128)S(1)} %get-tuple-element.15.new_ref, f32[16,8,128]{2,1,0:T(8,128)S(1)} %get-tuple-element.16.prs_ref), custom_call_target="tpu_custom_call" | custom-call | tf_op jit(solution)/shard_map/finish/pallas_call | solution.py:534
Async XLA Ops:
  0.6 39.4 %copy-start = (f32[3,16,8,128]{3,2,1,0:T(8,128)S(1)}, f32[3,16,8,128]{3,2,1,0:T(8,128)}, u32[]{:S(2)}) copy-start(f32[3,16,8,128]{3,2,1,0:T(8,128)} %vel_hbm.1) | copy-start | bytes 589828
  1.3 0.9 %copy-start.1 = (f32[3,128,128]{2,1,0:T(8,128)S(1)}, f32[3,128,128]{2,1,0:T(8,128)}, u32[]{:S(2)}) copy-start(f32[3,128,128]{2,1,0:T(8,128)} %off_hbm.1) | copy-start | bytes 589828
  2.3 0.9 %copy-start.2 = (f32[3,128,128]{2,1,0:T(8,128)S(1)}, f32[3,128,128]{2,1,0:T(8,128)}, u32[]{:S(2)}) copy-start(f32[3,128,128]{2,1,0:T(8,128)} %frc_hbm.1) | copy-start | bytes 589828
  3.2 0.7 copy-start.3
  3.9 0.7 copy-start.4

commit v5 on v4

--- a/solution.py
+++ b/solution.py
@@ -49,7 +49,7 @@
 
 def spread_rows(stage, row, values):
     for d in range(0, 128, 8):
-        stage[pl.ds(d * 16 + row, 8, stride=16), :] = values[d:d + 8]
+        stage[pl.ds(d % 64 * 32 + d // 64 * 13 + row, 8, stride=32), :] = values[d:d + 8]
 
 
 def pack_rows(first, second, off_ref, frc_ref, base_ref, stage):
@@ -60,7 +60,7 @@
         got = jnp.dot(both, parts, preferred_element_type=F32)
         got = got[:, :128] + (got[:, 128:256] + got[:, 256:])
         for r in range(2):
-            spread_rows(stage, (q // 3) * 8 + r * 3 + q % 3, got[r * 128:r * 128 + 128])
+            spread_rows(stage, (q // 3) * 7 + r * 3 + q % 3, got[r * 128:r * 128 + 128])
     rows = base_ref[...].astype(F32)
     none = jnp.zeros((122, 128), F32)
     blank = jnp.zeros((3, 128), F32)
@@ -70,8 +70,6 @@
     corner = lax.dot_general(both[:128], one, dims, preferred_element_type=F32)
     corner += lax.dot_general(both[128:], two, dims, preferred_element_type=F32)
     spread_rows(stage, 6, corner)
-    for row in (7, 14, 15):
-        spread_rows(stage, row, jnp.zeros((128, 128), F32))
 
 
 VM = pl.BlockSpec(memory_space=pltpu.VMEM)
@@ -84,12 +82,17 @@
     return gx >> 1, gx & 1, gy >> 2, gy & 3
 
 
-def shifted(k, here, sign):
+def shifted(chip, here, sign):
     y, core, z, x = here
-    kc, kx, ky, kz = k & 1, (k >> 1) & 3, (k >> 3) & 3, k >> 5
+    kx, ky, kz = chip & 3, (chip >> 2) & 3, chip >> 4
     if sign < 0:
         kx, ky, kz = 4 - kx, 4 - ky, 4 - kz
-    return (((y + ky) & 3) * 2 + ((core + kc) & 1), ((z + kz) & 3) * 4 + ((x + kx) & 3))
+    return (((y + ky) & 3) * 2 + core, ((z + kz) & 3) * 4 + ((x + kx) & 3))
+
+
+def sibling(here):
+    y, core, z, x = here
+    return (y * 2 + 1 - core, z * 4 + x)
 
 
 def steps_to(owner, here):
@@ -97,7 +100,7 @@
     row, column = owner >> 4, owner & 15
     kc, ky = ((row & 1) - core) & 1, ((row >> 1) - y) & 3
     kz, kx = ((column >> 2) - z) & 3, ((column & 3) - x) & 3
-    return kc + 2 * kx + 8 * ky + 32 * kz
+    return kx + 4 * ky + 16 * kz + 64 * kc
 
 
 def greet_all(line_sem, between):
@@ -114,7 +117,7 @@
     pl.semaphore_wait(line_sem, 7)
 
 
-def exchange_body(unroll, count_s, owner_ref, off_hbm, frc_hbm, base_ref, arrived, boxes, corners, back, off_ref, frc_ref, load, stage, fl, a1, a2, q8, wxs, line_sem, send, recv):
+def exchange_body(count_s, owner_ref, off_hbm, frc_hbm, base_ref, inbox, relay, boxes, corners, back, off_ref, frc_ref, load, stage, tables, wxs, line_sem, send, recv, pass_sem, take_sem):
     here = position()
     loads = [pltpu.make_async_copy(off_hbm, off_ref, load.at[0]), pltpu.make_async_copy(frc_hbm, frc_ref, load.at[1])]
     for copy in loads:
@@ -130,76 +133,93 @@
 
     greet_all(line_sem, prepare)
 
-    def message(k):
-        rows = pl.ds(pl.multiple_of(k * 16, 16), 14)
-        return pltpu.make_async_remote_copy(stage.at[rows], arrived.at[rows], send.at[k], recv.at[k], device_id=shifted(k, here, 1), device_id_type=MESH)
-
-    def begin(k, carry):
-        message(k).start()
-        return carry
-
-    lax.fori_loop(1, 128, begin, 0)
-    arrived[0:16] = stage[0:16]
+    def message(chip):
+        rows = pl.ds(pl.multiple_of(chip * 32, 32), 26)
+        return pltpu.make_async_remote_copy(stage.at[rows], inbox.at[rows], send.at[chip], recv.at[chip], device_id=shifted(chip, here, 1), device_id_type=MESH)
+
+    def onward(group):
+        return pltpu.make_async_remote_copy(
+            inbox.reshape(64, 32, 128).at[pl.ds(group * 8, 8), pl.ds(13, 13)],
+            relay.reshape(64, 16, 128).at[pl.ds(group * 8, 8), pl.ds(0, 13)],
+            pass_sem.at[group], take_sem.at[group], device_id=sibling(here), device_id_type=MESH)
+
+    def begin(chip, carry):
+        message(chip).start()
+        return carry
+
+    lax.fori_loop(1, 64, begin, 0, unroll=7)
+    inbox[0:32] = stage[0:32]
     iota8 = lax.broadcasted_iota(jnp.int32, (8, 128), 0).astype(F32) - 3.0
     iota16 = lax.broadcasted_iota(jnp.int32, (16, 128), 0).astype(F32) - 3.0
-    tabs = (fl, a1, a2, q8)
-
-    def work(ks):
-        for u, k in enumerate(ks):
-            at = k * 16 if isinstance(k, int) else pl.multiple_of(k * 16, 16)
-            t = arrived[pl.ds(at, 8), :]
+    tabs = [tables.at[n] for n in range(4)]
+
+    def work(box, pitch, group, shift):
+        for u in range(8):
+            at = group * (8 * pitch) + u * pitch
+            t = box[pl.ds(at, 8), :]
             whole = jnp.floor(t)
             f = t - whole
-            fl[u * 8:u * 8 + 8, :] = whole
-            a1[u * 8:u * 8 + 8, :] = (3.0 - 2.0 * f) * 0.125
-            a2[u * 8:u * 8 + 8, :] = (1.0 + 2.0 * f) * 0.125
-            q8[u * 8:u * 8 + 8, :] = jnp.sqrt(1.0 + 4.0 * f * (1.0 - f)) * 0.125
-        for u, k in enumerate(ks):
+            for n, v in enumerate((whole, (3.0 - 2.0 * f) * 0.125, (1.0 + 2.0 * f) * 0.125, jnp.sqrt(1.0 + 4.0 * f * (1.0 - f)) * 0.125)):
+                tables[n, u * 8:u * 8 + 8, :] = v
+        for u in range(8):
+            at = group * (8 * pitch) + u * pitch
             for r in range(2):
                 row = u * 8 + r * 3
-                y0 = arrived[pl.ds(k * 16 + 6, 1), r * 3 + 1:r * 3 + 2]
+                y0 = box[pl.ds(at + 6, 1), r * 3 + 1:r * 3 + 2]
                 B = plane_of(y0, row, tabs, wxs.at[u * 2 + r], iota8, iota16)
                 wz = weight(iota8, row + 2, tabs)
-                A = jnp.concatenate([arrived[pl.ds(k * 16 + 8 + r * 3 + c, 1), :] * wz for c in range(3)], axis=0)
+                A = jnp.concatenate([box[pl.ds(at + 7 + r * 3 + c, 1), :] * wz for c in range(3)], axis=0)
                 ah, al = split(A)
                 bh, bl = split(B)
-                o = lax.dot_general(jnp.concatenate([ah, al], 0), jnp.concatenate([bh, bl], 0), (((1,), (1,)), ((), ())), preferred_element_type=F32)
-                boxes[k * 2 + r] = o[:24, :128] + o[24:, :128] + o[:24, 128:]
-
-    for k in range(1, unroll):
-        message(k).wait_recv()
-    work(list(range(unroll)))
-
-    def turn(t, carry):
-        ks = [t * unroll + u for u in range(unroll)]
-        for k in ks:
-            message(k).wait_recv()
-        work(ks)
-        return carry
-
-    lax.fori_loop(1, 128 // unroll, turn, 0)
-    gathered = jnp.concatenate([arrived[pl.ds(d * 16 + 6, 8, stride=16), :] for d in range(0, 128, 8)], axis=0)
+                both = jnp.concatenate([ah, al], 0)
+                o = lax.dot_general(jnp.concatenate([both, both], 1), jnp.concatenate([bh, bl], 1), (((1,), (1,)), ((), ())), preferred_element_type=F32)
+                boxes[(shift + group * 8 + u) * 2 + r] = o[:24] + o[24:]
+
+    for chip in range(1, 8):
+        message(chip).wait_recv()
+    onward(0).start()
+    work(inbox, 32, 0, 0)
+
+    def turn(group, carry):
+        for u in range(8):
+            message(group * 8 + u).wait_recv()
+        onward(group).start()
+        work(inbox, 32, group, 0)
+        onward(group - 1).wait_recv()
+        work(relay, 16, group - 1, 64)
+        return carry
+
+    lax.fori_loop(1, 8, turn, 0)
+    onward(7).wait_recv()
+    work(relay, 16, 7, 64)
+    gathered = jnp.concatenate([inbox[pl.ds(d * 32 + 6, 8, stride=32), :] for d in range(0, 64, 8)] + [relay[pl.ds(d * 16 + 6, 8, stride=16), :] for d in range(0, 64, 8)], axis=0)
     corners[...] = gathered.T[0:8].astype(jnp.int32)
 
-    def end(k, carry):
-        message(k).wait_send()
-        return carry
-
-    lax.fori_loop(1, 128, end, 0)
-
-
-def exchange_call(counts, owner, offsets, forces, base, unroll=8):
-    shapes = ((2048, 128), F32), ((256, 24, 128), F32), ((8, 128), jnp.int32), ((128, 256), F32)
+    def end(chip, carry):
+        message(chip).wait_send()
+        return carry
+
+    lax.fori_loop(1, 64, end, 0)
+    for group in range(8):
+        onward(group).wait_send()
+
+
+def exchange_call(counts, owner, offsets, forces, base):
+    shapes = ((2048, 128), F32), ((1024, 128), F32), ((256, 24, 128), F32), ((8, 128), jnp.int32), ((128, 256), F32)
     return pl.pallas_call(
-        functools.partial(exchange_body, unroll),
+        exchange_body,
         out_shape=tuple(jax.ShapeDtypeStruct(*s) for s in shapes),
         in_specs=[SM, VM, ANY, ANY, VM],
-        out_specs=(VM,) * 4,
-        scratch_shapes=[pltpu.VMEM((3, 128, 128), F32), pltpu.VMEM((3, 128, 128), F32), pltpu.SemaphoreType.DMA((2,))] + [pltpu.VMEM((2048, 128), F32)] + [pltpu.VMEM((8 * unroll, 128), F32)] * 4 + [
-            pltpu.VMEM((2 * unroll, 8, 128), F32),
+        out_specs=(VM,) * 5,
+        scratch_shapes=[pltpu.VMEM((3, 128, 128), F32), pltpu.VMEM((3, 128, 128), F32), pltpu.SemaphoreType.DMA((2,))] + [
+            pltpu.VMEM((2048, 128), F32),
+            pltpu.VMEM((4, 64, 128), F32),
+            pltpu.VMEM((16, 8, 128), F32),
             pltpu.SemaphoreType.REGULAR,
-            pltpu.SemaphoreType.DMA((128,)),
-            pltpu.SemaphoreType.DMA((128,)),
+            pltpu.SemaphoreType.DMA((64,)),
+            pltpu.SemaphoreType.DMA((64,)),
+            pltpu.SemaphoreType.DMA((8,)),
+            pltpu.SemaphoreType.DMA((8,)),
         ],
         compiler_params=pltpu.CompilerParams(vmem_limit_bytes=40 * 2**20, collective_id=1, has_side_effects=True),
         name="exchange",
@@ -276,7 +296,7 @@
     return above, below
 
 
-def project_body(unroll, chunks, corners_s, arrived, w_ref, vel_hbm, new_ref, prs_ref, ret, vel_ref, load, v_ref, ve, pe, src, pa, pb, fold, tables, wxs, planes, depths, cop, ans, line_sem, send, recv, out_sem, in_sem):
+def project_body(unroll, chunks, corners_s, inbox, relay, w_ref, vel_hbm, new_ref, prs_ref, direct, passed, vel_ref, load, v_ref, ve, pe, src, pa, pb, fold, tables, wxs, planes, depths, cop, ans, line_sem, send, recv, out_sem, in_sem, pass_sem, take_sem):
     here = position()
     peers = neighbours()
     gx, gy = lax.axis_index("gx"), lax.axis_index("gy")
@@ -294,20 +314,23 @@
     iota16 = lax.broadcasted_iota(jnp.int32, (16, 128), 0).astype(F32) - 3.0
 
     def weigh(begin, end):
+        box, pitch, shift = (inbox, 32, 0) if begin < 64 else (relay, 16, 64)
+
         def turn(t, carry):
             for u in range(unroll):
                 k = t * unroll + u
                 rows = pl.ds(u * 8, 8)
-                whole = jnp.floor(arrived[k, 0:8, :])
-                f = arrived[k, 0:8, :] - whole
+                v = box[pl.ds((k - shift) * pitch, 8), :]
+                whole = jnp.floor(v)
+                f = v - whole
                 for n, v in enumerate((whole, (3.0 - 2.0 * f) * 0.125, (1.0 + 2.0 * f) * 0.125, jnp.sqrt(1.0 + 4.0 * f * (1.0 - f)) * 0.125)):
                     tables[n, rows, :] = v
                 for r in range(2):
                     row, p = u * 8 + r * 3, k * 2 + r
                     tabs = [tables.at[n] for n in range(4)]
                     bh, bl = split(plane_of(corners_s[r * 3 + 1, k].astype(F32), row, tabs, wxs.at[u * 2 + r], iota8, iota16))
-                    planes[p, :, :128] = bh
-                    planes[p, :, 128:] = bl
+                    planes[p, :128] = bh
+                    planes[p, 128:] = bl
                     depths[p] = weight(iota8, row + 2, tabs)
             return carry
 
@@ -423,8 +446,6 @@
     lax.fori_loop(5, 27, finish, 0, unroll=11)
     new_ref[...] = v_ref[:, 3:19, 3:11, :]
     prs_ref[...] = pa[8:24, 8:16, :]
-    for copy in started:
-        copy.wait_send()
 
 
     for c in range(3):
@@ -438,57 +459,70 @@
                 for t in range(2):
                     cop[8 * t + r, c] = jnp.where(wide < 128 - 16 * r, ro[t], ro[t + 1])
 
-    def message(k):
-        rows = pl.ds(pl.multiple_of(k * 8, 8), 6)
-        return pltpu.make_async_remote_copy(ans.at[rows], ret.at[rows], out_sem.at[k], in_sem.at[k], device_id=shifted(k, here, -1), device_id_type=MESH)
-
-    def work(ks):
-        for k in ks:
-            for r in range(2):
-                p = k * 2 + r
-                x0 = corners_s[r * 3, k]
-                z0 = jnp.maximum(corners_s[r * 3 + 2, k] - 3, 0)
-                ah, al = split(jnp.concatenate([cop[x0, c, pl.ds(z0, 8), :] for c in range(3)], axis=0))
-                o = jnp.dot(jnp.concatenate([ah, al], 0), planes[p], preferred_element_type=F32)
-                o = o[:24, :128] + o[24:, :128] + o[:24, 128:]
-                wz = depths[p]
-                for c in range(3):
-                    ans[pl.ds(k * 8 + r * 3 + c, 1), :] = jnp.sum(o[8 * c:8 * c + 8] * wz, axis=0, keepdims=True)
-
-    work(list(range(unroll)))
-    for k in range(1, unroll):
-        message(k).start()
+    def message(chip):
+        rows = pl.ds(pl.multiple_of(chip * 16, 16), 12)
+        return pltpu.make_async_remote_copy(ans.at[rows], direct.at[rows], out_sem.at[chip], in_sem.at[chip], device_id=shifted(chip, here, -1), device_id_type=MESH)
+
+    def onward(group):
+        return pltpu.make_async_remote_copy(
+            direct.reshape(64, 16, 128).at[pl.ds(group * 16, 16), pl.ds(6, 6)],
+            passed.reshape(64, 8, 128).at[pl.ds(group * 16, 16), pl.ds(0, 6)],
+            pass_sem.at[group], take_sem.at[group], device_id=sibling(here), device_id_type=MESH)
+
+    def work(chips):
+        for chip in chips:
+            for kc in range(2):
+                k = chip + 64 * kc
+                for r in range(2):
+                    p = k * 2 + r
+                    x0 = corners_s[r * 3, k]
+                    z0 = jnp.maximum(corners_s[r * 3 + 2, k] - 3, 0)
+                    ah, al = split(jnp.concatenate([cop[x0, c, pl.ds(z0, 8), :] for c in range(3)], axis=0))
+                    both = jnp.concatenate([ah, al], 0)
+                    o = jnp.dot(jnp.concatenate([both, both], 1), planes[p], preferred_element_type=F32)
+                    o = o[:24] + o[24:]
+                    wz = depths[p]
+                    for c in range(3):
+                        ans[pl.ds(chip * 16 + kc * 6 + r * 3 + c, 1), :] = jnp.sum(o[8 * c:8 * c + 8] * wz, axis=0, keepdims=True)
+
+    work(list(range(4)))
+    for chip in range(1, 4):
+        message(chip).start()
 
     def turn(t, carry):
-        ks = [t * unroll + u for u in range(unroll)]
-        work(ks)
-        for k in ks:
-            message(k).start()
-        return carry
-
-    lax.fori_loop(1, 128 // unroll, turn, 0)
-    ret[0:8] = ans[0:8]
-
-    def settle(k, carry):
-        message(k).wait_recv()
-        return carry
-
-    lax.fori_loop(1, 128, settle, 0)
-
-    def end(k, carry):
-        message(k).wait_send()
-        return carry
-
-    lax.fori_loop(1, 128, end, 0)
-
-
-def project_call(corners, arrived, widened, velocity, unroll=4, chunks=(0, 16, 56, 88, 128)):
-    shapes = (3, 16, 8, 128), (16, 8, 128), (1024, 128)
+        chips = [t * 4 + u for u in range(4)]
+        work(chips)
+        for chip in chips:
+            message(chip).start()
+        return carry
+
+    lax.fori_loop(1, 16, turn, 0)
+    direct[0:16] = ans[0:16]
+    for group in range(4):
+        for chip in range(max(group * 16, 1), group * 16 + 16):
+            message(chip).wait_recv()
+        onward(group).start()
+    for group in range(4):
+        onward(group).wait_recv()
+
+    def end(chip, carry):
+        message(chip).wait_send()
+        return carry
+
+    lax.fori_loop(1, 64, end, 0)
+    for group in range(4):
+        onward(group).wait_send()
+    for copy in started:
+        copy.wait_send()
+
+
+def project_call(corners, inbox, relay, widened, velocity, unroll=4, chunks=(0, 24, 64, 96, 128)):
+    shapes = (3, 16, 8, 128), (16, 8, 128), (1024, 128), (512, 128)
     return pl.pallas_call(
         functools.partial(project_body, unroll, chunks),
         out_shape=tuple(jax.ShapeDtypeStruct(s, F32) for s in shapes),
-        in_specs=[SM, VM, VM, ANY],
-        out_specs=(VM,) * 3,
+        in_specs=[SM, VM, VM, VM, ANY],
+        out_specs=(VM,) * 4,
         scratch_shapes=[
             pltpu.VMEM((3, 16, 8, 128), F32),
             pltpu.SemaphoreType.DMA,
@@ -501,52 +535,54 @@
             pltpu.VMEM((3, 3, 16, 8, 128), F32),
             pltpu.VMEM((4, 8 * unroll, 128), F32),
             pltpu.VMEM((2 * unroll, 8, 128), F32),
-            pltpu.VMEM((256, 128, 256), BF),
+            pltpu.VMEM((256, 256, 128), BF),
             pltpu.VMEM((256, 8, 128), F32),
             pltpu.VMEM((16, 3, 128, 128), F32),
             pltpu.VMEM((1024, 128), F32),
             pltpu.SemaphoreType.REGULAR,
             pltpu.SemaphoreType.DMA((32,)),
             pltpu.SemaphoreType.DMA((32,)),
-            pltpu.SemaphoreType.DMA((128,)),
-            pltpu.SemaphoreType.DMA((128,)),
+            pltpu.SemaphoreType.DMA((64,)),
+            pltpu.SemaphoreType.DMA((64,)),
+            pltpu.SemaphoreType.DMA((4,)),
+            pltpu.SemaphoreType.DMA((4,)),
         ],
         compiler_params=pltpu.CompilerParams(vmem_limit_bytes=40 * 2**20, collective_id=0, has_side_effects=True),
         name="project",
-    )(corners, arrived, widened, velocity)
-
-
-def finish_body(back, ret, new_ref, prs_ref, out_new, out_prs, out, sems):
+    )(corners, inbox, relay, widened, velocity)
+
+
+def finish_body(back, direct, passed, new_ref, prs_ref, out_new, out_prs, out, sems):
     copies = [pltpu.make_async_copy(new_ref, out_new, sems.at[0]), pltpu.make_async_copy(prs_ref, out_prs, sems.at[1])]
     for copy in copies:
         copy.start()
     pick = back[...].astype(BF)
     for c in range(3):
-        data = jnp.concatenate([ret[pl.ds(r * 3 + c, 128, stride=8), :] for r in range(2)], axis=0)
+        data = jnp.concatenate([box[pl.ds(r * 3 + c, 64, stride=pitch), :] for r in range(2) for box, pitch in ((direct, 16), (passed, 8))], axis=0)
         got = jnp.dot(pick, jnp.concatenate(split3(data), axis=1), preferred_element_type=F32)
         out[c] = got[:, :128] + (got[:, 128:256] + got[:, 256:])
     for copy in copies:
         copy.wait()
 
 
-def finish_call(back, ret, new, pressure):
+def finish_call(back, direct, passed, new, pressure):
     shapes = (3, 16, 8, 128), (16, 8, 128), (3, 128, 128)
     return pl.pallas_call(
         finish_body,
         out_shape=tuple(jax.ShapeDtypeStruct(s, F32) for s in shapes),
-        in_specs=[VM, VM, VM, VM],
+        in_specs=[VM] * 5,
         out_specs=(ANY, ANY, VM),
         scratch_shapes=[pltpu.SemaphoreType.DMA((2,))],
         compiler_params=pltpu.CompilerParams(vmem_limit_bytes=32 * 2**20),
         name="finish",
-    )(back, ret, new, pressure)
+    )(back, direct, passed, new, pressure)
 
 
 def shards(velocity, offsets, forces, owner, base, counts):
-    arrived, boxes, corners, back = exchange_call(counts, owner, offsets, forces, base)
+    inbox, relay, boxes, corners, back = exchange_call(counts, owner, offsets, forces, base)
     widened = deposit_call(corners, boxes)
-    new_velocity, pressure, returned = project_call(corners, arrived.reshape(128, 16, 128), widened, velocity)
-    return finish_call(back, returned, new_velocity, pressure)
+    new_velocity, pressure, direct, passed = project_call(corners, inbox, relay, widened, velocity)
+    return finish_call(back, direct, passed, new_velocity, pressure)
 
 
 def solution(mesh):

time: 83.4 us -> 78.8 us (0.945)
  Pallas kernels: 78.6 us -> 74.1 us
    pallas_call x1, Pallas kernels: 41.7 us -> 38.4 us  [project_call(): pl.pallas_call(functools.partial(project_body, unroll, chunks), out_shape...]
    pallas_call x1, Pallas kernels: 32.3 us -> 30.8 us  [exchange_call(): pl.pallas_call(exchange_body, out_shape=tuple((jax.ShapeDtypeStruct(*s) f...]
where the time goes in v5:
time: 78.8 us; the launch traced here: 78.6 us
  Pallas kernels  74.1 us (94%)
  local copies, waits for them, and re-layouts  3.19 us (4%)
  between operations  1.37 us (2%)
    pallas_call x1, Pallas kernels, project_call(): pl.pallas_call(functools.partial(project_body, unroll, chunks), out_shape...  38.4 us
    pallas_call x1, Pallas kernels, exchange_call(): pl.pallas_call(exchange_body, out_shape=tuple((jax.ShapeDtypeStruct(*s) f...  30.8 us
    pallas_call x1, Pallas kernels, deposit_call(): pl.pallas_call(deposit_body, out_shape=jax.ShapeDtypeStruct((3, 24, 16, 1...  3.35 us
    unnamed x10, local copies, waits for them, and re-layouts  3.19 us

profile of v5, /device:TPU:1, one launch (start us, length us, event | category | flops | bytes accessed | tf_op | source)
XLA Modules:
  0.0 78.6 jit_solution(603259922154042132)
XLA Ops:
  0.6 0.0 copy-start
  1.3 0.0 copy-start.1
  1.3 0.9 %copy-done.1 = f32[3,128,128]{2,1,0:T(8,128)S(1)} copy-done((f32[3,128,128]{2,1,0:T(8,128)S(1)}, f32[3,128,128]{2,1,0:T(8,128)}, u32[]{:S(2)}) %copy-start.1) | copy-done | bytes 196632
  2.3 0.0 copy-start.2
  2.3 0.9 %copy-done.2 = f32[3,128,128]{2,1,0:T(8,128)S(1)} copy-done((f32[3,128,128]{2,1,0:T(8,128)S(1)}, f32[3,128,128]{2,1,0:T(8,128)}, u32[]{:S(2)}) %copy-start.2) | copy-done | bytes 196632
  3.2 0.0 copy-start.3
  3.2 0.7 copy-done.3
  3.9 0.0 copy-start.4
  3.9 0.7 copy-done.4
  4.5 30.8 %exchange.1 = (f32[2048,128]{1,0:T(8,128)S(1)}, f32[1024,128]{1,0:T(8,128)S(1)}, f32[256,24,128]{2,1,0:T(8,128)S(1)}, s32[8,128]{1,0:T(8,128)S(1)}, f32[128,256]{1,0:T(8,128)S(1)}) custom-call(s32[1]{0:T(128)S(6)} %copy.9.count_s, s32[1,128]{1,0:T(1,128)S(1)} %bitcast.1, f32[3,128,128]{2,1,0:T(8,128)S(1)} %copy-done.1, f32[3,128,128]{2,1,0:T(8,128)S(1)} %copy-done.2, ...), custom_call_target="tpu_custom_call" | custom-call | tf_op jit(solution)/shard_map/exchange/pallas_call | solution.py:209
  35.4 3.4 %deposit.1.w_ref = f32[3,24,16,128]{3,2,1,0:T(8,128)S(1)} custom-call(s32[8,128]{1,0:T(8,128)S(1)} %get-tuple-element.13.corners_s, f32[256,24,128]{2,1,0:T(8,128)S(1)} %get-tuple-element.16.boxes), custom_call_target="tpu_custom_call" | custom-call | tf_op jit(solution)/shard_map/deposit/pallas_call | solution.py:264
  38.7 0.0 copy-done
  38.7 38.4 %project.1 = (f32[3,16,8,128]{3,2,1,0:T(8,128)S(1)}, f32[16,8,128]{2,1,0:T(8,128)S(1)}, f32[1024,128]{1,0:T(8,128)S(1)}, f32[512,128]{1,0:T(8,128)S(1)}) custom-call(s32[8,128]{1,0:T(8,128)S(1)} %get-tuple-element.13.corners_s, f32[2048,128]{1,0:T(8,128)S(1)} %get-tuple-element.14.inbox, f32[1024,128]{1,0:T(8,128)S(1)} %get-tuple-element.15.relay, ...), custom_call_target="tpu_custom_call" | custom-call | tf_op jit(solution)/shard_map/project/pallas_call | solution.py:521
  77.2 1.4 %finish.1 = (f32[3,16,8,128]{3,2,1,0:T(8,128)}, f32[16,8,128]{2,1,0:T(8,128)}, f32[3,128,128]{2,1,0:T(8,128)}) custom-call(f32[128,256]{1,0:T(8,128)S(1)} %get-tuple-element.12.back, f32[1024,128]{1,0:T(8,128)S(1)} %get-tuple-element.17.direct, f32[512,128]{1,0:T(8,128)S(1)} %get-tuple-element.18.passed, f32[3,16,8,128]{3,2,1,0:T(8,128)S(1)} %get-tuple-element.19.new_ref, ...), custom_call_target="tpu_custom_call" | custom-call | tf_op jit(solution)/shard_map/finish/pallas_call | solution.py:570
Async XLA Ops:
  0.6 38.1 %copy-start = (f32[3,16,8,128]{3,2,1,0:T(8,128)S(1)}, f32[3,16,8,128]{3,2,1,0:T(8,128)}, u32[]{:S(2)}) copy-start(f32[3,16,8,128]{3,2,1,0:T(8,128)} %vel_hbm.1) | copy-start | bytes 589828
  1.3 0.9 %copy-start.1 = (f32[3,128,128]{2,1,0:T(8,128)S(1)}, f32[3,128,128]{2,1,0:T(8,128)}, u32[]{:S(2)}) copy-start(f32[3,128,128]{2,1,0:T(8,128)} %off_hbm.1) | copy-start | bytes 589828
  2.3 0.9 %copy-start.2 = (f32[3,128,128]{2,1,0:T(8,128)S(1)}, f32[3,128,128]{2,1,0:T(8,128)}, u32[]{:S(2)}) copy-start(f32[3,128,128]{2,1,0:T(8,128)} %frc_hbm.1) | copy-start | bytes 589828
  3.2 0.7 copy-start.3
  3.9 0.7 copy-start.4

commit v6 on v5

--- a/solution.py
+++ b/solution.py
@@ -61,7 +61,7 @@
         got = got[:, :128] + (got[:, 128:256] + got[:, 256:])
         for r in range(2):
             spread_rows(stage, (q // 3) * 7 + r * 3 + q % 3, got[r * 128:r * 128 + 128])
-    rows = base_ref[...].astype(F32)
+    rows = base_ref[0:3].astype(F32)
     none = jnp.zeros((122, 128), F32)
     blank = jnp.zeros((3, 128), F32)
     dims = (((1,), (1,)), ((), ()))
@@ -117,19 +117,23 @@
     pl.semaphore_wait(line_sem, 7)
 
 
-def exchange_body(count_s, owner_ref, off_hbm, frc_hbm, base_ref, inbox, relay, boxes, corners, back, off_ref, frc_ref, load, stage, tables, wxs, line_sem, send, recv, pass_sem, take_sem):
+def exchange_body(route_ref, all_hbm, inbox, relay, boxes, corners, back, ve, off_ref, frc_ref, load, stage, tables, wxs, line_sem, send, recv, pass_sem, take_sem, rim_send, rim_recv):
     here = position()
-    loads = [pltpu.make_async_copy(off_hbm, off_ref, load.at[0]), pltpu.make_async_copy(frc_hbm, frc_ref, load.at[1])]
+    peers = neighbours()
+    velocity_in = pltpu.make_async_copy(all_hbm.at[2].reshape(3, 16, 8, 128), ve.at[:, pl.ds(2, 16), pl.ds(8, 8), :], load.at[2])
+    velocity_in.start()
+    loads = [pltpu.make_async_copy(all_hbm.at[0], off_ref, load.at[0]), pltpu.make_async_copy(all_hbm.at[1], frc_ref, load.at[1])]
     for copy in loads:
         copy.start()
 
     def prepare():
-        first, second = routes(steps_to(owner_ref[...], here), count_s[0])
+        first, second = routes(steps_to(route_ref[3:4], here), route_ref[4:5])
         back[:, :128] = first.T
         back[:, 128:] = second.T
         for copy in loads:
             copy.wait()
-        pack_rows(first, second, off_ref, frc_ref, base_ref, stage)
+        pack_rows(first, second, off_ref, frc_ref, route_ref, stage)
+        velocity_in.wait()
 
     greet_all(line_sem, prepare)
 
@@ -148,15 +152,23 @@
         return carry
 
     lax.fori_loop(1, 64, begin, 0, unroll=7)
+    rims = []
+    for k, (dx, dy) in enumerate(SIDES):
+        width = 2 if k < 4 else 1
+        copy = pltpu.make_async_remote_copy(box(ve, near(dx, 16, width), near(dy, 8, width), 2, 8),
+                                            box(ve, there(dx, 16, width), there(dy, 8, width), 2, 8),
+                                            rim_send.at[k], rim_recv.at[k], device_id=peers[k], device_id_type=MESH)
+        copy.start()
+        rims.append(copy)
     inbox[0:32] = stage[0:32]
     iota8 = lax.broadcasted_iota(jnp.int32, (8, 128), 0).astype(F32) - 3.0
     iota16 = lax.broadcasted_iota(jnp.int32, (16, 128), 0).astype(F32) - 3.0
     tabs = [tables.at[n] for n in range(4)]
 
-    def work(box, pitch, group, shift):
+    def work(held, pitch, group, shift):
         for u in range(8):
             at = group * (8 * pitch) + u * pitch
-            t = box[pl.ds(at, 8), :]
+            t = held[pl.ds(at, 8), :]
             whole = jnp.floor(t)
             f = t - whole
             for n, v in enumerate((whole, (3.0 - 2.0 * f) * 0.125, (1.0 + 2.0 * f) * 0.125, jnp.sqrt(1.0 + 4.0 * f * (1.0 - f)) * 0.125)):
@@ -165,10 +177,10 @@
             at = group * (8 * pitch) + u * pitch
             for r in range(2):
                 row = u * 8 + r * 3
-                y0 = box[pl.ds(at + 6, 1), r * 3 + 1:r * 3 + 2]
+                y0 = held[pl.ds(at + 6, 1), r * 3 + 1:r * 3 + 2]
                 B = plane_of(y0, row, tabs, wxs.at[u * 2 + r], iota8, iota16)
                 wz = weight(iota8, row + 2, tabs)
-                A = jnp.concatenate([box[pl.ds(at + 7 + r * 3 + c, 1), :] * wz for c in range(3)], axis=0)
+                A = jnp.concatenate([held[pl.ds(at + 7 + r * 3 + c, 1), :] * wz for c in range(3)], axis=0)
                 ah, al = split(A)
                 bh, bl = split(B)
                 both = jnp.concatenate([ah, al], 0)
@@ -202,16 +214,18 @@
     lax.fori_loop(1, 64, end, 0)
     for group in range(8):
         onward(group).wait_send()
-
-
-def exchange_call(counts, owner, offsets, forces, base):
-    shapes = ((2048, 128), F32), ((1024, 128), F32), ((256, 24, 128), F32), ((8, 128), jnp.int32), ((128, 256), F32)
+    for copy in rims:
+        copy.wait()
+
+
+def exchange_call(counts, owner, offsets, forces, base, velocity):
+    shapes = ((2048, 128), F32), ((1024, 128), F32), ((256, 24, 128), F32), ((8, 128), jnp.int32), ((128, 256), F32), ((3, 20, 24, 128), F32)
     return pl.pallas_call(
         exchange_body,
         out_shape=tuple(jax.ShapeDtypeStruct(*s) for s in shapes),
-        in_specs=[SM, VM, ANY, ANY, VM],
-        out_specs=(VM,) * 5,
-        scratch_shapes=[pltpu.VMEM((3, 128, 128), F32), pltpu.VMEM((3, 128, 128), F32), pltpu.SemaphoreType.DMA((2,))] + [
+        in_specs=[VM, ANY],
+        out_specs=(VM,) * 6,
+        scratch_shapes=[pltpu.VMEM((3, 128, 128), F32), pltpu.VMEM((3, 128, 128), F32), pltpu.SemaphoreType.DMA((3,))] + [
             pltpu.VMEM((2048, 128), F32),
             pltpu.VMEM((4, 64, 128), F32),
             pltpu.VMEM((16, 8, 128), F32),
@@ -220,10 +234,12 @@
             pltpu.SemaphoreType.DMA((64,)),
             pltpu.SemaphoreType.DMA((8,)),
             pltpu.SemaphoreType.DMA((8,)),
+            pltpu.SemaphoreType.DMA((8,)),
+            pltpu.SemaphoreType.DMA((8,)),
         ],
         compiler_params=pltpu.CompilerParams(vmem_limit_bytes=40 * 2**20, collective_id=1, has_side_effects=True),
         name="exchange",
-    )(counts, owner.reshape(1, 128), offsets, forces, base)
+    )(jnp.concatenate([base, owner[None], jnp.broadcast_to(counts[:, None], (1, 128))], axis=0), jnp.stack([offsets, forces, velocity.reshape(3, 128, 128)]))
 
 
 def deposit_body(corners_s, boxes, out, acc, tot):
@@ -290,37 +306,37 @@
     return (0, size) if step == 0 else ((-width, width) if step > 0 else (size, width))
 
 
+def box(ref, xs, ys, x_at, y_at):
+    return ref.at[..., pl.ds(xs[0] + x_at, xs[1]), pl.ds(ys[0] + y_at, ys[1]), :]
+
+
 def inward(lane, v):
     above = jnp.where(lane == 127, 0.0, pltpu.roll(v, 127, 1))
     below = jnp.where(lane == 0, 0.0, pltpu.roll(v, 1, 1))
     return above, below
 
 
-def project_body(unroll, chunks, corners_s, inbox, relay, w_ref, vel_hbm, new_ref, prs_ref, direct, passed, vel_ref, load, v_ref, ve, pe, src, pa, pb, fold, tables, wxs, planes, depths, cop, ans, line_sem, send, recv, out_sem, in_sem, pass_sem, take_sem):
+def project_body(unroll, chunks, corners_s, inbox, relay, w_ref, ve, new_ref, prs_ref, direct, passed, v_ref, pe, src, pa, pb, fold, tables, wxs, planes, depths, cop, ans, line_sem, send, recv, out_sem, in_sem, pass_sem, take_sem):
     here = position()
     peers = neighbours()
     gx, gy = lax.axis_index("gx"), lax.axis_index("gy")
     barrier = pltpu.get_barrier_semaphore()
-    velocity_in = pltpu.make_async_copy(vel_hbm, vel_ref, load)
-    velocity_in.start()
     fold[...] = jnp.zeros(fold.shape, F32)
     for i in range(1, 16):
         pl.semaphore_signal(barrier, inc=1, device_id=(gx, (gy + i) & 15), device_id_type=MESH)
     for i in range(1, 8):
         pl.semaphore_signal(barrier, inc=1, device_id=((gx + i) & 7, gy), device_id_type=MESH)
-    velocity_in.wait()
-    ve[:, 1:17, 8:16, :] = vel_ref[...]
     iota8 = lax.broadcasted_iota(jnp.int32, (8, 128), 0).astype(F32) - 3.0
     iota16 = lax.broadcasted_iota(jnp.int32, (16, 128), 0).astype(F32) - 3.0
 
     def weigh(begin, end):
-        box, pitch, shift = (inbox, 32, 0) if begin < 64 else (relay, 16, 64)
+        held, pitch, shift = (inbox, 32, 0) if begin < 64 else (relay, 16, 64)
 
         def turn(t, carry):
             for u in range(unroll):
                 k = t * unroll + u
                 rows = pl.ds(u * 8, 8)
-                v = box[pl.ds((k - shift) * pitch, 8), :]
+                v = held[pl.ds((k - shift) * pitch, 8), :]
                 whole = jnp.floor(v)
                 f = v - whole
                 for n, v in enumerate((whole, (3.0 - 2.0 * f) * 0.125, (1.0 + 2.0 * f) * 0.125, jnp.sqrt(1.0 + 4.0 * f * (1.0 - f)) * 0.125)):
@@ -349,44 +365,40 @@
         started.append(copy)
         return copy
 
-    def box(ref, xs, ys, x_at, y_at):
-        return ref.at[..., pl.ds(xs[0] + x_at, xs[1]), pl.ds(ys[0] + y_at, ys[1]), :]
-
     first = []
     for k, (dx, dy) in enumerate(SIDES):
         if k == 4:
             pl.semaphore_wait(line_sem, 7)
-        xs = (3, 16) if dx == 0 else ((19, 3) if dx > 0 else (0, 3))
-        ys = (3, 8) if dy == 0 else ((11, 3) if dy > 0 else (0, 3))
-        xd = (0, 16) if dx == 0 else ((0, 3) if dx > 0 else (13, 3))
-        yd = (0, 8) if dy == 0 else ((0, 3) if dy > 0 else (5, 3))
+        xs = (2, 18) if dx == 0 else ((18, 4) if dx > 0 else (0, 4))
+        ys = (2, 10) if dy == 0 else ((10, 4) if dy > 0 else (0, 4))
+        xd = (0, 18) if dx == 0 else ((0, 4) if dx > 0 else (14, 4))
+        yd = (2, 10) if dy == 0 else ((2, 4) if dy > 0 else (8, 4))
         layer = 0 if dy == 0 else (1 if dx == 0 else 2)
         first.append(push(w_ref.at[:, pl.ds(xs[0], xs[1]), pl.ds(ys[0], ys[1]), :],
                           fold.at[layer, :, pl.ds(xd[0], xd[1]), pl.ds(yd[0], yd[1]), :], k))
-        if k < 4:
-            first.append(push(box(vel_ref, near(dx, 16, 1), near(dy, 8, 1), 0, 0),
-                              box(ve, there(dx, 16, 1), there(dy, 8, 1), 1, 8), k))
     weigh(chunks[1], chunks[2])
     for copy in first:
         copy.wait_recv()
     lane = lax.broadcasted_iota(jnp.int32, (8, 128), 1)
 
+    def provide_rows(x, s):
+        here_ = pl.ds(8 + s, 8)
+        at = pl.ds(3 + s, 8)
+        for c in range(3):
+            v = ve[c, x + 2, here_, :]
+            above, below = inward(lane, v)
+            lap = (ve[c, x + 3, here_, :] + ve[c, x + 1, here_, :]) + (ve[c, x + 2, 9 + s:17 + s, :] + ve[c, x + 2, 7 + s:15 + s, :]) + (above + below) - 6.0 * v
+            force = w_ref[c, x + 3, at, :] + fold[0, c, x + 1, at, :] + fold[1, c, x + 1, at, :] + fold[2, c, x + 1, at, :]
+            pe[c, x + 8, here_, :] = v + time_step * (viscosity * lap + force)
+
     def provide(x, carry):
-        for c in range(3):
-            v = ve[c, x + 1, 8:16, :]
-            above, below = inward(lane, v)
-            lap = (ve[c, x + 2, 8:16, :] + ve[c, x, 8:16, :]) + (ve[c, x + 1, 9:17, :] + ve[c, x + 1, 7:15, :]) + (above + below) - 6.0 * v
-            force = w_ref[c, x + 3, 3:11, :] + fold[0, c, x] + fold[1, c, x] + fold[2, c, x]
-            pe[c, x + 8, 8:16, :] = v + time_step * (viscosity * lap + force)
-        return carry
-
-    lax.fori_loop(0, 16, provide, 0, unroll=8)
-
-    second = [push(box(pe, near(dx, 16, 1), near(dy, 8, 1), 8, 8),
-                   box(pe, there(dx, 16, 1), there(dy, 8, 1), 8, 8), k) for k, (dx, dy) in enumerate(SIDES[:4])]
-    weigh(chunks[2], chunks[3])
-    for copy in second:
-        copy.wait_recv()
+        provide_rows(x, -1)
+        provide_rows(x, 1)
+        return carry
+
+    lax.fori_loop(0, 16, provide, 0, unroll=4)
+    provide_rows(-1, 0)
+    provide_rows(16, 0)
 
     def diverge(x, carry):
         above, below = inward(lane, pe[2, x + 8, 8:16, :])
@@ -408,7 +420,7 @@
         else:
             xs, ys, xd, yd = near(dx, 16, 3), near(dy, 8, 3), there(dx, 16, 3), there(dy, 8, 3)
         fourth.append(push(box(pe, xs, ys, 8, 8), box(pe, xd, yd, 8, 8), k))
-    weigh(chunks[3], chunks[4])
+    weigh(chunks[2], chunks[3])
     for copy in third:
         copy.wait_recv()
 
@@ -516,23 +528,20 @@
         copy.wait_send()
 
 
-def project_call(corners, inbox, relay, widened, velocity, unroll=4, chunks=(0, 24, 64, 96, 128)):
+def project_call(corners, inbox, relay, widened, moving, unroll=4, chunks=(0, 24, 64, 128)):
     shapes = (3, 16, 8, 128), (16, 8, 128), (1024, 128), (512, 128)
     return pl.pallas_call(
         functools.partial(project_body, unroll, chunks),
         out_shape=tuple(jax.ShapeDtypeStruct(s, F32) for s in shapes),
-        in_specs=[SM, VM, VM, VM, ANY],
+        in_specs=[SM, VM, VM, VM, VM],
         out_specs=(VM,) * 4,
         scratch_shapes=[
-            pltpu.VMEM((3, 16, 8, 128), F32),
-            pltpu.SemaphoreType.DMA,
             pltpu.VMEM((3, 24, 16, 128), F32),
-            pltpu.VMEM((3, 18, 24, 128), F32),
             pltpu.VMEM((3, 32, 24, 128), F32),
             pltpu.VMEM((32, 24, 128), F32),
             pltpu.VMEM((32, 24, 128), F32),
             pltpu.VMEM((32, 24, 128), F32),
-            pltpu.VMEM((3, 3, 16, 8, 128), F32),
+            pltpu.VMEM((3, 3, 18, 16, 128), F32),
             pltpu.VMEM((4, 8 * unroll, 128), F32),
             pltpu.VMEM((2 * unroll, 8, 128), F32),
             pltpu.VMEM((256, 256, 128), BF),
@@ -549,7 +558,7 @@
         ],
         compiler_params=pltpu.CompilerParams(vmem_limit_bytes=40 * 2**20, collective_id=0, has_side_effects=True),
         name="project",
-    )(corners, inbox, relay, widened, velocity)
+    )(corners, inbox, relay, widened, moving)
 
 
 def finish_body(back, direct, passed, new_ref, prs_ref, out_new, out_prs, out, sems):
@@ -579,9 +588,9 @@
 
 
 def shards(velocity, offsets, forces, owner, base, counts):
-    inbox, relay, boxes, corners, back = exchange_call(counts, owner, offsets, forces, base)
+    inbox, relay, boxes, corners, back, moving = exchange_call(counts, owner, offsets, forces, base, velocity)
     widened = deposit_call(corners, boxes)
-    new_velocity, pressure, direct, passed = project_call(corners, inbox, relay, widened, velocity)
+    new_velocity, pressure, direct, passed = project_call(corners, inbox, relay, widened, moving)
     return finish_call(back, direct, passed, new_velocity, pressure)
 
 

time: 78.8 us -> 75 us (0.952)
  local copies, waits for them, and re-layouts: 3.19 us -> 0.07 us
  Pallas kernels: 74.1 us -> 71.5 us
  other arithmetic: 0 us -> 1.92 us
    pallas_call x1, Pallas kernels: 38.4 us -> 33.9 us  [project_call(): pl.pallas_call(functools.partial(project_body, unroll, chunks), out_shape...]
    unnamed x10 -> x0, local copies, waits for them, and re-layouts: 3.19 us -> none
    pallas_call x1, Pallas kernels: 30.8 us -> 32.8 us  [exchange_call(): pl.pallas_call(exchange_body, out_shape=tuple((jax.ShapeDtypeStruct(*s) f...]
    another operation x0 -> x1, other arithmetic: none -> 1.15 us  [exchange_call(): jnp.stack([offsets, forces, velocity.reshape(3, 128, 128)])]
where the time goes in v6:
time: 75 us; the launch traced here: 74.8 us
  Pallas kernels  71.5 us (95%)
  other arithmetic  1.92 us (3%)
  between operations  1.31 us (2%)
    pallas_call x1, Pallas kernels, project_call(): pl.pallas_call(functools.partial(project_body, unroll, chunks), out_shape...  33.9 us
    pallas_call x1, Pallas kernels, exchange_call(): pl.pallas_call(exchange_body, out_shape=tuple((jax.ShapeDtypeStruct(*s) f...  32.8 us
    pallas_call x1, Pallas kernels, deposit_call(): pl.pallas_call(deposit_body, out_shape=jax.ShapeDtypeStruct((3, 24, 16, 1...  3.37 us

profile of v6, /device:TPU:1, one launch (start us, length us, event | category | flops | bytes accessed | tf_op | source)
XLA Modules:
  0.0 74.8 jit_solution(361567365647267014)
XLA Ops:
  1.3 0.1 pad.5.clone
  1.4 0.8 %add_add_fusion.route_ref = s32[5,128]{1,0:T(8,128)S(1)} fusion(s32[1,128]{1,0:T(1,128)} %bitcast.8, s32[3,128]{1,0:T(4,128)} %param.10, s32[5]{0:T(128)S(1)} %pad.5.clone), kind=kLoop, calls=%fused_computation.1 | loop fusion | flops 1280 | bytes 4628 | tf_op jit(solution)/shard_map/concatenate | solution.py:242
  2.1 1.2 %pad_maximum_fusion.all_hbm = f32[3,3,128,128]{3,2,1,0:T(8,128)S(1)} fusion(f32[1,3,128,128]{3,2,1,0:T(8,128)} %bitcast.5, f32[1,3,128,128]{3,2,1,0:T(8,128)} %bitcast.6, f32[1,3,128,128]{3,2,1,0:T(8,128)} %bitcast.7), kind=kLoop, calls=%fused_computation | loop fusion | flops 294912 | bytes 1179648 | tf_op jit(solution)/shard_map/stack | solution.py:242
  3.3 32.8 %exchange.1 = (f32[2048,128]{1,0:T(8,128)S(1)}, f32[1024,128]{1,0:T(8,128)S(1)}, f32[256,24,128]{2,1,0:T(8,128)S(1)}, s32[8,128]{1,0:T(8,128)S(1)}, f32[128,256]...) custom-call(s32[5,128]{1,0:T(8,128)S(1)} %add_add_fusion.route_ref, f32[3,3,128,128]{3,2,1,0:T(8,128)S(1)} %pad_maximum_fusion.all_hbm), custom_call_target="tpu_custom_call" | custom-call | tf_op jit(solution)/shard_map/exchange/pallas_call | solution.py:223
  36.1 3.4 %deposit.1.w_ref = f32[3,24,16,128]{3,2,1,0:T(8,128)S(1)} custom-call(s32[8,128]{1,0:T(8,128)S(1)} %get-tuple-element.14.corners_s, f32[256,24,128]{2,1,0:T(8,128)S(1)} %get-tuple-element.17.boxes), custom_call_target="tpu_custom_call" | custom-call | tf_op jit(solution)/shard_map/deposit/pallas_call | solution.py:280
  39.4 33.9 %project.1 = (f32[3,16,8,128]{3,2,1,0:T(8,128)S(1)}, f32[16,8,128]{2,1,0:T(8,128)S(1)}, f32[1024,128]{1,0:T(8,128)S(1)}, f32[512,128]{1,0:T(8,128)S(1)}) custom-call(s32[8,128]{1,0:T(8,128)S(1)} %get-tuple-element.14.corners_s, f32[2048,128]{1,0:T(8,128)S(1)} %get-tuple-element.15.inbox, f32[1024,128]{1,0:T(8,128)S(1)} %get-tuple-element.16.relay, ...), custom_call_target="tpu_custom_call" | custom-call | tf_op jit(solution)/shard_map/project/pallas_call | solution.py:533
  73.4 1.5 %finish.1 = (f32[3,16,8,128]{3,2,1,0:T(8,128)}, f32[16,8,128]{2,1,0:T(8,128)}, f32[3,128,128]{2,1,0:T(8,128)}) custom-call(f32[128,256]{1,0:T(8,128)S(1)} %get-tuple-element.13.back, f32[1024,128]{1,0:T(8,128)S(1)} %get-tuple-element.19.direct, f32[512,128]{1,0:T(8,128)S(1)} %get-tuple-element.20.passed, f32[3,16,8,128]{3,2,1,0:T(8,128)S(1)} %get-tuple-element.21.new_ref, ...), custom_call_target="tpu_custom_call" | custom-call | tf_op jit(solution)/shard_map/finish/pallas_call | solution.py:579

commit v7 on v6

--- a/solution.py
+++ b/solution.py
@@ -84,7 +84,8 @@
 
 def shifted(chip, here, sign):
     y, core, z, x = here
-    kx, ky, kz = chip & 3, (chip >> 2) & 3, chip >> 4
+    kx, by, bz = chip & 3, (chip >> 2) & 3, chip >> 4
+    ky, kz = (by + 3 * kx) & 3, (bz + by + kx) & 3
     if sign < 0:
         kx, ky, kz = 4 - kx, 4 - ky, 4 - kz
     return (((y + ky) & 3) * 2 + core, ((z + kz) & 3) * 4 + ((x + kx) & 3))
@@ -100,7 +101,8 @@
     row, column = owner >> 4, owner & 15
     kc, ky = ((row & 1) - core) & 1, ((row >> 1) - y) & 3
     kz, kx = ((column >> 2) - z) & 3, ((column & 3) - x) & 3
-    return kx + 4 * ky + 16 * kz + 64 * kc
+    by = (ky - 3 * kx) & 3
+    return kx + 4 * by + 16 * ((kz - by - kx) & 3) + 64 * kc
 
 
 def greet_all(line_sem, between):
@@ -242,7 +244,7 @@
     )(jnp.concatenate([base, owner[None], jnp.broadcast_to(counts[:, None], (1, 128))], axis=0), jnp.stack([offsets, forces, velocity.reshape(3, 128, 128)]))
 
 
-def deposit_body(corners_s, boxes, out, acc, tot):
+def deposit_body(corners_s, boxes, acc):
     def zero(x, carry):
         acc[x] = jnp.zeros((3, 128, 128), F32)
         return carry
@@ -258,31 +260,14 @@
         return carry
 
     lax.fori_loop(0, 128, add, 0, unroll=4)
-    lane = lax.broadcasted_iota(jnp.int32, (128, 128), 1)
-    for c in range(3):
-        filled = [False] * 3
-        for t in range(2):
-            for r in range(8):
-                a = acc[8 * t + r, c]
-                if r == 0:
-                    parts = [(t, a)]
-                else:
-                    a = pltpu.roll(a, 16 * r, 1)
-                    parts = [(t, jnp.where(lane >= 16 * r, a, 0.0)), (t + 1, jnp.where(lane < 16 * r, a, 0.0))]
-                for k, v in parts:
-                    tot[k] = tot[k] + v if filled[k] else v
-                    filled[k] = True
-        for k in range(3):
-            out[c, 8 * k:8 * k + 8] = tot[k].T.reshape(8, 16, 128)
 
 
 def deposit_call(corners, boxes):
     return pl.pallas_call(
         deposit_body,
-        out_shape=jax.ShapeDtypeStruct((3, 24, 16, 128), F32),
+        out_shape=jax.ShapeDtypeStruct((16, 3, 128, 128), F32),
         in_specs=[SM, VM],
         out_specs=VM,
-        scratch_shapes=[pltpu.VMEM((16, 3, 128, 128), F32), pltpu.VMEM((3, 128, 128), F32)],
         compiler_params=pltpu.CompilerParams(vmem_limit_bytes=40 * 2**20),
         name="deposit",
     )(corners, boxes)
@@ -316,7 +301,7 @@
     return above, below
 
 
-def project_body(unroll, chunks, corners_s, inbox, relay, w_ref, ve, new_ref, prs_ref, direct, passed, v_ref, pe, src, pa, pb, fold, tables, wxs, planes, depths, cop, ans, line_sem, send, recv, out_sem, in_sem, pass_sem, take_sem):
+def project_body(unroll, chunks, corners_s, inbox, relay, acc, ve, new_ref, prs_ref, direct, passed, w_ref, tot, v_ref, pe, src, pa, pb, fold, tables, wxs, planes, depths, cop, ans, line_sem, send, recv, out_sem, in_sem, pass_sem, take_sem):
     here = position()
     peers = neighbours()
     gx, gy = lax.axis_index("gx"), lax.axis_index("gy")
@@ -352,6 +337,22 @@
 
         lax.fori_loop(begin // unroll, end // unroll, turn, 0)
 
+    wide = lax.broadcasted_iota(jnp.int32, (128, 128), 1)
+    for c in range(3):
+        filled = [False] * 3
+        for t in range(2):
+            for r in range(8):
+                a = acc[8 * t + r, c]
+                if r == 0:
+                    parts = [(t, a)]
+                else:
+                    a = pltpu.roll(a, 16 * r, 1)
+                    parts = [(t, jnp.where(wide >= 16 * r, a, 0.0)), (t + 1, jnp.where(wide < 16 * r, a, 0.0))]
+                for k, v in parts:
+                    tot[k] = tot[k] + v if filled[k] else v
+                    filled[k] = True
+        for k in range(3):
+            w_ref[c, 8 * k:8 * k + 8] = tot[k].T.reshape(8, 16, 128)
     weigh(chunks[0], chunks[1])
     pl.semaphore_wait(barrier, 22)
     for i in range(1, 8):
@@ -462,7 +463,6 @@
 
     for c in range(3):
         tiles = [v_ref[c, 8 * k:8 * k + 8].reshape(128, 128).T for k in range(3)]
-        wide = lax.broadcasted_iota(jnp.int32, (128, 128), 1)
         for r in range(8):
             if r == 0:
                 cop[0, c], cop[8, c] = tiles[0], tiles[1]
@@ -497,18 +497,18 @@
                     for c in range(3):
                         ans[pl.ds(chip * 16 + kc * 6 + r * 3 + c, 1), :] = jnp.sum(o[8 * c:8 * c + 8] * wz, axis=0, keepdims=True)
 
-    work(list(range(4)))
-    for chip in range(1, 4):
+    work(list(range(8)))
+    for chip in range(1, 8):
         message(chip).start()
 
     def turn(t, carry):
-        chips = [t * 4 + u for u in range(4)]
+        chips = [t * 8 + u for u in range(8)]
         work(chips)
         for chip in chips:
             message(chip).start()
         return carry
 
-    lax.fori_loop(1, 16, turn, 0)
+    lax.fori_loop(1, 8, turn, 0)
     direct[0:16] = ans[0:16]
     for group in range(4):
         for chip in range(max(group * 16, 1), group * 16 + 16):
@@ -528,7 +528,7 @@
         copy.wait_send()
 
 
-def project_call(corners, inbox, relay, widened, moving, unroll=4, chunks=(0, 24, 64, 128)):
+def project_call(corners, inbox, relay, spread, moving, unroll=4, chunks=(0, 0, 64, 128)):
     shapes = (3, 16, 8, 128), (16, 8, 128), (1024, 128), (512, 128)
     return pl.pallas_call(
         functools.partial(project_body, unroll, chunks),
@@ -536,6 +536,8 @@
         in_specs=[SM, VM, VM, VM, VM],
         out_specs=(VM,) * 4,
         scratch_shapes=[
+            pltpu.VMEM((3, 24, 16, 128), F32),
+            pltpu.VMEM((3, 128, 128), F32),
             pltpu.VMEM((3, 24, 16, 128), F32),
             pltpu.VMEM((3, 32, 24, 128), F32),
             pltpu.VMEM((32, 24, 128), F32),
@@ -558,7 +560,7 @@
         ],
         compiler_params=pltpu.CompilerParams(vmem_limit_bytes=40 * 2**20, collective_id=0, has_side_effects=True),
         name="project",
-    )(corners, inbox, relay, widened, moving)
+    )(corners, inbox, relay, spread, moving)
 
 
 def finish_body(back, direct, passed, new_ref, prs_ref, out_new, out_prs, out, sems):
@@ -589,8 +591,8 @@
 
 def shards(velocity, offsets, forces, owner, base, counts):
     inbox, relay, boxes, corners, back, moving = exchange_call(counts, owner, offsets, forces, base, velocity)
-    widened = deposit_call(corners, boxes)
-    new_velocity, pressure, direct, passed = project_call(corners, inbox, relay, widened, moving)
+    spread = deposit_call(corners, boxes)
+    new_velocity, pressure, direct, passed = project_call(corners, inbox, relay, spread, moving)
     return finish_call(back, direct, passed, new_velocity, pressure)
 
 

time: 75 us -> 70.1 us (0.935)
  Pallas kernels: 71.5 us -> 66.7 us
    pallas_call x1, Pallas kernels: 32.8 us -> 29.5 us  [exchange_call(): pl.pallas_call(exchange_body, out_shape=tuple((jax.ShapeDtypeStruct(*s) f...]
    pallas_call x1, Pallas kernels: 3.37 us -> 2.41 us  [deposit_call(): pl.pallas_call(deposit_body, out_shape=jax.ShapeDtypeStruct((16, 3, 128,...]
where the time goes in v7:
time: 70.1 us; the launch traced here: 70 us
  Pallas kernels  66.7 us (95%)
  other arithmetic  1.92 us (3%)
  between operations  1.3 us (2%)
    pallas_call x1, Pallas kernels, project_call(): pl.pallas_call(functools.partial(project_body, unroll, chunks), out_shape...  33.4 us
    pallas_call x1, Pallas kernels, exchange_call(): pl.pallas_call(exchange_body, out_shape=tuple((jax.ShapeDtypeStruct(*s) f...  29.5 us
    pallas_call x1, Pallas kernels, deposit_call(): pl.pallas_call(deposit_body, out_shape=jax.ShapeDtypeStruct((16, 3, 128,...  2.41 us
    pallas_call x1, Pallas kernels, finish_call(): pl.pallas_call(finish_body, out_shape=tuple((jax.ShapeDtypeStruct(s, F32)...  1.45 us

profile of v7, /device:TPU:1, one launch (start us, length us, event | category | flops | bytes accessed | tf_op | source)
XLA Modules:
  0.0 70.0 jit_solution(15588517848364256981)
XLA Ops:
  1.3 0.1 pad.5.clone
  1.4 0.8 %add_add_fusion.route_ref = s32[5,128]{1,0:T(8,128)S(1)} fusion(s32[1,128]{1,0:T(1,128)} %bitcast.8, s32[3,128]{1,0:T(4,128)} %param.10, s32[5]{0:T(128)S(1)} %pad.5.clone), kind=kLoop, calls=%fused_computation.1 | loop fusion | flops 1280 | bytes 4628 | tf_op jit(solution)/shard_map/concatenate | solution.py:244
  2.1 1.2 %pad_maximum_fusion.all_hbm = f32[3,3,128,128]{3,2,1,0:T(8,128)S(1)} fusion(f32[1,3,128,128]{3,2,1,0:T(8,128)} %bitcast.5, f32[1,3,128,128]{3,2,1,0:T(8,128)} %bitcast.6, f32[1,3,128,128]{3,2,1,0:T(8,128)} %bitcast.7), kind=kLoop, calls=%fused_computation | loop fusion | flops 294912 | bytes 1179648 | tf_op jit(solution)/shard_map/stack | solution.py:244
  3.3 29.5 %exchange.1 = (f32[2048,128]{1,0:T(8,128)S(1)}, f32[1024,128]{1,0:T(8,128)S(1)}, f32[256,24,128]{2,1,0:T(8,128)S(1)}, s32[8,128]{1,0:T(8,128)S(1)}, f32[128,256]...) custom-call(s32[5,128]{1,0:T(8,128)S(1)} %add_add_fusion.route_ref, f32[3,3,128,128]{3,2,1,0:T(8,128)S(1)} %pad_maximum_fusion.all_hbm), custom_call_target="tpu_custom_call" | custom-call | tf_op jit(solution)/shard_map/exchange/pallas_call | solution.py:225
  32.7 2.4 %deposit.1.acc = f32[16,3,128,128]{3,2,1,0:T(8,128)S(1)} custom-call(s32[8,128]{1,0:T(8,128)S(1)} %get-tuple-element.14.corners_s, f32[256,24,128]{2,1,0:T(8,128)S(1)} %get-tuple-element.17.boxes), custom_call_target="tpu_custom_call" | custom-call | tf_op jit(solution)/shard_map/deposit/pallas_call | solution.py:266
  35.2 33.4 %project.1 = (f32[3,16,8,128]{3,2,1,0:T(8,128)S(1)}, f32[16,8,128]{2,1,0:T(8,128)S(1)}, f32[1024,128]{1,0:T(8,128)S(1)}, f32[512,128]{1,0:T(8,128)S(1)}) custom-call(s32[8,128]{1,0:T(8,128)S(1)} %get-tuple-element.14.corners_s, f32[2048,128]{1,0:T(8,128)S(1)} %get-tuple-element.15.inbox, f32[1024,128]{1,0:T(8,128)S(1)} %get-tuple-element.16.relay, ...), custom_call_target="tpu_custom_call" | custom-call | tf_op jit(solution)/shard_map/project/pallas_call | solution.py:533
  68.5 1.5 %finish.1 = (f32[3,16,8,128]{3,2,1,0:T(8,128)}, f32[16,8,128]{2,1,0:T(8,128)}, f32[3,128,128]{2,1,0:T(8,128)}) custom-call(f32[128,256]{1,0:T(8,128)S(1)} %get-tuple-element.13.back, f32[1024,128]{1,0:T(8,128)S(1)} %get-tuple-element.19.direct, f32[512,128]{1,0:T(8,128)S(1)} %get-tuple-element.20.passed, f32[3,16,8,128]{3,2,1,0:T(8,128)S(1)} %get-tuple-element.21.new_ref, ...), custom_call_target="tpu_custom_call" | custom-call | tf_op jit(solution)/shard_map/finish/pallas_call | solution.py:581

commit v8 on v7

--- a/solution.py
+++ b/solution.py
@@ -259,7 +259,7 @@
                 acc[x0, c, pl.ds(z0, 8), :] += boxes[k * 2 + r, c * 8:c * 8 + 8]
         return carry
 
-    lax.fori_loop(0, 128, add, 0, unroll=4)
+    lax.fori_loop(0, 128, add, 0, unroll=16)
 
 
 def deposit_call(corners, boxes):
@@ -528,7 +528,7 @@
         copy.wait_send()
 
 
-def project_call(corners, inbox, relay, spread, moving, unroll=4, chunks=(0, 0, 64, 128)):
+def project_call(corners, inbox, relay, spread, moving, unroll=8, chunks=(0, 0, 64, 128)):
     shapes = (3, 16, 8, 128), (16, 8, 128), (1024, 128), (512, 128)
     return pl.pallas_call(
         functools.partial(project_body, unroll, chunks),

time: 70.1 us -> 70.2 us (level)
  no operation moved by 1% of the time
where the time goes in v8:
time: 70.2 us; the launch traced here: 70 us
  Pallas kernels  66.7 us (95%)
  other arithmetic  1.92 us (3%)
  between operations  1.3 us (2%)
    pallas_call x1, Pallas kernels, project_call(): pl.pallas_call(functools.partial(project_body, unroll, chunks), out_shape...  33.4 us
    pallas_call x1, Pallas kernels, exchange_call(): pl.pallas_call(exchange_body, out_shape=tuple((jax.ShapeDtypeStruct(*s) f...  29.5 us
    pallas_call x1, Pallas kernels, deposit_call(): pl.pallas_call(deposit_body, out_shape=jax.ShapeDtypeStruct((16, 3, 128,...  2.44 us
    pallas_call x1, Pallas kernels, finish_call(): pl.pallas_call(finish_body, out_shape=tuple((jax.ShapeDtypeStruct(s, F32)...  1.45 us

profile of v8, /device:TPU:1, one launch (start us, length us, event | category | flops | bytes accessed | tf_op | source)
XLA Modules:
  0.0 70.0 jit_solution(13246233125026644583)
XLA Ops:
  1.3 0.1 pad.5.clone
  1.4 0.8 %add_add_fusion.route_ref = s32[5,128]{1,0:T(8,128)S(1)} fusion(s32[1,128]{1,0:T(1,128)} %bitcast.8, s32[3,128]{1,0:T(4,128)} %param.10, s32[5]{0:T(128)S(1)} %pad.5.clone), kind=kLoop, calls=%fused_computation.1 | loop fusion | flops 1280 | bytes 4628 | tf_op jit(solution)/shard_map/concatenate | solution.py:244
  2.1 1.2 %pad_maximum_fusion.all_hbm = f32[3,3,128,128]{3,2,1,0:T(8,128)S(1)} fusion(f32[1,3,128,128]{3,2,1,0:T(8,128)} %bitcast.5, f32[1,3,128,128]{3,2,1,0:T(8,128)} %bitcast.6, f32[1,3,128,128]{3,2,1,0:T(8,128)} %bitcast.7), kind=kLoop, calls=%fused_computation | loop fusion | flops 294912 | bytes 1179648 | tf_op jit(solution)/shard_map/stack | solution.py:244
  3.3 29.5 %exchange.1 = (f32[2048,128]{1,0:T(8,128)S(1)}, f32[1024,128]{1,0:T(8,128)S(1)}, f32[256,24,128]{2,1,0:T(8,128)S(1)}, s32[8,128]{1,0:T(8,128)S(1)}, f32[128,256]...) custom-call(s32[5,128]{1,0:T(8,128)S(1)} %add_add_fusion.route_ref, f32[3,3,128,128]{3,2,1,0:T(8,128)S(1)} %pad_maximum_fusion.all_hbm), custom_call_target="tpu_custom_call" | custom-call | tf_op jit(solution)/shard_map/exchange/pallas_call | solution.py:225
  32.7 2.4 %deposit.1.acc = f32[16,3,128,128]{3,2,1,0:T(8,128)S(1)} custom-call(s32[8,128]{1,0:T(8,128)S(1)} %get-tuple-element.14.corners_s, f32[256,24,128]{2,1,0:T(8,128)S(1)} %get-tuple-element.17.boxes), custom_call_target="tpu_custom_call" | custom-call | tf_op jit(solution)/shard_map/deposit/pallas_call | solution.py:266
  35.2 33.4 %project.1 = (f32[3,16,8,128]{3,2,1,0:T(8,128)S(1)}, f32[16,8,128]{2,1,0:T(8,128)S(1)}, f32[1024,128]{1,0:T(8,128)S(1)}, f32[512,128]{1,0:T(8,128)S(1)}) custom-call(s32[8,128]{1,0:T(8,128)S(1)} %get-tuple-element.14.corners_s, f32[2048,128]{1,0:T(8,128)S(1)} %get-tuple-element.15.inbox, f32[1024,128]{1,0:T(8,128)S(1)} %get-tuple-element.16.relay, ...), custom_call_target="tpu_custom_call" | custom-call | tf_op jit(solution)/shard_map/project/pallas_call | solution.py:533
  68.6 1.5 %finish.1 = (f32[3,16,8,128]{3,2,1,0:T(8,128)}, f32[16,8,128]{2,1,0:T(8,128)}, f32[3,128,128]{2,1,0:T(8,128)}) custom-call(f32[128,256]{1,0:T(8,128)S(1)} %get-tuple-element.13.back, f32[1024,128]{1,0:T(8,128)S(1)} %get-tuple-element.19.direct, f32[512,128]{1,0:T(8,128)S(1)} %get-tuple-element.20.passed, f32[3,16,8,128]{3,2,1,0:T(8,128)S(1)} %get-tuple-element.21.new_ref, ...), custom_call_target="tpu_custom_call" | custom-call | tf_op jit(solution)/shard_map/finish/pallas_call | solution.py:581
